TPU v7x, 32 devices: a whole 2x2x4 slice. The times are simulated.
32 devices in a mesh: groups: 2 (over x), ept: 8 (over z, y), exp: 2 (over core).
Axes of the slice: x: 2, y: 2, z: 4, core: 2. Of those that a mesh axis runs over, the one named last changes fastest.
Arguments:
- tokens: bfloat16 [4096, 6144], P(('groups', 'ept', 'exp')), parts along dimension 0, may hold values from -6 to 6
- expert_ids: int32 [4096, 2], P(('groups', 'ept', 'exp')), parts along dimension 0, may hold values from 0 to 7, as said below
- route_weights: float32 [4096, 2], P(('groups', 'ept', 'exp')), parts along dimension 0, may hold values from 0.1 to 1
- w_gate: bfloat16 [2, 6144, 8192], P('exp', None, 'ept'), may hold values from -0.078125 to 0.078125
- w_up: bfloat16 [2, 6144, 8192], P('exp', None, 'ept'), may hold values from -0.078125 to 0.078125
- w_down: bfloat16 [2, 8192, 6144], P('exp', 'ept'), may hold values from -0.0625 to 0.0625
Outputs:
- mixed_out: bfloat16 [4096, 6144], P(('groups', 'ept', 'exp')), parts along dimension 0
There are 2 independent parts, one for each index of `groups`. A program takes and returns all parts, laid end to end along the dimension named above; an argument that names none is the same for every part. Nothing has to cross between parts.
Inputs may be any that keep to these rules, and one draw needn't show every extreme that they name: `expert_ids`: the 2 experts named in one row differ.
All inputs are finite; a program needn't handle non-finite values.
Results may differ from a plain program's by a relative error of at most 0.013.
Values may be sent and summed in bfloat16 or wider, within the bound.
No kernel may reach another device: no remote copies, remote signals or barrier semaphores. Data moves between devices by JAX's collectives and lax.ppermute only.
A program may use at most 128 MiB of HBM per device.

v0:
```python
import jax
import jax.numpy as jnp
from jax import lax
from jax.sharding import PartitionSpec as P

CAP = 16


def body(tokens, expert_ids, route_weights, w_gate, w_up, w_down):
    local_count = w_gate.shape[0]
    exp_count = lax.axis_size("exp")
    experts_all = local_count * exp_count
    token_count = tokens.shape[0]
    model_width = tokens.shape[1]
    choices_per = expert_ids.shape[1]
    capacity = CAP
    choice_ids = expert_ids.reshape(-1)
    onehot = (choice_ids[:, None] == jnp.arange(experts_all, dtype=jnp.int32)).astype(jnp.int32)
    before = jnp.cumsum(onehot, axis=0) - onehot
    slot_index = jnp.sum(before * onehot, axis=-1)
    kept_mask = (jnp.sum(onehot, axis=-1) > 0) & (slot_index < capacity)
    matches = onehot.T[:, None, :] == 1
    matches = matches & (
        slot_index[None, None, :] == jnp.arange(capacity, dtype=jnp.int32)[None, :, None]
    )
    matches = matches & kept_mask[None, None, :]
    picker = jnp.sum(
        matches.reshape(experts_all, capacity, token_count, choices_per).astype(jnp.int32), axis=-1
    )
    picker = picker.astype(jnp.bfloat16)
    buffer = jnp.einsum("ecs,sd->ecd", picker, tokens, preferred_element_type=jnp.float32).astype(
        jnp.bfloat16
    )
    incoming = lax.all_to_all(buffer, "exp", split_axis=0, concat_axis=0, tiled=True)
    gathered = lax.all_gather(incoming, "ept", axis=0, tiled=True)
    row_count = gathered.shape[0]
    pieces = []
    expert = 0
    row_block = gathered.reshape(-1, model_width)
    gate_value = jnp.dot(row_block, w_gate[expert], preferred_element_type=jnp.float32)
    up_value = jnp.dot(row_block, w_up[expert], preferred_element_type=jnp.float32)
    hidden_rows = (jax.nn.silu(gate_value) * up_value).astype(jnp.bfloat16)
    pieces.append(hidden_rows.reshape(row_count, capacity, -1))
    hidden = jnp.stack(pieces, axis=1)
    row_count = hidden.shape[0]
    hidden_width = hidden.shape[3]
    pieces = []
    expert = 0
    flat_hidden = hidden[:, expert].reshape(-1, hidden_width)
    product = jnp.dot(flat_hidden, w_down[expert], preferred_element_type=jnp.float32)
    pieces.append(product.reshape(row_count, capacity, model_width))
    summed = lax.psum_scatter(
        jnp.stack(pieces, axis=1)
        .reshape(row_count, local_count * capacity, model_width)
        .astype(jnp.bfloat16),
        "ept",
        scatter_dimension=0,
        tiled=True,
    )
    returned = lax.all_to_all(summed, "exp", split_axis=0, concat_axis=0, tiled=True)
    flat_rows = returned.reshape(experts_all * capacity, model_width)
    row_index = jnp.where(
        kept_mask, jnp.clip(choice_ids * capacity + slot_index, 0, experts_all * capacity - 1), 0
    )
    picked = jnp.take(flat_rows, row_index, axis=0).astype(jnp.float32)
    scaled = route_weights.reshape(-1) * kept_mask.astype(jnp.float32)
    mixed_out = jnp.sum(
        (picked * scaled[:, None]).reshape(token_count, choices_per, model_width), axis=1
    )
    return mixed_out.astype(jnp.bfloat16)


def solution(mesh):
    placed = (
        P(("groups", "ept", "exp"), None),
        P(("groups", "ept", "exp"), None),
        P(("groups", "ept", "exp"), None),
        P("exp", None, "ept"),
        P("exp", None, "ept"),
        P("exp", "ept", None),
    )
    return jax.shard_map(
        body,
        mesh=mesh,
        in_specs=placed,
        out_specs=P(("groups", "ept", "exp"), None),
        check_vma=False,
    )
```

profile of v0, /device:TPU:0, one launch (start us, length us, event | category | flops | bytes accessed | tf_op | source)
XLA Modules:
  0.0 213.2 jit_solution(984918847539725406)
XLA Ops:
  6.5 0.9 copy.28
  7.4 0.1 eq.69
  7.6 0.1 eq.65
  7.7 0.7 fusion.19
  8.4 0.6 reduce-window.6
  9.0 0.2 slice_reduce_fusion
  9.2 0.2 reduce-window.9
  9.4 0.1 add_bitcast_fusion
  9.5 0.1 reduce_sum.42
  9.7 0.1 copy.30
  9.7 0.2 gt.35
  9.9 0.1 copy.31
  10.0 0.7 broadcast_select_fusion.1
  10.7 0.3 convolution_convert_fusion
  11.1 4.8 %all_to_all.10 = bf16[2,16,6144]{2,1,0:T(8,128)(2,1)} all-to-all(bf16[2,16,6144]{2,1,0:T(8,128)(2,1)S(1)} %convolution_convert_fusion), channel_id=1, replica_groups=mesh['groups'=2,'ept'=8,'exp'=2] {'exp'}, dimensions={0} | all-to-all | bytes 786432 | tf_op jit(solution)/shard_map/all_to_all | solution.py:34
  15.9 0.0 all-gather.2.cloned.1.call-update
  15.9 0.0 reduce-scatter.2.cloned.1.call-start
  15.9 63.3 %all-gather.2.cloned.1.call-done = bf16[16,16,6144]{2,1,0:T(8,128)(2,1)} async-done(((bf16[2,16,6144]{2,1,0:T(8,128)(2,1)}), bf16[16,16,6144]{2,1,0:T(8,128)(2,1)}) %all-gather.2.cloned.1.call-update) | async-done | bytes 3145744 | tf_op jit(solution)/shard_map/all_gather | solution.py:35
  79.2 7.5 %fusion.4 = f32[256,1024]{1,0:T(8,128)S(1)} fusion(bf16[256,6144]{1,0:T(8,128)(2,1)} %bitcast.44, bf16[1,6144,1024]{2,1,0:T(8,128)(2,1)} %param.9), kind=kOutput, calls=%fused_computation.5 | convolution fusion | flops 3221225472 | bytes 16777216 | tf_op jit(solution)/shard_map/dot_general | solution.py:40
  86.7 8.5 %fusion.13 = bf16[256,1024]{1,0:T(8,128)(2,1)S(1)} fusion(bf16[256,6144]{1,0:T(8,128)(2,1)S(1)} %bitcast.45, bf16[1,6144,1024]{2,1,0:T(8,128)(2,1)} %param.10, f32[256,1024]{1,0:T(8,128)S(1)} %fusion.4), kind=kOutput, calls=%fused_computation.13 | convolution fusion | flops 3222798336 | bytes 17301504 | tf_op jit(solution)/shard_map/dot_general | solution.py:41
  95.2 4.8 %fusion.6 = bf16[16,16,6144]{2,1,0:T(8,128)(2,1)} fusion(bf16[16,16,1024]{2,1,0:T(8,128)(2,1)S(1)} %bitcast.46, bf16[1,1024,6144]{2,1,0:T(8,128)(2,1)S(1)} %bitcast.43), kind=kOutput, calls=%fused_computation.7 | convolution fusion | flops 3222798336 | bytes 16252928 | tf_op jit(solution)/shard_map/dot_general | solution.py:50
  100.0 0.0 reduce-scatter.2.cloned.1.call-update
  100.1 0.7 copy-done.1
  100.7 0.1 copy.35
  100.8 0.1 mul.42
  101.0 0.1 copy.33
  101.1 0.1 copy.36
  101.3 71.8 %reduce-scatter.2.cloned.1.call-done = bf16[2,16,6144]{2,1,0:T(8,128)(2,1)} async-done(((bf16[16,16,6144]{2,1,0:T(8,128)(2,1)}), bf16[2,16,6144]{2,1,0:T(8,128)(2,1)}) %reduce-scatter.2.cloned.1.call-update) | async-done | bytes 393232 | tf_op jit(solution)/shard_map/reduce_scatter | solution.py:52
  173.0 5.1 %all_to_all.11 = bf16[2,16,6144]{2,1,0:T(8,128)(2,1)S(1)} all-to-all(bf16[2,16,6144]{2,1,0:T(8,128)(2,1)} %reduce-scatter.2.cloned.1.call-done), channel_id=1, replica_groups=mesh['groups'=2,'ept'=8,'exp'=2] {'exp'}, dimensions={0} | all-to-all | bytes 786432 | tf_op jit(solution)/shard_map/all_to_all | solution.py:60
  178.1 4.1 %gather_fusion = bf16[256,6144]{1,0:T(8,128)(2,1)} fusion(bf16[32,6144]{1,0:T(8,128)(2,1)S(1)} %bitcast.38, s32[1024]{0:T(1024)S(1)} %pad_clamp_fusion), kind=kCustom, calls=%fused_computation | custom fusion | bytes 6292480 | tf_op jit(solution)/shard_map/jit(_take)/gather | solution.py:65
  182.2 7.1 %gather.7 = bf16[128,2,6144]{2,1,0:T(2,128)(2,1)} reshape(bf16[256,6144]{1,0:T(8,128)(2,1)} %gather_fusion) | data formatting | bytes 6291456 | tf_op jit(solution)/shard_map/jit(_take)/gather | solution.py:65
  189.3 17.0 %multiply_reduce_fusion = bf16[128,6144]{1,0:T(8,128)(2,1)} fusion(bf16[128,2,6144]{2,1,0:T(2,128)(2,1)} %gather.7, pred[128,2]{1,0:T(8,128)(4,1)S(1)} %copy.33, f32[128,2]{1,0:T(8,128)S(1)} %copy.36), kind=kLoop, calls=%fused_computation.9 | loop fusion | flops 5505024 | bytes 4719872 | tf_op jit(solution)/shard_map/reduce_sum | solution.py:67
  (22 shorter events, 0.1 us)
Async XLA Ops:
  6.5 4.2 %copy-start = (bf16[128,6144]{1,0:T(8,128)(2,1)S(1)}, bf16[128,6144]{1,0:T(8,128)(2,1)}, u32[]{:S(2)}) copy-start(bf16[128,6144]{1,0:T(8,128)(2,1)} %param.6) | copy-start | bytes 4718596
  6.5 72.7 %all-gather.2.cloned.1.call-start = ((), (), s32[]{:S(2)}) async-start(), calls=%async_computation.3 | async-start | bytes 3538944 | tf_op jit(solution)/shard_map/all_gather | solution.py:35
  15.9 157.1 %reduce-scatter.2.cloned.1.call-start = ((), (), s32[]{:S(2)}) async-start(), calls=%async_computation.4 | async-start | bytes 3538944 | tf_op jit(solution)/shard_map/reduce_scatter | solution.py:52
  79.2 7.5 %copy-start.2 = (bf16[16,16,6144]{2,1,0:T(8,128)(2,1)S(1)}, bf16[16,16,6144]{2,1,0:T(8,128)(2,1)}, u32[]{:S(2)}) copy-start(bf16[16,16,6144]{2,1,0:T(8,128)(2,1)} %all-gather.2.cloned.1.call-done) | copy-start | bytes 9437188
  79.2 16.0 %slice-start = ((s8[12582912]{0:T(1024)(128)(4,1)}), s8[4194304]{0:T(1024)(128)(4,1)S(1)}, s32[]{:S(2)}) async-start(s8[12582912]{0:T(1024)(128)(4,1)} %bitcast.42), calls=%async_computation.5 | async-start | bytes 8388608
  79.2 16.0 %slice-start.1 = ((s8[12582912]{0:T(1024)(128)(4,1)}), s8[4194304]{0:T(1024)(128)(4,1)S(1)}, s32[]{:S(2)}) async-start(s8[12582912]{0:T(1024)(128)(4,1)} %bitcast.42), calls=%async_computation.6 | async-start | bytes 8388608
  86.7 8.5 %slice-start.2 = ((s8[12582912]{0:T(1024)(128)(4,1)}), s8[4194304]{0:T(1024)(128)(4,1)S(1)}, s32[]{:S(2)}) async-start(s8[12582912]{0:T(1024)(128)(4,1)} %bitcast.42), calls=%async_computation.7 | async-start | bytes 8388608
  100.0 0.7 copy-start.1
Sparse Core Ops, SparseCore 0:
  16.0 63.1 all-gather.1
  100.2 72.8 reduce-scatter.1
where the time goes:
time: 214 us; the launch traced here: 213 us
  waiting for transfers between devices  135 us (63%)
  matrix products  21.1 us (10%)
  other arithmetic  19.4 us (9%)
  local copies, waits for them, and re-layouts  14.2 us (7%)
  between operations  13.5 us (6%)
  blocking collectives  9.89 us (5%)
    reduce_scatter x1, waiting for transfers between devices, body(): lax.psum_scatter(jnp.stack(pieces, axis=1).reshape(row_count, local_count...  71.8 us
    all_gather x1, waiting for transfers between devices, body(): gathered = lax.all_gather(incoming, 'ept', axis=0, tiled=True)  63.3 us
    reduce_sum x1, other arithmetic, body(): jnp.sum((picked * scaled[:, None]).reshape(token_count, choices_per, mode...  17 us
    gather x2, local copies, waits for them, and re-layouts, body(): picked = jnp.take(flat_rows, row_index, axis=0).astype(jnp.float32)  11.2 us
    dot_general x1, matrix products, body(): jnp.dot(row_block, w_up[expert], preferred_element_type=jnp.float32)  8.5 us
    dot_general x1, matrix products, body(): jnp.dot(row_block, w_gate[expert], preferred_element_type=jnp.float32)  7.45 us
    all_to_all x1, blocking collectives, body(): lax.all_to_all(summed, 'exp', split_axis=0, concat_axis=0, tiled=True)  5.1 us
    all_to_all x1, blocking collectives, body(): lax.all_to_all(buffer, 'exp', split_axis=0, concat_axis=0, tiled=True)  4.79 us
  transfers between devices with their start and end apart: 2, of which 2 were waited for; matrix products, arithmetic and copies ran while one was open for 0% of the time, Pallas kernels for 0%

commit v1 on v0

v1 whole, which is shorter than its diff:
```python
import jax
import jax.numpy as jnp
from jax import lax
from jax.experimental import pallas as pl
from jax.experimental.pallas import tpu as pltpu
from jax.sharding import PartitionSpec as P

CAP = 16
BLOCK = 2 * CAP
LANES = 128
VMEM_LIMIT = 8 * 1024 * 1024


def ring_pairs(count, columns):
    rows = count // columns
    if columns == 2:
        cycle = [2 * r for r in range(rows)] + [2 * r + 1 for r in reversed(range(rows))]
    else:
        cycle = list(range(count))
    forward = [(cycle[i], cycle[(i + 1) % count]) for i in range(count)]
    return forward, [(b, a) for a, b in forward]


def swap(value):
    return lax.ppermute(value, "exp", [(0, 1), (1, 0)])


def tile_of(size, most):
    return max(t for t in range(LANES, most + 1, LANES) if size % t == 0)


def in_hbm(value):
    return pltpu.with_memory_space_constraint(value, pltpu.HBM)


def dispatch_kernel(me_ref, ids_ref, weights_ref, tokens_ref, mine_ref, theirs_ref, mixer_ref, picker):
    @pl.when(pl.program_id(0) == 0)
    def _():
        token_count = ids_ref.shape[1]
        line = lax.broadcasted_iota(jnp.int32, (BLOCK, token_count), 0)
        expert = (line // CAP + me_ref[0]) % 2
        first = ids_ref[0:1, :] == expert
        second = ids_ref[1:2, :] == expert
        named = first.astype(jnp.float32) + second.astype(jnp.float32)
        row = lax.broadcasted_iota(jnp.int32, (token_count, token_count), 0)
        column = lax.broadcasted_iota(jnp.int32, (token_count, token_count), 1)
        earlier = (row < column).astype(jnp.bfloat16)
        before = jnp.dot(named.astype(jnp.bfloat16), earlier, preferred_element_type=jnp.float32)
        slot = (line % CAP).astype(jnp.float32)
        hit_first = jnp.where(first & (before == slot), 1.0, 0.0)
        after = before + first.astype(jnp.float32)
        hit_second = jnp.where(second & (after == slot), 1.0, 0.0)
        picker[...] = (hit_first + hit_second).astype(jnp.bfloat16)
        mixer = hit_first * weights_ref[0:1, :] + hit_second * weights_ref[1:2, :]
        high = mixer.astype(jnp.bfloat16).astype(jnp.float32)
        empty = jnp.zeros((LANES - 2 * BLOCK, token_count), jnp.float32)
        stacked = jnp.concatenate([high, mixer - high, empty], axis=0)
        mixer_ref[...] = stacked.T.astype(jnp.bfloat16)

    rows = jnp.dot(picker[...], tokens_ref[...], preferred_element_type=jnp.float32)
    mine_ref[...] = rows[:CAP].astype(jnp.bfloat16)
    theirs_ref[...] = rows[CAP:].astype(jnp.bfloat16)


def dispatch(me, expert_ids, route_weights, tokens):
    token_count, width = tokens.shape
    tile = tile_of(width, 1536)
    whole = lambda j, me: (0, 0)
    column = lambda j, me: (0, j)
    return pl.pallas_call(
        dispatch_kernel,
        grid_spec=pltpu.PrefetchScalarGridSpec(
            num_scalar_prefetch=1,
            grid=(width // tile,),
            in_specs=[
                pl.BlockSpec((2, token_count), whole),
                pl.BlockSpec((2, token_count), whole),
                pl.BlockSpec((token_count, tile), column),
            ],
            out_specs=[
                pl.BlockSpec((CAP, tile), column),
                pl.BlockSpec((CAP, tile), column),
                pl.BlockSpec((token_count, LANES), whole),
            ],
            scratch_shapes=[pltpu.VMEM((BLOCK, token_count), jnp.bfloat16)],
        ),
        out_shape=[
            jax.ShapeDtypeStruct((CAP, width), jnp.bfloat16),
            jax.ShapeDtypeStruct((CAP, width), jnp.bfloat16),
            jax.ShapeDtypeStruct((token_count, LANES), jnp.bfloat16),
        ],
        compiler_params=pltpu.CompilerParams(vmem_limit_bytes=VMEM_LIMIT),
        name="dispatch",
    )(me, in_hbm(expert_ids.T), in_hbm(route_weights.T), in_hbm(tokens))


def hold_kernel(source_ref, held_ref, done):
    copy = pltpu.make_async_copy(source_ref, held_ref, done)
    copy.start()
    copy.wait()


def hold(weights):
    return pl.pallas_call(
        hold_kernel,
        in_specs=[pl.BlockSpec(memory_space=pltpu.HBM)],
        out_specs=pl.BlockSpec(memory_space=pltpu.VMEM),
        out_shape=pltpu.VMEM(weights.shape, weights.dtype),
        scratch_shapes=[pltpu.SemaphoreType.DMA],
        cost_estimate=pl.CostEstimate(
            flops=0, bytes_accessed=2 * weights.size, transcendentals=0
        ),
        compiler_params=pltpu.CompilerParams(vmem_limit_bytes=VMEM_LIMIT),
        name="hold",
    )(in_hbm(weights))


def hidden_kernel(count, *refs):
    rows, (gate_ref, up_ref, out_ref) = refs[:count], refs[count:]
    block = jnp.concatenate([r[...] for r in rows], axis=0)
    width = out_ref.shape[1]
    tile = tile_of(width, 256)

    @pl.loop(0, width // tile)
    def _(j):
        here = pl.ds(pl.multiple_of(j * tile, tile), tile)
        gate = jnp.dot(block, gate_ref[:, here], preferred_element_type=jnp.float32)
        up = jnp.dot(block, up_ref[:, here], preferred_element_type=jnp.float32)
        out_ref[:, here] = (gate / (1.0 + jnp.exp(-gate)) * up).astype(jnp.bfloat16)


def hidden_of(rows, w_gate, w_up):
    depth, width = w_gate.shape
    total = sum(r.shape[0] for r in rows)
    local = pl.BlockSpec(memory_space=pltpu.VMEM)
    return pl.pallas_call(
        lambda *refs: hidden_kernel(len(rows), *refs),
        in_specs=[local] * (len(rows) + 2),
        out_specs=local,
        out_shape=jax.ShapeDtypeStruct((total, width), jnp.bfloat16),
        cost_estimate=pl.CostEstimate(
            flops=4 * total * depth * width,
            bytes_accessed=4 * depth * width,
            transcendentals=total * width,
        ),
        compiler_params=pltpu.CompilerParams(vmem_limit_bytes=VMEM_LIMIT),
        name="hidden",
    )(*rows, w_gate, w_up)


def product_kernel(start, count, hidden_ref, down_ref, out_ref):
    width = out_ref.shape[1]
    tile = tile_of(width, 512)
    block = hidden_ref[start : start + count, :]

    @pl.loop(0, width // tile)
    def _(j):
        here = pl.ds(pl.multiple_of(j * tile, tile), tile)
        out_ref[:, here] = jnp.dot(
            block, down_ref[:, here], preferred_element_type=jnp.float32
        ).astype(jnp.bfloat16)


def product_of(hidden, start, count, w_down):
    depth, width = w_down.shape
    local = pl.BlockSpec(memory_space=pltpu.VMEM)
    return pl.pallas_call(
        lambda *refs: product_kernel(start, count, *refs),
        in_specs=[local, local],
        out_specs=local,
        out_shape=jax.ShapeDtypeStruct((count, width), jnp.bfloat16),
        cost_estimate=pl.CostEstimate(
            flops=2 * count * depth * width, bytes_accessed=2 * depth * width, transcendentals=0
        ),
        compiler_params=pltpu.CompilerParams(vmem_limit_bytes=VMEM_LIMIT),
        name="product",
    )(hidden, pltpu.with_memory_space_constraint(w_down, pltpu.VMEM))


def combine_kernel(own_ref, ahead_ref, behind_ref, theirs_ref, mixer_ref, out_ref):
    mine = (
        own_ref[...].astype(jnp.float32)
        + ahead_ref[...].astype(jnp.float32)
        + behind_ref[...].astype(jnp.float32)
    ).astype(jnp.bfloat16)
    theirs = theirs_ref[...]
    rows = jnp.concatenate([mine, theirs, mine, theirs], axis=0)
    out_ref[...] = jnp.dot(
        mixer_ref[:, : 2 * BLOCK], rows, preferred_element_type=jnp.float32
    ).astype(jnp.bfloat16)


def combine(own, ahead, behind, theirs, mixer):
    width = own.shape[1]
    token_count = mixer.shape[0]
    tile = tile_of(width, 1536)
    part = pl.BlockSpec((CAP, tile), lambda j: (0, j))
    return pl.pallas_call(
        combine_kernel,
        grid=(width // tile,),
        in_specs=[part, part, part, part, pl.BlockSpec(mixer.shape, lambda j: (0, 0))],
        out_specs=pl.BlockSpec((token_count, tile), lambda j: (0, j)),
        out_shape=jax.ShapeDtypeStruct((token_count, width), jnp.bfloat16),
        compiler_params=pltpu.CompilerParams(vmem_limit_bytes=VMEM_LIMIT),
        name="combine",
    )(own, ahead, behind, theirs, mixer)


def body(tokens, expert_ids, route_weights, w_gate, w_up, w_down):
    ept_count = lax.axis_size("ept")
    forward, backward = ring_pairs(ept_count, 2 if ept_count == 8 else 1)
    reach = ept_count // 2
    half = tokens.shape[1] // 2
    w_gate, w_up, w_down = w_gate[0], w_up[0], w_down[0]
    me = lax.axis_index("exp").astype(jnp.int32).reshape(1)
    mine, theirs, mixer = dispatch(me, expert_ids, route_weights, tokens)
    own = jnp.concatenate([mine, swap(theirs)], axis=0)

    ahead = behind = own
    arrived = [(own,)]
    held = []
    for k in range(1, reach):
        if k > 1 and len(held) < 2:
            weights = hold((w_gate, w_up)[len(held)])
            ahead, behind, weights = lax.optimization_barrier((ahead, behind, weights))
            held.append(pltpu.with_memory_space_constraint(weights, pltpu.VMEM))
        ahead = lax.ppermute(ahead, "ept", forward)
        behind = lax.ppermute(behind, "ept", backward)
        arrived.append((behind, ahead))
    w_gate, w_up = held
    early = [r for k in range(reach - 1) for r in arrived[reach - 2 - k]]
    hidden_early = hidden_of(early, w_gate, w_up)
    ahead, behind, w_down, hidden_early = lax.optimization_barrier((ahead, behind, w_down, hidden_early))
    ahead = lax.ppermute(ahead[:, :half], "ept", forward)
    behind = lax.ppermute(behind[:, half:], "ept", backward)
    w_down = hold(w_down)
    arrived.append((jnp.concatenate([ahead, behind], axis=1),))
    late = [r for k in (reach - 1, reach) for r in arrived[k]]
    hidden_late = hidden_of(late, w_gate, w_up)

    def product_at(k):
        if k == reach:
            return product_of(hidden_late, 2 * BLOCK, BLOCK, w_down)
        if k == reach - 1:
            return product_of(hidden_late, 0, 2 * BLOCK, w_down)
        return product_of(
            hidden_early, 2 * BLOCK * (reach - 2 - k), 2 * BLOCK if k else BLOCK, w_down
        )

    product = product_at(reach)
    ahead = lax.ppermute(product[:, :half], "ept", forward)
    behind = lax.ppermute(product[:, half:], "ept", backward)
    for k in reversed(range(1, reach)):
        product = product_at(k)
        to_ahead, to_behind = product[:BLOCK], product[BLOCK:]
        if k == reach - 1:
            to_ahead = jnp.concatenate([to_ahead[:, :half] + ahead, to_ahead[:, half:]], axis=1)
            to_behind = jnp.concatenate([to_behind[:, :half], to_behind[:, half:] + behind], axis=1)
        else:
            to_ahead += ahead
            to_behind += behind
        ahead = lax.ppermute(to_ahead, "ept", forward)
        behind = lax.ppermute(to_behind, "ept", backward)
    product = product_at(0)
    for_theirs = (
        product[CAP:].astype(jnp.float32)
        + ahead[CAP:].astype(jnp.float32)
        + behind[CAP:].astype(jnp.float32)
    ).astype(jnp.bfloat16)
    return combine(product, ahead, behind, swap(for_theirs), mixer)


def solution(mesh):
    placed = (
        P(("groups", "ept", "exp"), None),
        P(("groups", "ept", "exp"), None),
        P(("groups", "ept", "exp"), None),
        P("exp", None, "ept"),
        P("exp", None, "ept"),
        P("exp", "ept", None),
    )
    return jax.shard_map(
        body,
        mesh=mesh,
        in_specs=placed,
        out_specs=P(("groups", "ept", "exp"), None),
        check_vma=False,
    )
```

time: 214 us -> 103 us (0.48)
  waiting for transfers between devices: 135 us -> 35.3 us
  Pallas kernels: 0 us -> 47.6 us
  matrix products: 21.1 us -> 0 us
  other arithmetic: 19.4 us -> 0.4 us
  starting transfers between devices: 0.04 us -> 18.1 us
  local copies, waits for them, and re-layouts: 14.2 us -> 0.79 us
  between operations: 13.5 us -> 0.23 us
  blocking collectives: 9.89 us -> 0 us
    reduce_scatter x1 -> x0, waiting for transfers between devices: 71.8 us -> none  [body(): lax.psum_scatter(jnp.stack(pieces, axis=1).reshape(row_count, local_count...]
    all_gather x1 -> x0, waiting for transfers between devices: 63.3 us -> none  [body(): gathered = lax.all_gather(incoming, 'ept', axis=0, tiled=True)]
    pallas_call x0 -> x12, Pallas kernels: none -> 47.6 us  [the longest x5 17.8 us: product_of(): pl.pallas_call(lambda *refs: product_kernel(start, count, *refs), in_spec...]
    ppermute x0 -> x18, waiting for transfers between devices: none -> 35.3 us  [the longest x3 10.2 us: body(): behind = lax.ppermute(to_behind, 'ept', backward)]
    dot_general x4 -> x0, matrix products: 21.1 us -> none  [the longest x1 8.5 us: body(): jnp.dot(row_block, w_up[expert], preferred_element_type=jnp.float32)]
    ppermute x0 -> x18, starting transfers between devices: none -> 18.1 us  [the longest x3 5.07 us: body(): behind = lax.ppermute(behind, 'ept', backward)]
    reduce_sum x3 -> x0, other arithmetic: 17.1 us -> none  [the longest x1 17 us: body(): jnp.sum((picked * scaled[:, None]).reshape(token_count, choices_per, mode...]
    gather x2 -> x0, local copies, waits for them, and re-layouts: 11.2 us -> none  [body(): picked = jnp.take(flat_rows, row_index, axis=0).astype(jnp.float32)]
  transfers between devices with their start and end apart: 2 -> 18, of which waited for: 2 -> 16; matrix products, arithmetic and copies ran while one was open for 0% -> 0% of each run, Pallas kernels for 0% -> 33%
where the time goes in v1:
time: 103 us; the launch traced here: 102 us
  Pallas kernels  47.6 us (46%)
  waiting for transfers between devices  35.3 us (34%)
  starting transfers between devices  18.1 us (18%)
    pallas_call x5, Pallas kernels, product_of(): pl.pallas_call(lambda *refs: product_kernel(start, count, *refs), in_spec...  17.8 us
    pallas_call x3, Pallas kernels, hold(): pl.pallas_call(hold_kernel, in_specs=[pl.BlockSpec(memory_space=pltpu.HBM...  14.5 us
    ppermute x3, waiting for transfers between devices, body(): behind = lax.ppermute(to_behind, 'ept', backward)  10.2 us
    pallas_call x2, Pallas kernels, hidden_of(): pl.pallas_call(lambda *refs: hidden_kernel(len(rows), *refs), in_specs=[l...  9.96 us
    ppermute x3, waiting for transfers between devices, body(): behind = lax.ppermute(behind, 'ept', backward)  6.75 us
    ppermute x3, waiting for transfers between devices, body(): ahead = lax.ppermute(ahead, 'ept', forward)  6.72 us
    ppermute x3, waiting for transfers between devices, body(): ahead = lax.ppermute(to_ahead, 'ept', forward)  6.65 us
    ppermute x3, starting transfers between devices, body(): behind = lax.ppermute(behind, 'ept', backward)  5.07 us
  transfers between devices with their start and end apart: 18, of which 16 were waited for; matrix products, arithmetic and copies ran while one was open for 0% of the time, Pallas kernels for 33%

profile of v1, /device:TPU:0, one launch (start us, length us, event | category | flops | bytes accessed | tf_op | source)
XLA Modules:
  0.0 102.5 jit_solution(17071945349701162813)
XLA Ops:
  0.0 2.9 %dispatch.1 = (bf16[16,6144]{1,0:T(8,128)(2,1)S(1)}, bf16[16,6144]{1,0:T(8,128)(2,1)S(1)}, bf16[128,128]{1,0:T(8,128)(2,1)S(1)}) custom-call(s32[1]{0:T(128)} %bitcast.me_ref, s32[2,128]{1,0:T(2,128)} %bitcast.11, f32[2,128]{1,0:T(2,128)} %bitcast.12, bf16[128,6144]{1,0:T(8,128)(2,1)} %tokens_ref.1), custom_call_target="tpu_custom_call" | custom-call | tf_op jit(solution)/shard_map/dispatch/pallas_call | solution.py:70
  4.5 2.9 %collective-permute-start.2 = (bf16[32,6144]{1,0:T(8,128)(2,1)S(1)}, bf16[32,6144]{1,0:T(8,128)(2,1)S(1)}, u32[]{:S(2)}, u32[]{:S(2)}) collective-permute-start(bf16[32,6144]{1,0:T(8,128)(2,1)S(1)} %constant_dynamic-update-slice_fusion.refs_4_), channel_id=1, source_target_pairs={{4,0},{8,4},{12,8},{14,12},{10,14},{6,10},{2,6},{0,2},{5,1},{9,5},... | collective-permute-start | bytes 1179656 | tf_op jit(solution)/shard_map/ppermute | solution.py:228
  7.6 4.6 %hold.3.refs_5_.refs_3_ = bf16[6144,1024]{1,0:T(8,128)(2,1)S(1)} custom-call(bf16[6144,1024]{1,0:T(8,128)(2,1)} %bitcast.8), custom_call_target="tpu_custom_call" | custom-call | bytes 12582912 | tf_op jit(solution)/shard_map/hold/pallas_call | solution.py:104
  12.2 4.8 %collective-permute-done.2.refs_2_ = bf16[32,6144]{1,0:T(8,128)(2,1)S(1)} collective-permute-done((bf16[32,6144]{1,0:T(8,128)(2,1)S(1)}, bf16[32,6144]{1,0:T(8,128)(2,1)S(1)}, u32[]{:S(2)}, u32[]{:S(2)}) %collective-permute-start.2) | collective-permute-done | bytes 393248 | tf_op jit(solution)/shard_map/ppermute | solution.py:228
  16.9 1.4 %collective-permute-done.1.refs_3_ = bf16[32,6144]{1,0:T(8,128)(2,1)S(1)} collective-permute-done((bf16[32,6144]{1,0:T(8,128)(2,1)S(1)}, bf16[32,6144]{1,0:T(8,128)(2,1)S(1)}, u32[]{:S(2)}, u32[]{:S(2)}) %collective-permute-start.1) | collective-permute-done | bytes 393248 | tf_op jit(solution)/shard_map/ppermute | solution.py:227
  18.7 1.6 %collective-permute-start.4 = (bf16[32,6144]{1,0:T(8,128)(2,1)S(1)}, bf16[32,6144]{1,0:T(8,128)(2,1)S(1)}, u32[]{:S(2)}, u32[]{:S(2)}) collective-permute-start(bf16[32,6144]{1,0:T(8,128)(2,1)S(1)} %collective-permute-done.2.refs_2_), channel_id=1, source_target_pairs={{4,0},{8,4},{12,8},{14,12},{10,14},{6,10},{2,6},{0,2},{5,1},{9,5},... | collective-permute-start | bytes 1179656 | tf_op jit(solution)/shard_map/ppermute | solution.py:228
  20.4 4.6 %hold.4.refs_6_.refs_4_ = bf16[6144,1024]{1,0:T(8,128)(2,1)S(1)} custom-call(bf16[6144,1024]{1,0:T(8,128)(2,1)} %bitcast.9), custom_call_target="tpu_custom_call" | custom-call | bytes 12582912 | tf_op jit(solution)/shard_map/hold/pallas_call | solution.py:104
  25.0 3.4 %collective-permute-done.3.refs_1_ = bf16[32,6144]{1,0:T(8,128)(2,1)S(1)} collective-permute-done((bf16[32,6144]{1,0:T(8,128)(2,1)S(1)}, bf16[32,6144]{1,0:T(8,128)(2,1)S(1)}, u32[]{:S(2)}, u32[]{:S(2)}) %collective-permute-start.3) | collective-permute-done | bytes 393248 | tf_op jit(solution)/shard_map/ppermute | solution.py:227
  28.8 1.5 %collective-permute-start.5 = (bf16[32,6144]{1,0:T(8,128)(2,1)S(1)}, bf16[32,6144]{1,0:T(8,128)(2,1)S(1)}, u32[]{:S(2)}, u32[]{:S(2)}) collective-permute-start(bf16[32,6144]{1,0:T(8,128)(2,1)S(1)} %collective-permute-done.3.refs_1_), channel_id=1, source_target_pairs={{0,4},{4,8},{8,12},{12,14},{14,10},{10,6},{6,2},{2,0},{1,5},{5,9},... | collective-permute-start | bytes 1179656 | tf_op jit(solution)/shard_map/ppermute | solution.py:227
  30.8 5.1 %hidden.2.refs_0_ = bf16[160,1024]{1,0:T(8,128)(2,1)S(1)} custom-call(bf16[32,6144]{1,0:T(8,128)(2,1)S(1)} %collective-permute-done.4.refs_0_, bf16[32,6144]{1,0:T(8,128)(2,1)S(1)} %collective-permute-done.3.refs_1_, bf16[32,6144]{1,0:T(8,128)(2,1)S(1)} %collective-permute-done.2.refs_2_, bf16[32,6144]{1,0:T(8,128)(2,1)S(1)} %collective-permute-done.1.refs_3_, ...), custom_call_target="tpu_custom_call" | custom-call | flops 4026531840 | bytes 25165824 | tf_op jit(solution)/shard_map/hidden/pallas_call | solution.py:136
  36.0 1.9 %collective-permute-done.5.refs_1_ = bf16[32,6144]{1,0:T(8,128)(2,1)S(1)} collective-permute-done((bf16[32,6144]{1,0:T(8,128)(2,1)S(1)}, bf16[32,6144]{1,0:T(8,128)(2,1)S(1)}, u32[]{:S(2)}, u32[]{:S(2)}) %collective-permute-start.5) | collective-permute-done | bytes 393248 | tf_op jit(solution)/shard_map/ppermute | solution.py:227
  37.9 1.5 %collective-permute-done.6.refs_0_ = bf16[32,6144]{1,0:T(8,128)(2,1)S(1)} collective-permute-done((bf16[32,6144]{1,0:T(8,128)(2,1)S(1)}, bf16[32,6144]{1,0:T(8,128)(2,1)S(1)}, u32[]{:S(2)}, u32[]{:S(2)}) %collective-permute-start.6) | collective-permute-done | bytes 393248 | tf_op jit(solution)/shard_map/ppermute | solution.py:228
  40.1 1.5 %collective-permute-start.7 = (bf16[32,3072]{1,0:T(8,128)(2,1)S(1)}, bf16[32,3072]{1,0:T(8,128)(2,1)S(1)}, u32[]{:S(2)}, u32[]{:S(2)}) collective-permute-start(bf16[32,3072]{1,0:T(8,128)(2,1)S(1)} %slice.53), channel_id=1, source_target_pairs={{0,4},{4,8},{8,12},{12,14},{14,10},{10,6},{6,2},{2,0},{1,5},{5,9},... | collective-permute-start | bytes 589832 | tf_op jit(solution)/shard_map/ppermute | solution.py:234
  41.6 5.4 %hold.5.refs_1_ = bf16[1024,6144]{1,0:T(8,128)(2,1)S(1)} custom-call(bf16[1024,6144]{1,0:T(8,128)(2,1)} %bitcast.10), custom_call_target="tpu_custom_call" | custom-call | bytes 12582912 | tf_op jit(solution)/shard_map/hold/pallas_call | solution.py:104
  47.7 4.8 %hidden.3.refs_0_ = bf16[96,1024]{1,0:T(8,128)(2,1)S(1)} custom-call(bf16[32,6144]{1,0:T(8,128)(2,1)S(1)} %collective-permute-done.6.refs_0_, bf16[32,6144]{1,0:T(8,128)(2,1)S(1)} %collective-permute-done.5.refs_1_, bf16[32,6144]{1,0:T(8,128)(2,1)S(1)} %pad_maximum_fusion.refs_2_, bf16[6144,1024]{1,0:T(8,128)(2,1)S(1)} %hold.3.refs_5_.refs_3_, ...), custom_call_target="tpu_custom_call" | custom-call | flops 2415919104 | bytes 25165824 | tf_op jit(solution)/shard_map/hidden/pallas_call | solution.py:136
  52.6 3.5 %product.9 = bf16[32,6144]{1,0:T(8,128)(2,1)S(1)} custom-call(bf16[96,1024]{1,0:T(8,128)(2,1)S(1)} %hidden.3.refs_0_, bf16[1024,6144]{1,0:T(8,128)(2,1)S(1)} %hold.5.refs_1_), custom_call_target="tpu_custom_call" | custom-call | flops 402653184 | bytes 12582912 | tf_op jit(solution)/shard_map/product/pallas_call | solution.py:167
  56.7 1.5 %collective-permute-start.9 = (bf16[32,3072]{1,0:T(8,128)(2,1)S(1)}, bf16[32,3072]{1,0:T(8,128)(2,1)S(1)}, u32[]{:S(2)}, u32[]{:S(2)}) collective-permute-start(bf16[32,3072]{1,0:T(8,128)(2,1)S(1)} %get-tuple-element.40), channel_id=1, source_target_pairs={{0,4},{4,8},{8,12},{12,14},{14,10},{10,6},{6,2},{2,0},{1,5},{5,9},... | collective-permute-start | bytes 589832 | tf_op jit(solution)/shard_map/ppermute | solution.py:251
  58.2 3.6 %product.8 = bf16[64,6144]{1,0:T(8,128)(2,1)S(1)} custom-call(bf16[96,1024]{1,0:T(8,128)(2,1)S(1)} %hidden.3.refs_0_, bf16[1024,6144]{1,0:T(8,128)(2,1)S(1)} %hold.5.refs_1_), custom_call_target="tpu_custom_call" | custom-call | flops 805306368 | bytes 12582912 | tf_op jit(solution)/shard_map/product/pallas_call | solution.py:167
  61.9 2.5 %collective-permute-done.9 = bf16[32,3072]{1,0:T(8,128)(2,1)S(1)} collective-permute-done((bf16[32,3072]{1,0:T(8,128)(2,1)S(1)}, bf16[32,3072]{1,0:T(8,128)(2,1)S(1)}, u32[]{:S(2)}, u32[]{:S(2)}) %collective-permute-start.9) | collective-permute-done | bytes 196640 | tf_op jit(solution)/shard_map/ppermute | solution.py:251
  64.5 1.5 %collective-permute-start.10 = (bf16[32,6144]{1,0:T(8,128)(2,1)S(1)}, bf16[32,6144]{1,0:T(8,128)(2,1)S(1)}, u32[]{:S(2)}, u32[]{:S(2)}) collective-permute-start(bf16[32,6144]{1,0:T(8,128)(2,1)S(1)} %pad_maximum_fusion.1), channel_id=1, source_target_pairs={{0,4},{4,8},{8,12},{12,14},{14,10},{10,6},{6,2},{2,0},{1,5},{5,9},... | collective-permute-start | bytes 1179656 | tf_op jit(solution)/shard_map/ppermute | solution.py:262
  66.6 3.6 %product.7 = bf16[64,6144]{1,0:T(8,128)(2,1)S(1)} custom-call(bf16[160,1024]{1,0:T(8,128)(2,1)S(1)} %hidden.2.refs_0_, bf16[1024,6144]{1,0:T(8,128)(2,1)S(1)} %hold.5.refs_1_), custom_call_target="tpu_custom_call" | custom-call | flops 805306368 | bytes 12582912 | tf_op jit(solution)/shard_map/product/pallas_call | solution.py:167
  70.3 4.4 %collective-permute-done.10 = bf16[32,6144]{1,0:T(8,128)(2,1)S(1)} collective-permute-done((bf16[32,6144]{1,0:T(8,128)(2,1)S(1)}, bf16[32,6144]{1,0:T(8,128)(2,1)S(1)}, u32[]{:S(2)}, u32[]{:S(2)}) %collective-permute-start.10) | collective-permute-done | bytes 393248 | tf_op jit(solution)/shard_map/ppermute | solution.py:262
  74.7 2.9 %collective-permute-done.14 = bf16[32,6144]{1,0:T(8,128)(2,1)S(1)} collective-permute-done((bf16[32,6144]{1,0:T(8,128)(2,1)S(1)}, bf16[32,6144]{1,0:T(8,128)(2,1)S(1)}, u32[]{:S(2)}, u32[]{:S(2)}) %collective-permute-start.14) | collective-permute-done | bytes 393248 | tf_op jit(solution)/shard_map/ppermute | solution.py:263
  77.6 1.1 %collective-permute-start.15 = (bf16[32,6144]{1,0:T(8,128)(2,1)S(1)}, bf16[32,6144]{1,0:T(8,128)(2,1)S(1)}, u32[]{:S(2)}, u32[]{:S(2)}) collective-permute-start(bf16[32,6144]{1,0:T(8,128)(2,1)S(1)} %get-tuple-element.33), channel_id=1, source_target_pairs={{4,0},{8,4},{12,8},{14,12},{10,14},{6,10},{2,6},{0,2},{5,1},{9,5},... | collective-permute-start | bytes 1179656 | tf_op jit(solution)/shard_map/ppermute | solution.py:263
  79.7 3.6 %product.6 = bf16[64,6144]{1,0:T(8,128)(2,1)S(1)} custom-call(bf16[160,1024]{1,0:T(8,128)(2,1)S(1)} %hidden.2.refs_0_, bf16[1024,6144]{1,0:T(8,128)(2,1)S(1)} %hold.5.refs_1_), custom_call_target="tpu_custom_call" | custom-call | flops 805306368 | bytes 12582912 | tf_op jit(solution)/shard_map/product/pallas_call | solution.py:167
  83.3 5.0 %collective-permute-done.15 = bf16[32,6144]{1,0:T(8,128)(2,1)S(1)} collective-permute-done((bf16[32,6144]{1,0:T(8,128)(2,1)S(1)}, bf16[32,6144]{1,0:T(8,128)(2,1)S(1)}, u32[]{:S(2)}, u32[]{:S(2)}) %collective-permute-start.15) | collective-permute-done | bytes 393248 | tf_op jit(solution)/shard_map/ppermute | solution.py:263
  88.4 1.2 %collective-permute-done.11 = bf16[32,6144]{1,0:T(8,128)(2,1)S(1)} collective-permute-done((bf16[32,6144]{1,0:T(8,128)(2,1)S(1)}, bf16[32,6144]{1,0:T(8,128)(2,1)S(1)}, u32[]{:S(2)}, u32[]{:S(2)}) %collective-permute-start.11) | collective-permute-done | bytes 393248 | tf_op jit(solution)/shard_map/ppermute | solution.py:262
  89.6 1.1 %collective-permute-start.16 = (bf16[32,6144]{1,0:T(8,128)(2,1)S(1)}, bf16[32,6144]{1,0:T(8,128)(2,1)S(1)}, u32[]{:S(2)}, u32[]{:S(2)}) collective-permute-start(bf16[32,6144]{1,0:T(8,128)(2,1)S(1)} %get-tuple-element.31), channel_id=1, source_target_pairs={{4,0},{8,4},{12,8},{14,12},{10,14},{6,10},{2,6},{0,2},{5,1},{9,5},... | collective-permute-start | bytes 1179656 | tf_op jit(solution)/shard_map/ppermute | solution.py:263
  91.7 3.5 %product.5.own_ref = bf16[32,6144]{1,0:T(8,128)(2,1)S(1)} custom-call(bf16[160,1024]{1,0:T(8,128)(2,1)S(1)} %hidden.2.refs_0_, bf16[1024,6144]{1,0:T(8,128)(2,1)S(1)} %hold.5.refs_1_), custom_call_target="tpu_custom_call" | custom-call | flops 402653184 | bytes 12582912 | tf_op jit(solution)/shard_map/product/pallas_call | solution.py:167
  95.2 2.3 %collective-permute-done.16.behind_ref = bf16[32,6144]{1,0:T(8,128)(2,1)S(1)} collective-permute-done((bf16[32,6144]{1,0:T(8,128)(2,1)S(1)}, bf16[32,6144]{1,0:T(8,128)(2,1)S(1)}, u32[]{:S(2)}, u32[]{:S(2)}) %collective-permute-start.16) | collective-permute-done | bytes 393248 | tf_op jit(solution)/shard_map/ppermute | solution.py:263
  98.7 1.4 %collective-permute-done.17.theirs_ref = bf16[16,6144]{1,0:T(8,128)(2,1)S(1)} collective-permute-done((bf16[16,6144]{1,0:T(8,128)(2,1)S(1)}, bf16[16,6144]{1,0:T(8,128)(2,1)S(1)}, u32[]{:S(2)}, u32[]{:S(2)}) %collective-permute-start.17) | collective-permute-done | bytes 196640 | tf_op jit(solution)/shard_map/ppermute | solution.py:25
  100.1 2.3 %combine.1 = bf16[128,6144]{1,0:T(8,128)(2,1)} custom-call(bf16[32,6144]{1,0:T(8,128)(2,1)S(1)} %product.5.own_ref, bf16[32,6144]{1,0:T(8,128)(2,1)S(1)} %collective-permute-done.12.ahead_ref, bf16[32,6144]{1,0:T(8,128)(2,1)S(1)} %collective-permute-done.16.behind_ref, bf16[16,6144]{1,0:T(8,128)(2,1)S(1)} %collective-permute-done.17.theirs_ref, ...), custom_call_target="tpu_custom_call" | custom-call | tf_op jit(solution)/shard_map/combine/pallas_call | solution.py:198
  (37 shorter events, 9.2 us)
Async XLA Ops:
  2.9 1.6 %collective-permute-start = (bf16[16,6144]{1,0:T(8,128)(2,1)S(1)}, bf16[16,6144]{1,0:T(8,128)(2,1)S(1)}, u32[]{:S(2)}, u32[]{:S(2)}) collective-permute-start(bf16[16,6144]{1,0:T(8,128)(2,1)S(1)} %get-tuple-element.19), channel_id=1, source_target_pairs={{0,1},{1,0},{2,3},{3,2},{4,5},{5,4},{6,7},{7,6},{8,9},{9,8},{10,11... | collective-permute-start | bytes 589832 | tf_op jit(solution)/shard_map/ppermute | solution.py:25
  4.5 12.4 %collective-permute-start.2 = (bf16[32,6144]{1,0:T(8,128)(2,1)S(1)}, bf16[32,6144]{1,0:T(8,128)(2,1)S(1)}, u32[]{:S(2)}, u32[]{:S(2)}) collective-permute-start(bf16[32,6144]{1,0:T(8,128)(2,1)S(1)} %constant_dynamic-update-slice_fusion.refs_4_), channel_id=1, source_target_pairs={{4,0},{8,4},{12,8},{14,12},{10,14},{6,10},{2,6},{0,2},{5,1},{9,5},... | collective-permute-start | bytes 1179656 | tf_op jit(solution)/shard_map/ppermute | solution.py:228
  7.5 10.9 %collective-permute-start.1 = (bf16[32,6144]{1,0:T(8,128)(2,1)S(1)}, bf16[32,6144]{1,0:T(8,128)(2,1)S(1)}, u32[]{:S(2)}, u32[]{:S(2)}) collective-permute-start(bf16[32,6144]{1,0:T(8,128)(2,1)S(1)} %constant_dynamic-update-slice_fusion.refs_4_), channel_id=1, source_target_pairs={{0,4},{4,8},{8,12},{12,14},{14,10},{10,6},{6,2},{2,0},{1,5},{5,9},... | collective-permute-start | bytes 1179656 | tf_op jit(solution)/shard_map/ppermute | solution.py:227
  18.3 10.0 %collective-permute-start.3 = (bf16[32,6144]{1,0:T(8,128)(2,1)S(1)}, bf16[32,6144]{1,0:T(8,128)(2,1)S(1)}, u32[]{:S(2)}, u32[]{:S(2)}) collective-permute-start(bf16[32,6144]{1,0:T(8,128)(2,1)S(1)} %collective-permute-done.1.refs_3_), channel_id=1, source_target_pairs={{0,4},{4,8},{8,12},{12,14},{14,10},{10,6},{6,2},{2,0},{1,5},{5,9},... | collective-permute-start | bytes 1179656 | tf_op jit(solution)/shard_map/ppermute | solution.py:227
  18.7 10.0 %collective-permute-start.4 = (bf16[32,6144]{1,0:T(8,128)(2,1)S(1)}, bf16[32,6144]{1,0:T(8,128)(2,1)S(1)}, u32[]{:S(2)}, u32[]{:S(2)}) collective-permute-start(bf16[32,6144]{1,0:T(8,128)(2,1)S(1)} %collective-permute-done.2.refs_2_), channel_id=1, source_target_pairs={{4,0},{8,4},{12,8},{14,12},{10,14},{6,10},{2,6},{0,2},{5,1},{9,5},... | collective-permute-start | bytes 1179656 | tf_op jit(solution)/shard_map/ppermute | solution.py:228
  25.0 11.0 %copy-start = (bf16[6144,1024]{1,0:T(8,128)(2,1)}, bf16[6144,1024]{1,0:T(8,128)(2,1)S(1)}, u32[]{:S(2)}) copy-start(bf16[6144,1024]{1,0:T(8,128)(2,1)S(1)} %hold.4.refs_6_.refs_4_) | copy-start | bytes 37748740
  28.8 9.1 %collective-permute-start.5 = (bf16[32,6144]{1,0:T(8,128)(2,1)S(1)}, bf16[32,6144]{1,0:T(8,128)(2,1)S(1)}, u32[]{:S(2)}, u32[]{:S(2)}) collective-permute-start(bf16[32,6144]{1,0:T(8,128)(2,1)S(1)} %collective-permute-done.3.refs_1_), channel_id=1, source_target_pairs={{0,4},{4,8},{8,12},{12,14},{14,10},{10,6},{6,2},{2,0},{1,5},{5,9},... | collective-permute-start | bytes 1179656 | tf_op jit(solution)/shard_map/ppermute | solution.py:227
  30.3 9.2 %collective-permute-start.6 = (bf16[32,6144]{1,0:T(8,128)(2,1)S(1)}, bf16[32,6144]{1,0:T(8,128)(2,1)S(1)}, u32[]{:S(2)}, u32[]{:S(2)}) collective-permute-start(bf16[32,6144]{1,0:T(8,128)(2,1)S(1)} %collective-permute-done.4.refs_0_), channel_id=1, source_target_pairs={{4,0},{8,4},{12,8},{14,12},{10,14},{6,10},{2,6},{0,2},{5,1},{9,5},... | collective-permute-start | bytes 1179656 | tf_op jit(solution)/shard_map/ppermute | solution.py:228
  39.5 7.6 %slice-start = ((s8[12582912]{0:T(1024)(128)(4,1)}), s8[4194304]{0:T(1024)(128)(4,1)S(1)}, s32[]{:S(2)}) async-start(s8[12582912]{0:T(1024)(128)(4,1)} %bitcast.6), calls=%async_computation | async-start | bytes 8388608
  39.5 7.5 %slice-start.1 = ((s8[12582912]{0:T(1024)(128)(4,1)}), s8[4194304]{0:T(1024)(128)(4,1)S(1)}, s32[]{:S(2)}) async-start(s8[12582912]{0:T(1024)(128)(4,1)} %bitcast.6), calls=%async_computation.1 | async-start | bytes 8388608
  39.5 8.2 %slice-start.2 = ((s8[12582912]{0:T(1024)(128)(4,1)}), s8[4194304]{0:T(1024)(128)(4,1)S(1)}, s32[]{:S(2)}) async-start(s8[12582912]{0:T(1024)(128)(4,1)} %bitcast.6), calls=%async_computation.2 | async-start | bytes 8388608
  39.5 7.4 %collective-permute-start.8 = (bf16[32,3072]{1,0:T(8,128)(2,1)S(1)}, bf16[32,3072]{1,0:T(8,128)(2,1)S(1)}, u32[]{:S(2)}, u32[]{:S(2)}) collective-permute-start(bf16[32,3072]{1,0:T(8,128)(2,1)S(1)} %slice.54), channel_id=1, source_target_pairs={{4,0},{8,4},{12,8},{14,12},{10,14},{6,10},{2,6},{0,2},{5,1},{9,5},... | collective-permute-start | bytes 589832 | tf_op jit(solution)/shard_map/ppermute | solution.py:235
  40.1 6.9 %collective-permute-start.7 = (bf16[32,3072]{1,0:T(8,128)(2,1)S(1)}, bf16[32,3072]{1,0:T(8,128)(2,1)S(1)}, u32[]{:S(2)}, u32[]{:S(2)}) collective-permute-start(bf16[32,3072]{1,0:T(8,128)(2,1)S(1)} %slice.53), channel_id=1, source_target_pairs={{0,4},{4,8},{8,12},{12,14},{14,10},{10,6},{6,2},{2,0},{1,5},{5,9},... | collective-permute-start | bytes 589832 | tf_op jit(solution)/shard_map/ppermute | solution.py:234
  56.1 5.8 %collective-permute-start.13 = (bf16[32,3072]{1,0:T(8,128)(2,1)S(1)}, bf16[32,3072]{1,0:T(8,128)(2,1)S(1)}, u32[]{:S(2)}, u32[]{:S(2)}) collective-permute-start(bf16[32,3072]{1,0:T(8,128)(2,1)S(1)} %get-tuple-element.39), channel_id=1, source_target_pairs={{4,0},{8,4},{12,8},{14,12},{10,14},{6,10},{2,6},{0,2},{5,1},{9,5},... | collective-permute-start | bytes 589832 | tf_op jit(solution)/shard_map/ppermute | solution.py:252
  56.7 7.7 %collective-permute-start.9 = (bf16[32,3072]{1,0:T(8,128)(2,1)S(1)}, bf16[32,3072]{1,0:T(8,128)(2,1)S(1)}, u32[]{:S(2)}, u32[]{:S(2)}) collective-permute-start(bf16[32,3072]{1,0:T(8,128)(2,1)S(1)} %get-tuple-element.40), channel_id=1, source_target_pairs={{0,4},{4,8},{8,12},{12,14},{14,10},{10,6},{6,2},{2,0},{1,5},{5,9},... | collective-permute-start | bytes 589832 | tf_op jit(solution)/shard_map/ppermute | solution.py:251
  64.5 10.2 %collective-permute-start.10 = (bf16[32,6144]{1,0:T(8,128)(2,1)S(1)}, bf16[32,6144]{1,0:T(8,128)(2,1)S(1)}, u32[]{:S(2)}, u32[]{:S(2)}) collective-permute-start(bf16[32,6144]{1,0:T(8,128)(2,1)S(1)} %pad_maximum_fusion.1), channel_id=1, source_target_pairs={{0,4},{4,8},{8,12},{12,14},{14,10},{10,6},{6,2},{2,0},{1,5},{5,9},... | collective-permute-start | bytes 1179656 | tf_op jit(solution)/shard_map/ppermute | solution.py:262
  66.0 11.5 %collective-permute-start.14 = (bf16[32,6144]{1,0:T(8,128)(2,1)S(1)}, bf16[32,6144]{1,0:T(8,128)(2,1)S(1)}, u32[]{:S(2)}, u32[]{:S(2)}) collective-permute-start(bf16[32,6144]{1,0:T(8,128)(2,1)S(1)} %pad_maximum_fusion.2), channel_id=1, source_target_pairs={{4,0},{8,4},{12,8},{14,12},{10,14},{6,10},{2,6},{0,2},{5,1},{9,5},... | collective-permute-start | bytes 1179656 | tf_op jit(solution)/shard_map/ppermute | solution.py:263
  77.6 10.7 %collective-permute-start.15 = (bf16[32,6144]{1,0:T(8,128)(2,1)S(1)}, bf16[32,6144]{1,0:T(8,128)(2,1)S(1)}, u32[]{:S(2)}, u32[]{:S(2)}) collective-permute-start(bf16[32,6144]{1,0:T(8,128)(2,1)S(1)} %get-tuple-element.33), channel_id=1, source_target_pairs={{4,0},{8,4},{12,8},{14,12},{10,14},{6,10},{2,6},{0,2},{5,1},{9,5},... | collective-permute-start | bytes 1179656 | tf_op jit(solution)/shard_map/ppermute | solution.py:263
  78.7 10.8 %collective-permute-start.11 = (bf16[32,6144]{1,0:T(8,128)(2,1)S(1)}, bf16[32,6144]{1,0:T(8,128)(2,1)S(1)}, u32[]{:S(2)}, u32[]{:S(2)}) collective-permute-start(bf16[32,6144]{1,0:T(8,128)(2,1)S(1)} %get-tuple-element.34), channel_id=1, source_target_pairs={{0,4},{4,8},{8,12},{12,14},{14,10},{10,6},{6,2},{2,0},{1,5},{5,9},... | collective-permute-start | bytes 1179656 | tf_op jit(solution)/shard_map/ppermute | solution.py:262
  89.6 7.8 %collective-permute-start.16 = (bf16[32,6144]{1,0:T(8,128)(2,1)S(1)}, bf16[32,6144]{1,0:T(8,128)(2,1)S(1)}, u32[]{:S(2)}, u32[]{:S(2)}) collective-permute-start(bf16[32,6144]{1,0:T(8,128)(2,1)S(1)} %get-tuple-element.31), channel_id=1, source_target_pairs={{4,0},{8,4},{12,8},{14,12},{10,14},{6,10},{2,6},{0,2},{5,1},{9,5},... | collective-permute-start | bytes 1179656 | tf_op jit(solution)/shard_map/ppermute | solution.py:263
  90.8 7.8 %collective-permute-start.12 = (bf16[32,6144]{1,0:T(8,128)(2,1)S(1)}, bf16[32,6144]{1,0:T(8,128)(2,1)S(1)}, u32[]{:S(2)}, u32[]{:S(2)}) collective-permute-start(bf16[32,6144]{1,0:T(8,128)(2,1)S(1)} %get-tuple-element.32), channel_id=1, source_target_pairs={{0,4},{4,8},{8,12},{12,14},{14,10},{10,6},{6,2},{2,0},{1,5},{5,9},... | collective-permute-start | bytes 1179656 | tf_op jit(solution)/shard_map/ppermute | solution.py:262
  98.6 1.5 %collective-permute-start.17 = (bf16[16,6144]{1,0:T(8,128)(2,1)S(1)}, bf16[16,6144]{1,0:T(8,128)(2,1)S(1)}, u32[]{:S(2)}, u32[]{:S(2)}) collective-permute-start(bf16[16,6144]{1,0:T(8,128)(2,1)S(1)} %add_convert_fusion), channel_id=1, source_target_pairs={{0,1},{1,0},{2,3},{3,2},{4,5},{5,4},{6,7},{7,6},{8,9},{9,8},{10,11... | collective-permute-start | bytes 589832 | tf_op jit(solution)/shard_map/ppermute | solution.py:25

commit v2 on v0

v2 whole, which is shorter than its diff:
```python
import jax
import jax.numpy as jnp
from jax import lax
from jax.experimental import pallas as pl
from jax.experimental.pallas import tpu as pltpu
from jax.sharding import PartitionSpec as P

CAP = 16
BLOCK = 2 * CAP
LANES = 128
ROWS = 256
VMEM_LIMIT = 8 * 1024 * 1024


def ring_hops(count, cores):
    cycle = [0, 2, 4, 6, 7, 5, 3, 1] if count == 8 else list(range(count))
    hops = []
    for here, there in zip(cycle, cycle[1:] + cycle[:1]):
        hops.append((here * cores, there * cores))
        hops.append((there * cores + 1, here * cores + 1))
    return hops


def swap(value):
    return lax.ppermute(value, "exp", [(0, 1), (1, 0)])


def tile_of(size, most):
    return max(t for t in range(LANES, most + 1, LANES) if size % t == 0)


def in_hbm(value):
    return pltpu.with_memory_space_constraint(value, pltpu.HBM)


def dispatch_kernel(me_ref, ids_ref, weights_ref, tokens_ref, rows_ref, turned_ref, mixer_ref, picker):
    @pl.when(pl.program_id(0) == 0)
    def _():
        token_count = ids_ref.shape[1]
        line = lax.broadcasted_iota(jnp.int32, (BLOCK, token_count), 0)
        expert = (line // CAP + me_ref[0]) % 2
        first = ids_ref[0:1, :] == expert
        second = ids_ref[1:2, :] == expert
        named = first.astype(jnp.float32) + second.astype(jnp.float32)
        row = lax.broadcasted_iota(jnp.int32, (token_count, token_count), 0)
        column = lax.broadcasted_iota(jnp.int32, (token_count, token_count), 1)
        earlier = (row < column).astype(jnp.bfloat16)
        before = jnp.dot(named.astype(jnp.bfloat16), earlier, preferred_element_type=jnp.float32)
        slot = (line % CAP).astype(jnp.float32)
        hit_first = jnp.where(first & (before == slot), 1.0, 0.0)
        after = before + first.astype(jnp.float32)
        hit_second = jnp.where(second & (after == slot), 1.0, 0.0)
        picker[...] = (hit_first + hit_second).astype(jnp.bfloat16)
        mixer = hit_first * weights_ref[0:1, :] + hit_second * weights_ref[1:2, :]
        high = mixer.astype(jnp.bfloat16).astype(jnp.float32)
        empty = jnp.zeros((LANES - 2 * BLOCK, token_count), jnp.float32)
        stacked = jnp.concatenate([high, mixer - high, empty], axis=0)
        mixer_ref[...] = stacked.T.astype(jnp.bfloat16)

    rows = jnp.dot(picker[...], tokens_ref[...], preferred_element_type=jnp.float32)
    rows_ref[...] = rows.astype(jnp.bfloat16)
    turned_ref[:CAP, :] = rows[CAP:].astype(jnp.bfloat16)
    turned_ref[CAP:, :] = rows[:CAP].astype(jnp.bfloat16)


def dispatch(me, expert_ids, route_weights, tokens):
    token_count, width = tokens.shape
    tile = tile_of(width, 1536)
    whole = lambda j, me: (0, 0)
    column = lambda j, me: (0, j)
    return pl.pallas_call(
        dispatch_kernel,
        grid_spec=pltpu.PrefetchScalarGridSpec(
            num_scalar_prefetch=1,
            grid=(width // tile,),
            in_specs=[
                pl.BlockSpec((2, token_count), whole),
                pl.BlockSpec((2, token_count), whole),
                pl.BlockSpec((token_count, tile), column),
            ],
            out_specs=[
                pl.BlockSpec((BLOCK, tile), column),
                pl.BlockSpec((BLOCK, tile), column),
                pl.BlockSpec((token_count, LANES), whole),
            ],
            scratch_shapes=[pltpu.VMEM((BLOCK, token_count), jnp.bfloat16)],
        ),
        out_shape=[
            jax.ShapeDtypeStruct((BLOCK, width), jnp.bfloat16),
            jax.ShapeDtypeStruct((BLOCK, width), jnp.bfloat16),
            jax.ShapeDtypeStruct((token_count, LANES), jnp.bfloat16),
        ],
        compiler_params=pltpu.CompilerParams(vmem_limit_bytes=VMEM_LIMIT),
        name="dispatch",
    )(me, in_hbm(expert_ids.T), in_hbm(route_weights.T), in_hbm(tokens))


def call(kernel, name, operands, outs, scratch=(), flops=0, bytes_accessed=0):
    return pl.pallas_call(
        kernel,
        in_specs=[pl.BlockSpec(memory_space=m) for _, m in operands],
        out_specs=[pl.BlockSpec(memory_space=pltpu.VMEM)] * len(outs),
        out_shape=outs,
        scratch_shapes=scratch,
        cost_estimate=pl.CostEstimate(
            flops=flops, bytes_accessed=bytes_accessed, transcendentals=0
        ),
        compiler_params=pltpu.CompilerParams(vmem_limit_bytes=VMEM_LIMIT),
        name=name,
    )(*[v for v, _ in operands])


def local(*values):
    return [(v, pltpu.VMEM) for v in values]


def held(*values):
    return [(pltpu.with_memory_space_constraint(v, pltpu.VMEM), pltpu.VMEM) for v in values]


def remote(*values):
    return [(in_hbm(v), pltpu.HBM) for v in values]


def array(*shape, dtype=jnp.bfloat16):
    return jax.ShapeDtypeStruct(shape, dtype)


def activate(gate, up):
    return (gate / (1.0 + jnp.exp(-gate)) * up).astype(jnp.bfloat16)


def hold_and_multiply(rows, weights, begin, depth, before, pieces=4):
    width = weights.shape[1]
    total = sum(c for _, _, c in rows)
    step = depth // pieces
    before = [] if before is None else [before]

    def kernel(*refs):
        row_refs, (source_ref, *refs) = refs[: len(rows)], refs[len(rows) :]
        held_ref, sum_ref, done = refs[len(before) :]
        copies = [
            pltpu.make_async_copy(
                source_ref.at[pl.ds(begin + i * step, step)],
                held_ref.at[pl.ds(i * step, step)],
                done.at[i],
            )
            for i in range(pieces)
        ]
        for copy in copies:
            copy.start()
        for i, copy in enumerate(copies):
            there = slice(begin + i * step, begin + (i + 1) * step)
            block = jnp.concatenate(
                [r[f : f + c, there] for r, (_, f, c) in zip(row_refs, rows)], axis=0
            )
            copy.wait()
            value = jnp.dot(
                block, held_ref[i * step : (i + 1) * step, :], preferred_element_type=jnp.float32
            )
            if i:
                value += sum_ref[...]
            elif before:
                value += refs[0][...]
            sum_ref[...] = value

    return call(
        kernel,
        "hold_and_multiply",
        local(*[r for r, _, _ in rows]) + remote(weights) + local(*before),
        [pltpu.VMEM((depth, width), weights.dtype), array(total, width, dtype=jnp.float32)],
        [pltpu.SemaphoreType.DMA((pieces,))],
        flops=2 * total * depth * width,
        bytes_accessed=2 * depth * width,
    )


def hidden_of(rows, gates, ups, gate_done=None, up_done=None):
    total = sum(c for _, _, c in rows)
    width = gates[0].shape[1]
    tile = tile_of(width, 256)
    before = [] if gate_done is None else [gate_done, up_done]

    def kernel(*refs):
        row_refs, refs = refs[: len(rows)], refs[len(rows) :]
        gate_refs, refs = refs[: len(gates)], refs[len(gates) :]
        up_refs, (*before_refs, out_ref) = refs[: len(ups)], refs[len(ups) :]
        block = jnp.concatenate([r[f : f + c, :] for r, (_, f, c) in zip(row_refs, rows)], axis=0)

        @pl.loop(0, width // tile)
        def _(j):
            here = pl.ds(pl.multiple_of(j * tile, tile), tile)
            values = []
            for i, pieces in enumerate((gate_refs, up_refs)):
                known = before_refs[i].shape[0] if before_refs else 0
                value, first = 0.0, 0
                for ref in pieces:
                    last = first + ref.shape[0]
                    value += jnp.dot(
                        block[known:, first:last], ref[:, here], preferred_element_type=jnp.float32
                    )
                    first = last
                if known:
                    value = jnp.concatenate([before_refs[i][:, here], value], axis=0)
                values.append(value)
            out_ref[:, here] = activate(*values)

    depth = sum(g.shape[0] for g in gates)
    return call(
        kernel,
        "hidden",
        local(*[r for r, _, _ in rows]) + held(*gates, *ups) + local(*before),
        [array(total, width)],
        flops=4 * total * depth * width,
        bytes_accessed=4 * depth * width,
    )[0]


def add(value, *others):
    total = value.astype(jnp.float32)
    for other in others:
        total += other.astype(jnp.float32)
    return total.astype(jnp.bfloat16)


def combine(arrived, handed, product, mixer):
    width = arrived.shape[1]
    token_count = mixer.shape[0]
    tile = tile_of(width, 1536)
    column = lambda j: (0, j)

    def kernel(arrived_ref, handed_ref, product_ref, mixer_ref, out_ref):
        rows = arrived_ref[...].astype(jnp.float32) + handed_ref[...].astype(jnp.float32)
        mine = (rows[:CAP] + product_ref[...].astype(jnp.float32)).astype(jnp.bfloat16)
        theirs = rows[CAP:].astype(jnp.bfloat16)
        rows = jnp.concatenate([mine, theirs, mine, theirs], axis=0)
        out_ref[...] = jnp.dot(
            mixer_ref[:, : 2 * BLOCK], rows, preferred_element_type=jnp.float32
        ).astype(jnp.bfloat16)

    return pl.pallas_call(
        kernel,
        grid=(width // tile,),
        in_specs=[
            pl.BlockSpec((BLOCK, tile), column),
            pl.BlockSpec((BLOCK, tile), column),
            pl.BlockSpec((CAP, tile), column),
            pl.BlockSpec(mixer.shape, lambda j: (0, 0)),
        ],
        out_specs=pl.BlockSpec((token_count, tile), column),
        out_shape=array(token_count, width),
        compiler_params=pltpu.CompilerParams(vmem_limit_bytes=VMEM_LIMIT),
        name="combine",
    )(arrived, handed, product, mixer)


def after(value, other):
    return lax.optimization_barrier((value, other))


def body(tokens, expert_ids, route_weights, w_gate, w_up, w_down):
    ept_count = lax.axis_size("ept")
    hops = ring_hops(ept_count, lax.axis_size("exp"))
    reach = ept_count // 2
    w_gate, w_up, w_down = w_gate[0], w_up[0], w_down[0]
    me = lax.axis_index("exp").astype(jnp.int32).reshape(1)

    def hop(value):
        return lax.ppermute(value, ("ept", "exp"), hops)

    own, turned, mixer = dispatch(me, expert_ids, route_weights, tokens)
    units = [own, swap(turned)]
    arriving = [hop(units[0]), hop(units[1])]
    plan = [(0, 0, 1, 3, 4, 5), (1, 0, 1, 5, 6, 8)] if ept_count == 8 else []
    weights, held_weights, sums, todo = [w_up, w_gate], [[], []], [None, None], []
    given = [None]
    while len(units) < 2 * reach + 1:
        unit = arriving[len(units) - 2]
        for i, before in list(todo):
            if before == len(units):
                unit, sums[i] = after(unit, sums[i])
                todo.remove((i, before))
        units.append(unit)
        if len(arriving) < 2 * reach - 1:
            arriving.append(hop(unit))
        for i, part, parts, newest, count, before in plan:
            if newest == len(units) - 1:
                units[-1], source = after(units[-1], weights[i])
                depth = source.shape[0] // parts
                rows = [(u, 0, CAP) for u in units[:count]]
                if given[-1] is not None and i == 1 and part == 0:
                    source, given[-1] = after(source, given[-1])
                piece, sums[i] = hold_and_multiply(rows, source, part * depth, depth, sums[i])
                held_weights[i].append(piece)
                todo.append((i, before))
        if len(units) == 2 * reach - 2:
            given = [swap(jnp.concatenate([u[CAP:] for u in units[2:]], axis=0))]
    far = swap(jnp.concatenate([u[CAP:] for u in units[-3:]], axis=0))
    ups, gates = (h if h else [w] for h, w in zip(held_weights, weights))
    up_done, gate_done = sums

    rows = [(u, 0, CAP) for u in units[:-1]]
    rows += [(given[0], BLOCK * k, BLOCK) for k in range(reach - 2)] + [(far, 0, BLOCK)]
    rows += [(units[-1], 0, CAP), (far, BLOCK, CAP)]
    groups = [[]]
    for row in rows:
        if sum(c for _, _, c in groups[-1]) + row[2] > ROWS:
            groups.append([])
        groups[-1].append(row)
    hidden = [hidden_of(groups[0], gates, ups, gate_done, up_done)]
    hidden += [hidden_of(group, gates, ups) for group in groups[1:]]
    hidden = jnp.concatenate(hidden, axis=0) if len(hidden) > 1 else hidden[0]
    mine = [hidden[BLOCK * k : BLOCK * (k + 1)] for k in range(reach)]
    others = [hidden[BLOCK * k : BLOCK * (k + 1)] for k in range(reach, 2 * reach)]

    def product_of(*parts):
        product = jnp.dot(
            jnp.concatenate(parts, axis=0), w_down, preferred_element_type=jnp.float32
        )
        return lax.optimization_barrier(product.astype(jnp.bfloat16))

    product = product_of(mine[reach - 1], *others[-2:])
    handed, kept = [swap(product[:BLOCK])], [product[BLOCK : 2 * BLOCK]]
    a = product[2 * BLOCK :]
    a = hop(jnp.concatenate([a[:CAP], swap(a[CAP:])], axis=0))
    product = product_of(*mine[:-1], *others[:-2])
    own = product[:BLOCK]
    if reach > 2:
        more = swap(product[BLOCK : BLOCK * (reach - 1)])
        handed += [more[BLOCK * k : BLOCK * (k + 1)] for k in reversed(range(reach - 2))]
        more = product[BLOCK * (reach - 1) :]
        kept += [more[BLOCK * k : BLOCK * (k + 1)] for k in reversed(range(reach - 2))]
    b = None
    for mine, theirs in zip(kept, handed):
        unit = jnp.concatenate([mine[:CAP], theirs[:CAP]], axis=0)
        b = hop(unit if b is None else add(unit, b))
        a = hop(add(jnp.concatenate([mine[CAP:], theirs[CAP:]], axis=0), a))
    handover = swap(jnp.concatenate([b[CAP:], add(b[:CAP], own[CAP:])], axis=0))
    return combine(a, handover, own[:CAP], mixer)


def solution(mesh):
    placed = (
        P(("groups", "ept", "exp"), None),
        P(("groups", "ept", "exp"), None),
        P(("groups", "ept", "exp"), None),
        P("exp", None, "ept"),
        P("exp", None, "ept"),
        P("exp", "ept", None),
    )
    return jax.shard_map(
        body,
        mesh=mesh,
        in_specs=placed,
        out_specs=P(("groups", "ept", "exp"), None),
        check_vma=False,
    )
```

time: 214 us -> 88.6 us (0.41)
  waiting for transfers between devices: 135 us -> 34.5 us
  starting transfers between devices: 0.04 us -> 26.7 us
  Pallas kernels: 0 us -> 21.5 us
  other arithmetic: 19.4 us -> 0.68 us
  matrix products: 21.1 us -> 4.32 us
  local copies, waits for them, and re-layouts: 14.2 us -> 0.44 us
  between operations: 13.5 us -> 0.31 us
  blocking collectives: 9.89 us -> 0 us
    reduce_scatter x1 -> x0, waiting for transfers between devices: 71.8 us -> none  [body(): lax.psum_scatter(jnp.stack(pieces, axis=1).reshape(row_count, local_count...]
    all_gather x1 -> x0, waiting for transfers between devices: 63.3 us -> none  [body(): gathered = lax.all_gather(incoming, 'ept', axis=0, tiled=True)]
    ppermute x0 -> x21, waiting for transfers between devices: none -> 34.5 us  [the longest x14 32.5 us: hop(): return lax.ppermute(value, ('ept', 'exp'), hops)]
    ppermute x0 -> x21, starting transfers between devices: none -> 26.7 us  [the longest x14 25.2 us: hop(): return lax.ppermute(value, ('ept', 'exp'), hops)]
    pallas_call x0 -> x5, Pallas kernels: none -> 21.5 us  [the longest x3 16.2 us: call(): pl.pallas_call(kernel, in_specs=[pl.BlockSpec(memory_space=m) for _, m in...]
    reduce_sum x3 -> x0, other arithmetic: 17.1 us -> none  [the longest x1 17 us: body(): jnp.sum((picked * scaled[:, None]).reshape(token_count, choices_per, mode...]
    dot_general x4 -> x2, matrix products: 21.1 us -> 4.32 us  [product_of(): jnp.dot(jnp.concatenate(parts, axis=0), w_down, preferred_element_type=jn...]
    gather x2 -> x0, local copies, waits for them, and re-layouts: 11.2 us -> none  [body(): picked = jnp.take(flat_rows, row_index, axis=0).astype(jnp.float32)]
  transfers between devices with their start and end apart: 2 -> 21, of which waited for: 2 -> 12; matrix products, arithmetic and copies ran while one was open for 0% -> 4% of each run, Pallas kernels for 0% -> 12%
where the time goes in v2:
time: 88.6 us; the launch traced here: 88.4 us
  waiting for transfers between devices  34.5 us (39%)
  starting transfers between devices  26.7 us (30%)
  Pallas kernels  21.5 us (24%)
  matrix products  4.32 us (5%)
    ppermute x14, waiting for transfers between devices, hop(): return lax.ppermute(value, ('ept', 'exp'), hops)  32.5 us
    ppermute x14, starting transfers between devices, hop(): return lax.ppermute(value, ('ept', 'exp'), hops)  25.2 us
    pallas_call x3, Pallas kernels, call(): pl.pallas_call(kernel, in_specs=[pl.BlockSpec(memory_space=m) for _, m in...  16.2 us
    dot_general x2, matrix products, product_of(): jnp.dot(jnp.concatenate(parts, axis=0), w_down, preferred_element_type=jn...  4.32 us
    pallas_call x1, Pallas kernels, dispatch(): pl.pallas_call(dispatch_kernel, grid_spec=pltpu.PrefetchScalarGridSpec(nu...  2.95 us
    pallas_call x1, Pallas kernels, combine(): pl.pallas_call(kernel, grid=(width // tile,), in_specs=[pl.BlockSpec((BLO...  2.35 us
    ppermute x7, waiting for transfers between devices, swap(): return lax.ppermute(value, 'exp', [(0, 1), (1, 0)])  2 us
  transfers between devices with their start and end apart: 21, of which 12 were waited for; matrix products, arithmetic and copies ran while one was open for 4% of the time, Pallas kernels for 12%

profile of v2, /device:TPU:0, one launch (start us, length us, event | category | flops | bytes accessed | tf_op | source)
XLA Modules:
  0.0 88.4 jit_solution(8534492082730069126)
XLA Ops:
  0.0 2.9 %dispatch.1 = (bf16[32,6144]{1,0:T(8,128)(2,1)S(1)}, bf16[32,6144]{1,0:T(8,128)(2,1)S(1)}, bf16[128,128]{1,0:T(8,128)(2,1)S(1)}) custom-call(s32[1]{0:T(128)} %bitcast.me_ref, s32[2,128]{1,0:T(2,128)} %bitcast.18, f32[2,128]{1,0:T(2,128)} %bitcast.19, bf16[128,6144]{1,0:T(8,128)(2,1)} %tokens_ref.1), custom_call_target="tpu_custom_call" | custom-call | tf_op jit(solution)/shard_map/dispatch/pallas_call | solution.py:71
  3.5 2.6 %collective-permute-start.1 = (bf16[32,6144]{1,0:T(8,128)(2,1)S(1)}, bf16[32,6144]{1,0:T(8,128)(2,1)S(1)}, u32[]{:S(2)}, u32[]{:S(2)}) collective-permute-start(bf16[32,6144]{1,0:T(8,128)(2,1)S(1)} %get-tuple-element.20.refs_0_), channel_id=1, source_target_pairs={{0,4},{5,1},{4,8},{9,5},{8,12},{13,9},{12,14},{15,13},{14,10},{11,... | collective-permute-start | bytes 1179656 | tf_op jit(solution)/shard_map/ppermute | solution.py:269
  6.1 1.7 %collective-permute-start.2 = (bf16[32,6144]{1,0:T(8,128)(2,1)S(1)}, bf16[32,6144]{1,0:T(8,128)(2,1)S(1)}, u32[]{:S(2)}, u32[]{:S(2)}) collective-permute-start(bf16[32,6144]{1,0:T(8,128)(2,1)S(1)} %collective-permute-done.refs_1_), channel_id=1, source_target_pairs={{0,4},{5,1},{4,8},{9,5},{8,12},{13,9},{12,14},{15,13},{14,10},{11,... | collective-permute-start | bytes 1179656 | tf_op jit(solution)/shard_map/ppermute | solution.py:269
  7.8 4.0 %collective-permute-done.1.refs_2_ = bf16[32,6144]{1,0:T(8,128)(2,1)S(1)} collective-permute-done((bf16[32,6144]{1,0:T(8,128)(2,1)S(1)}, bf16[32,6144]{1,0:T(8,128)(2,1)S(1)}, u32[]{:S(2)}, u32[]{:S(2)}) %collective-permute-start.1) | collective-permute-done | bytes 393248 | tf_op jit(solution)/shard_map/ppermute | solution.py:269
  11.8 2.1 %collective-permute-start.3 = (bf16[32,6144]{1,0:T(8,128)(2,1)S(1)}, bf16[32,6144]{1,0:T(8,128)(2,1)S(1)}, u32[]{:S(2)}, u32[]{:S(2)}) collective-permute-start(bf16[32,6144]{1,0:T(8,128)(2,1)S(1)} %collective-permute-done.1.refs_2_), channel_id=1, source_target_pairs={{0,4},{5,1},{4,8},{9,5},{8,12},{13,9},{12,14},{15,13},{14,10},{11,... | collective-permute-start | bytes 1179656 | tf_op jit(solution)/shard_map/ppermute | solution.py:269
  13.9 2.1 %collective-permute-done.2.refs_3_ = bf16[32,6144]{1,0:T(8,128)(2,1)S(1)} collective-permute-done((bf16[32,6144]{1,0:T(8,128)(2,1)S(1)}, bf16[32,6144]{1,0:T(8,128)(2,1)S(1)}, u32[]{:S(2)}, u32[]{:S(2)}) %collective-permute-start.2) | collective-permute-done | bytes 393248 | tf_op jit(solution)/shard_map/ppermute | solution.py:269
  16.0 2.1 %collective-permute-start.4 = (bf16[32,6144]{1,0:T(8,128)(2,1)S(1)}, bf16[32,6144]{1,0:T(8,128)(2,1)S(1)}, u32[]{:S(2)}, u32[]{:S(2)}) collective-permute-start(bf16[32,6144]{1,0:T(8,128)(2,1)S(1)} %collective-permute-done.2.refs_3_), channel_id=1, source_target_pairs={{0,4},{5,1},{4,8},{9,5},{8,12},{13,9},{12,14},{15,13},{14,10},{11,... | collective-permute-start | bytes 1179656 | tf_op jit(solution)/shard_map/ppermute | solution.py:269
  18.1 2.1 %collective-permute-done.3.refs_4_ = bf16[32,6144]{1,0:T(8,128)(2,1)S(1)} collective-permute-done((bf16[32,6144]{1,0:T(8,128)(2,1)S(1)}, bf16[32,6144]{1,0:T(8,128)(2,1)S(1)}, u32[]{:S(2)}, u32[]{:S(2)}) %collective-permute-start.3) | collective-permute-done | bytes 393248 | tf_op jit(solution)/shard_map/ppermute | solution.py:269
  20.2 2.1 %collective-permute-start.5 = (bf16[32,6144]{1,0:T(8,128)(2,1)S(1)}, bf16[32,6144]{1,0:T(8,128)(2,1)S(1)}, u32[]{:S(2)}, u32[]{:S(2)}) collective-permute-start(bf16[32,6144]{1,0:T(8,128)(2,1)S(1)} %collective-permute-done.3.refs_4_), channel_id=1, source_target_pairs={{0,4},{5,1},{4,8},{9,5},{8,12},{13,9},{12,14},{15,13},{14,10},{11,... | collective-permute-start | bytes 1179656 | tf_op jit(solution)/shard_map/ppermute | solution.py:269
  22.4 5.4 %hold_and_multiply.2 = (bf16[6144,1024]{1,0:T(8,128)(2,1)S(1)}, f32[64,1024]{1,0:T(8,128)S(1)}) custom-call(bf16[32,6144]{1,0:T(8,128)(2,1)S(1)} %get-tuple-element.20.refs_0_, bf16[32,6144]{1,0:T(8,128)(2,1)S(1)} %collective-permute-done.refs_1_, bf16[32,6144]{1,0:T(8,128)(2,1)S(1)} %collective-permute-done.1.refs_2_, ...), custom_call_target="tpu_custom_call" | custom-call | flops 805306368 | bytes 12582912 | tf_op jit(solution)/shard_map/hold_and_multiply/pallas_call | solution.py:99
  27.7 1.6 %collective-permute-start.6 = (bf16[32,6144]{1,0:T(8,128)(2,1)S(1)}, bf16[32,6144]{1,0:T(8,128)(2,1)S(1)}, u32[]{:S(2)}, u32[]{:S(2)}) collective-permute-start(bf16[32,6144]{1,0:T(8,128)(2,1)S(1)} %collective-permute-done.4.refs_5_), channel_id=1, source_target_pairs={{0,4},{5,1},{4,8},{9,5},{8,12},{13,9},{12,14},{15,13},{14,10},{11,... | collective-permute-start | bytes 1179656 | tf_op jit(solution)/shard_map/ppermute | solution.py:269
  29.4 1.6 %collective-permute-start.8 = (bf16[32,6144]{1,0:T(8,128)(2,1)S(1)}, bf16[32,6144]{1,0:T(8,128)(2,1)S(1)}, u32[]{:S(2)}, u32[]{:S(2)}) collective-permute-start(bf16[32,6144]{1,0:T(8,128)(2,1)S(1)} %collective-permute-done.5.refs_6_), channel_id=1, source_target_pairs={{0,4},{5,1},{4,8},{9,5},{8,12},{13,9},{12,14},{15,13},{14,10},{11,... | collective-permute-start | bytes 1179656 | tf_op jit(solution)/shard_map/ppermute | solution.py:269
  31.2 5.3 %hold_and_multiply.3 = (bf16[6144,1024]{1,0:T(8,128)(2,1)S(1)}, f32[96,1024]{1,0:T(8,128)S(1)}) custom-call(bf16[32,6144]{1,0:T(8,128)(2,1)S(1)} %get-tuple-element.20.refs_0_, bf16[32,6144]{1,0:T(8,128)(2,1)S(1)} %collective-permute-done.refs_1_, bf16[32,6144]{1,0:T(8,128)(2,1)S(1)} %collective-permute-done.1.refs_2_, ...), custom_call_target="tpu_custom_call" | custom-call | flops 1207959552 | bytes 12582912 | tf_op jit(solution)/shard_map/hold_and_multiply/pallas_call | solution.py:99
  36.5 3.3 %collective-permute-done.8.refs_11_ = bf16[32,6144]{1,0:T(8,128)(2,1)S(1)} collective-permute-done((bf16[32,6144]{1,0:T(8,128)(2,1)S(1)}, bf16[32,6144]{1,0:T(8,128)(2,1)S(1)}, u32[]{:S(2)}, u32[]{:S(2)}) %collective-permute-start.8) | collective-permute-done | bytes 393248 | tf_op jit(solution)/shard_map/ppermute | solution.py:269
  40.0 2.0 %collective-permute-done.9.refs_10_.refs_12_ = bf16[48,6144]{1,0:T(8,128)(2,1)S(1)} collective-permute-done((bf16[48,6144]{1,0:T(8,128)(2,1)S(1)}, bf16[48,6144]{1,0:T(8,128)(2,1)S(1)}, u32[]{:S(2)}, u32[]{:S(2)}) %collective-permute-start.9) | collective-permute-done | bytes 589856 | tf_op jit(solution)/shard_map/ppermute | solution.py:25
  42.0 5.5 %hidden.1 = bf16[256,1024]{1,0:T(8,128)(2,1)S(1)} custom-call(bf16[32,6144]{1,0:T(8,128)(2,1)S(1)} %get-tuple-element.20.refs_0_, bf16[32,6144]{1,0:T(8,128)(2,1)S(1)} %collective-permute-done.refs_1_, bf16[32,6144]{1,0:T(8,128)(2,1)S(1)} %collective-permute-done.1.refs_2_, bf16[32,6144]{1,0:T(8,128)(2,1)S(1)} %collective-permute-done.2.refs_3_, ...), custom_call_target="tpu_custom_call" | custom-call | flops 6442450944 | bytes 25165824 | tf_op jit(solution)/shard_map/hidden/pallas_call | solution.py:99
  47.6 2.1 %fusion.7 = bf16[96,6144]{1,0:T(8,128)(2,1)S(1)} fusion(bf16[1,1024,6144]{2,1,0:T(8,128)(2,1)S(1)} %bitcast.15, bf16[64,1024]{1,0:T(8,128)(2,1)S(1)} %get-tuple-element.49, bf16[32,1024]{1,0:T(8,128)(2,1)S(1)} %slice.166), kind=kOutput, calls=%fused_computation.5 | convolution fusion | flops 1208942592 | bytes 13959168 | tf_op jit(solution)/shard_map/dot_general | solution.py:317
  50.0 2.2 %fusion.4 = bf16[160,6144]{1,0:T(8,128)(2,1)S(1)} fusion(bf16[1,1024,6144]{2,1,0:T(8,128)(2,1)S(1)} %bitcast.15, bf16[64,1024]{1,0:T(8,128)(2,1)S(1)} %get-tuple-element.48, bf16[96,1024]{1,0:T(8,128)(2,1)S(1)} %slice.159), kind=kOutput, calls=%fused_computation.4 | convolution fusion | flops 2014904320 | bytes 14876672 | tf_op jit(solution)/shard_map/dot_general | solution.py:317
  53.0 1.6 %collective-permute-start.13 = (bf16[32,6144]{1,0:T(8,128)(2,1)S(1)}, bf16[32,6144]{1,0:T(8,128)(2,1)S(1)}, u32[]{:S(2)}, u32[]{:S(2)}) collective-permute-start(bf16[32,6144]{1,0:T(8,128)(2,1)S(1)} %pad_maximum_fusion.2), channel_id=1, source_target_pairs={{0,4},{5,1},{4,8},{9,5},{8,12},{13,9},{12,14},{15,13},{14,10},{11,... | collective-permute-start | bytes 1179656 | tf_op jit(solution)/shard_map/ppermute | solution.py:269
  56.3 4.5 %collective-permute-done.13 = bf16[32,6144]{1,0:T(8,128)(2,1)S(1)} collective-permute-done((bf16[32,6144]{1,0:T(8,128)(2,1)S(1)}, bf16[32,6144]{1,0:T(8,128)(2,1)S(1)}, u32[]{:S(2)}, u32[]{:S(2)}) %collective-permute-start.13) | collective-permute-done | bytes 393248 | tf_op jit(solution)/shard_map/ppermute | solution.py:269
  60.9 1.6 %collective-permute-start.14 = (bf16[32,6144]{1,0:T(8,128)(2,1)S(1)}, bf16[32,6144]{1,0:T(8,128)(2,1)S(1)}, u32[]{:S(2)}, u32[]{:S(2)}) collective-permute-start(bf16[32,6144]{1,0:T(8,128)(2,1)S(1)} %add_convert_fusion.4), channel_id=1, source_target_pairs={{0,4},{5,1},{4,8},{9,5},{8,12},{13,9},{12,14},{15,13},{14,10},{11,... | collective-permute-start | bytes 1179656 | tf_op jit(solution)/shard_map/ppermute | solution.py:269
  62.6 2.4 %collective-permute-done.17 = bf16[32,6144]{1,0:T(8,128)(2,1)S(1)} collective-permute-done((bf16[32,6144]{1,0:T(8,128)(2,1)S(1)}, bf16[32,6144]{1,0:T(8,128)(2,1)S(1)}, u32[]{:S(2)}, u32[]{:S(2)}) %collective-permute-start.17) | collective-permute-done | bytes 393248 | tf_op jit(solution)/shard_map/ppermute | solution.py:269
  65.1 1.6 %collective-permute-start.18 = (bf16[32,6144]{1,0:T(8,128)(2,1)S(1)}, bf16[32,6144]{1,0:T(8,128)(2,1)S(1)}, u32[]{:S(2)}, u32[]{:S(2)}) collective-permute-start(bf16[32,6144]{1,0:T(8,128)(2,1)S(1)} %add_convert_fusion.1), channel_id=1, source_target_pairs={{0,4},{5,1},{4,8},{9,5},{8,12},{13,9},{12,14},{15,13},{14,10},{11,... | collective-permute-start | bytes 1179656 | tf_op jit(solution)/shard_map/ppermute | solution.py:269
  66.7 2.5 %collective-permute-done.14 = bf16[32,6144]{1,0:T(8,128)(2,1)S(1)} collective-permute-done((bf16[32,6144]{1,0:T(8,128)(2,1)S(1)}, bf16[32,6144]{1,0:T(8,128)(2,1)S(1)}, u32[]{:S(2)}, u32[]{:S(2)}) %collective-permute-start.14) | collective-permute-done | bytes 393248 | tf_op jit(solution)/shard_map/ppermute | solution.py:269
  69.3 1.6 %collective-permute-start.15 = (bf16[32,6144]{1,0:T(8,128)(2,1)S(1)}, bf16[32,6144]{1,0:T(8,128)(2,1)S(1)}, u32[]{:S(2)}, u32[]{:S(2)}) collective-permute-start(bf16[32,6144]{1,0:T(8,128)(2,1)S(1)} %add_convert_fusion.3), channel_id=1, source_target_pairs={{0,4},{5,1},{4,8},{9,5},{8,12},{13,9},{12,14},{15,13},{14,10},{11,... | collective-permute-start | bytes 1179656 | tf_op jit(solution)/shard_map/ppermute | solution.py:269
  70.9 2.5 %collective-permute-done.18 = bf16[32,6144]{1,0:T(8,128)(2,1)S(1)} collective-permute-done((bf16[32,6144]{1,0:T(8,128)(2,1)S(1)}, bf16[32,6144]{1,0:T(8,128)(2,1)S(1)}, u32[]{:S(2)}, u32[]{:S(2)}) %collective-permute-start.18) | collective-permute-done | bytes 393248 | tf_op jit(solution)/shard_map/ppermute | solution.py:269
  73.5 1.6 %collective-permute-start.19 = (bf16[32,6144]{1,0:T(8,128)(2,1)S(1)}, bf16[32,6144]{1,0:T(8,128)(2,1)S(1)}, u32[]{:S(2)}, u32[]{:S(2)}) collective-permute-start(bf16[32,6144]{1,0:T(8,128)(2,1)S(1)} %add_convert_fusion), channel_id=1, source_target_pairs={{0,4},{5,1},{4,8},{9,5},{8,12},{13,9},{12,14},{15,13},{14,10},{11,... | collective-permute-start | bytes 1179656 | tf_op jit(solution)/shard_map/ppermute | solution.py:269
  75.2 2.5 %collective-permute-done.15 = bf16[32,6144]{1,0:T(8,128)(2,1)S(1)} collective-permute-done((bf16[32,6144]{1,0:T(8,128)(2,1)S(1)}, bf16[32,6144]{1,0:T(8,128)(2,1)S(1)}, u32[]{:S(2)}, u32[]{:S(2)}) %collective-permute-start.15) | collective-permute-done | bytes 393248 | tf_op jit(solution)/shard_map/ppermute | solution.py:269
  77.7 1.6 %collective-permute-start.16 = (bf16[32,6144]{1,0:T(8,128)(2,1)S(1)}, bf16[32,6144]{1,0:T(8,128)(2,1)S(1)}, u32[]{:S(2)}, u32[]{:S(2)}) collective-permute-start(bf16[32,6144]{1,0:T(8,128)(2,1)S(1)} %add_convert_fusion.2), channel_id=1, source_target_pairs={{0,4},{5,1},{4,8},{9,5},{8,12},{13,9},{12,14},{15,13},{14,10},{11,... | collective-permute-start | bytes 1179656 | tf_op jit(solution)/shard_map/ppermute | solution.py:269
  79.4 2.5 %collective-permute-done.19 = bf16[32,6144]{1,0:T(8,128)(2,1)S(1)} collective-permute-done((bf16[32,6144]{1,0:T(8,128)(2,1)S(1)}, bf16[32,6144]{1,0:T(8,128)(2,1)S(1)}, u32[]{:S(2)}, u32[]{:S(2)}) %collective-permute-start.19) | collective-permute-done | bytes 393248 | tf_op jit(solution)/shard_map/ppermute | solution.py:269
  82.0 4.0 %collective-permute-done.16.arrived_ref = bf16[32,6144]{1,0:T(8,128)(2,1)S(1)} collective-permute-done((bf16[32,6144]{1,0:T(8,128)(2,1)S(1)}, bf16[32,6144]{1,0:T(8,128)(2,1)S(1)}, u32[]{:S(2)}, u32[]{:S(2)}) %collective-permute-start.16) | collective-permute-done | bytes 393248 | tf_op jit(solution)/shard_map/ppermute | solution.py:269
  86.1 2.3 %combine.1 = bf16[128,6144]{1,0:T(8,128)(2,1)} custom-call(bf16[32,6144]{1,0:T(8,128)(2,1)S(1)} %collective-permute-done.16.arrived_ref, bf16[32,6144]{1,0:T(8,128)(2,1)S(1)} %collective-permute-done.20.handed_ref, bf16[16,6144]{1,0:T(8,128)(2,1)S(1)} %get-tuple-element.35.product_ref, bf16[128,128]{1,0:T(8,128)(2,1)S(1)} %get-tuple-element.34.mixer_ref), custom_call_target="tpu_custom_call" | custom-call | tf_op jit(solution)/shard_map/combine/pallas_call | solution.py:241
  (52 shorter events, 4.3 us)
Async XLA Ops:
  3.0 3.2 %collective-permute-start = (bf16[32,6144]{1,0:T(8,128)(2,1)S(1)}, bf16[32,6144]{1,0:T(8,128)(2,1)S(1)}, u32[]{:S(2)}, u32[]{:S(2)}) collective-permute-start(bf16[32,6144]{1,0:T(8,128)(2,1)S(1)} %get-tuple-element.21), channel_id=1, source_target_pairs={{0,1},{1,0},{2,3},{3,2},{4,5},{5,4},{6,7},{7,6},{8,9},{9,8},{10,11... | collective-permute-start | bytes 1179656 | tf_op jit(solution)/shard_map/ppermute | solution.py:25
  3.5 8.3 %collective-permute-start.1 = (bf16[32,6144]{1,0:T(8,128)(2,1)S(1)}, bf16[32,6144]{1,0:T(8,128)(2,1)S(1)}, u32[]{:S(2)}, u32[]{:S(2)}) collective-permute-start(bf16[32,6144]{1,0:T(8,128)(2,1)S(1)} %get-tuple-element.20.refs_0_), channel_id=1, source_target_pairs={{0,4},{5,1},{4,8},{9,5},{8,12},{13,9},{12,14},{15,13},{14,10},{11,... | collective-permute-start | bytes 1179656 | tf_op jit(solution)/shard_map/ppermute | solution.py:269
  6.1 9.9 %collective-permute-start.2 = (bf16[32,6144]{1,0:T(8,128)(2,1)S(1)}, bf16[32,6144]{1,0:T(8,128)(2,1)S(1)}, u32[]{:S(2)}, u32[]{:S(2)}) collective-permute-start(bf16[32,6144]{1,0:T(8,128)(2,1)S(1)} %collective-permute-done.refs_1_), channel_id=1, source_target_pairs={{0,4},{5,1},{4,8},{9,5},{8,12},{13,9},{12,14},{15,13},{14,10},{11,... | collective-permute-start | bytes 1179656 | tf_op jit(solution)/shard_map/ppermute | solution.py:269
  11.8 8.4 %collective-permute-start.3 = (bf16[32,6144]{1,0:T(8,128)(2,1)S(1)}, bf16[32,6144]{1,0:T(8,128)(2,1)S(1)}, u32[]{:S(2)}, u32[]{:S(2)}) collective-permute-start(bf16[32,6144]{1,0:T(8,128)(2,1)S(1)} %collective-permute-done.1.refs_2_), channel_id=1, source_target_pairs={{0,4},{5,1},{4,8},{9,5},{8,12},{13,9},{12,14},{15,13},{14,10},{11,... | collective-permute-start | bytes 1179656 | tf_op jit(solution)/shard_map/ppermute | solution.py:269
  16.0 11.7 %collective-permute-start.4 = (bf16[32,6144]{1,0:T(8,128)(2,1)S(1)}, bf16[32,6144]{1,0:T(8,128)(2,1)S(1)}, u32[]{:S(2)}, u32[]{:S(2)}) collective-permute-start(bf16[32,6144]{1,0:T(8,128)(2,1)S(1)} %collective-permute-done.2.refs_3_), channel_id=1, source_target_pairs={{0,4},{5,1},{4,8},{9,5},{8,12},{13,9},{12,14},{15,13},{14,10},{11,... | collective-permute-start | bytes 1179656 | tf_op jit(solution)/shard_map/ppermute | solution.py:269
  20.2 9.2 %collective-permute-start.5 = (bf16[32,6144]{1,0:T(8,128)(2,1)S(1)}, bf16[32,6144]{1,0:T(8,128)(2,1)S(1)}, u32[]{:S(2)}, u32[]{:S(2)}) collective-permute-start(bf16[32,6144]{1,0:T(8,128)(2,1)S(1)} %collective-permute-done.3.refs_4_), channel_id=1, source_target_pairs={{0,4},{5,1},{4,8},{9,5},{8,12},{13,9},{12,14},{15,13},{14,10},{11,... | collective-permute-start | bytes 1179656 | tf_op jit(solution)/shard_map/ppermute | solution.py:269
  27.7 12.1 %collective-permute-start.6 = (bf16[32,6144]{1,0:T(8,128)(2,1)S(1)}, bf16[32,6144]{1,0:T(8,128)(2,1)S(1)}, u32[]{:S(2)}, u32[]{:S(2)}) collective-permute-start(bf16[32,6144]{1,0:T(8,128)(2,1)S(1)} %collective-permute-done.4.refs_5_), channel_id=1, source_target_pairs={{0,4},{5,1},{4,8},{9,5},{8,12},{13,9},{12,14},{15,13},{14,10},{11,... | collective-permute-start | bytes 1179656 | tf_op jit(solution)/shard_map/ppermute | solution.py:269
  29.4 10.4 %collective-permute-start.8 = (bf16[32,6144]{1,0:T(8,128)(2,1)S(1)}, bf16[32,6144]{1,0:T(8,128)(2,1)S(1)}, u32[]{:S(2)}, u32[]{:S(2)}) collective-permute-start(bf16[32,6144]{1,0:T(8,128)(2,1)S(1)} %collective-permute-done.5.refs_6_), channel_id=1, source_target_pairs={{0,4},{5,1},{4,8},{9,5},{8,12},{13,9},{12,14},{15,13},{14,10},{11,... | collective-permute-start | bytes 1179656 | tf_op jit(solution)/shard_map/ppermute | solution.py:269
  31.1 8.9 %collective-permute-start.7 = (bf16[64,6144]{1,0:T(8,128)(2,1)S(1)}, bf16[64,6144]{1,0:T(8,128)(2,1)S(1)}, u32[]{:S(2)}, u32[]{:S(2)}) collective-permute-start(bf16[64,6144]{1,0:T(8,128)(2,1)S(1)} %pad_maximum_fusion), channel_id=1, source_target_pairs={{0,1},{1,0},{2,3},{3,2},{4,5},{5,4},{6,7},{7,6},{8,9},{9,8},{10,11... | collective-permute-start | bytes 2359304 | tf_op jit(solution)/shard_map/ppermute | solution.py:25
  39.9 2.1 %collective-permute-start.9 = (bf16[48,6144]{1,0:T(8,128)(2,1)S(1)}, bf16[48,6144]{1,0:T(8,128)(2,1)S(1)}, u32[]{:S(2)}, u32[]{:S(2)}) collective-permute-start(bf16[48,6144]{1,0:T(8,128)(2,1)S(1)} %pad_maximum_fusion.1), channel_id=1, source_target_pairs={{0,1},{1,0},{2,3},{3,2},{4,5},{5,4},{6,7},{7,6},{8,9},{9,8},{10,11... | collective-permute-start | bytes 1769480 | tf_op jit(solution)/shard_map/ppermute | solution.py:25
  42.0 5.6 %slice-start = ((s8[12582912]{0:T(1024)(128)(4,1)}), s8[4194304]{0:T(1024)(128)(4,1)S(1)}, s32[]{:S(2)}) async-start(s8[12582912]{0:T(1024)(128)(4,1)} %bitcast.14), calls=%async_computation | async-start | bytes 8388608
  42.0 5.6 %slice-start.1 = ((s8[12582912]{0:T(1024)(128)(4,1)}), s8[4194304]{0:T(1024)(128)(4,1)S(1)}, s32[]{:S(2)}) async-start(s8[12582912]{0:T(1024)(128)(4,1)} %bitcast.14), calls=%async_computation.1 | async-start | bytes 8388608
  42.0 5.6 %slice-start.2 = ((s8[12582912]{0:T(1024)(128)(4,1)}), s8[4194304]{0:T(1024)(128)(4,1)S(1)}, s32[]{:S(2)}) async-start(s8[12582912]{0:T(1024)(128)(4,1)} %bitcast.14), calls=%async_computation.2 | async-start | bytes 8388608
  49.8 3.2 %collective-permute-start.12 = (bf16[16,6144]{1,0:T(8,128)(2,1)S(1)}, bf16[16,6144]{1,0:T(8,128)(2,1)S(1)}, u32[]{:S(2)}, u32[]{:S(2)}) collective-permute-start(bf16[16,6144]{1,0:T(8,128)(2,1)S(1)} %get-tuple-element.41), channel_id=1, source_target_pairs={{0,1},{1,0},{2,3},{3,2},{4,5},{5,4},{6,7},{7,6},{8,9},{9,8},{10,11... | collective-permute-start | bytes 589832 | tf_op jit(solution)/shard_map/ppermute | solution.py:25
  52.3 2.2 %collective-permute-start.11 = (bf16[32,6144]{1,0:T(8,128)(2,1)S(1)}, bf16[32,6144]{1,0:T(8,128)(2,1)S(1)}, u32[]{:S(2)}, u32[]{:S(2)}) collective-permute-start(bf16[32,6144]{1,0:T(8,128)(2,1)S(1)} %slice.169), channel_id=1, source_target_pairs={{0,1},{1,0},{2,3},{3,2},{4,5},{5,4},{6,7},{7,6},{8,9},{9,8},{10,11... | collective-permute-start | bytes 1179656 | tf_op jit(solution)/shard_map/ppermute | solution.py:25
  52.8 9.7 %collective-permute-start.10 = (bf16[64,6144]{1,0:T(8,128)(2,1)S(1)}, bf16[64,6144]{1,0:T(8,128)(2,1)S(1)}, u32[]{:S(2)}, u32[]{:S(2)}) collective-permute-start(bf16[64,6144]{1,0:T(8,128)(2,1)S(1)} %slice.162), channel_id=1, source_target_pairs={{0,1},{1,0},{2,3},{3,2},{4,5},{5,4},{6,7},{7,6},{8,9},{9,8},{10,11... | collective-permute-start | bytes 2359304 | tf_op jit(solution)/shard_map/ppermute | solution.py:25
  53.0 7.8 %collective-permute-start.13 = (bf16[32,6144]{1,0:T(8,128)(2,1)S(1)}, bf16[32,6144]{1,0:T(8,128)(2,1)S(1)}, u32[]{:S(2)}, u32[]{:S(2)}) collective-permute-start(bf16[32,6144]{1,0:T(8,128)(2,1)S(1)} %pad_maximum_fusion.2), channel_id=1, source_target_pairs={{0,4},{5,1},{4,8},{9,5},{8,12},{13,9},{12,14},{15,13},{14,10},{11,... | collective-permute-start | bytes 1179656 | tf_op jit(solution)/shard_map/ppermute | solution.py:269
  54.7 10.3 %collective-permute-start.17 = (bf16[32,6144]{1,0:T(8,128)(2,1)S(1)}, bf16[32,6144]{1,0:T(8,128)(2,1)S(1)}, u32[]{:S(2)}, u32[]{:S(2)}) collective-permute-start(bf16[32,6144]{1,0:T(8,128)(2,1)S(1)} %pad_maximum_fusion.3), channel_id=1, source_target_pairs={{0,4},{5,1},{4,8},{9,5},{8,12},{13,9},{12,14},{15,13},{14,10},{11,... | collective-permute-start | bytes 1179656 | tf_op jit(solution)/shard_map/ppermute | solution.py:269
  60.9 8.3 %collective-permute-start.14 = (bf16[32,6144]{1,0:T(8,128)(2,1)S(1)}, bf16[32,6144]{1,0:T(8,128)(2,1)S(1)}, u32[]{:S(2)}, u32[]{:S(2)}) collective-permute-start(bf16[32,6144]{1,0:T(8,128)(2,1)S(1)} %add_convert_fusion.4), channel_id=1, source_target_pairs={{0,4},{5,1},{4,8},{9,5},{8,12},{13,9},{12,14},{15,13},{14,10},{11,... | collective-permute-start | bytes 1179656 | tf_op jit(solution)/shard_map/ppermute | solution.py:269
  65.1 8.3 %collective-permute-start.18 = (bf16[32,6144]{1,0:T(8,128)(2,1)S(1)}, bf16[32,6144]{1,0:T(8,128)(2,1)S(1)}, u32[]{:S(2)}, u32[]{:S(2)}) collective-permute-start(bf16[32,6144]{1,0:T(8,128)(2,1)S(1)} %add_convert_fusion.1), channel_id=1, source_target_pairs={{0,4},{5,1},{4,8},{9,5},{8,12},{13,9},{12,14},{15,13},{14,10},{11,... | collective-permute-start | bytes 1179656 | tf_op jit(solution)/shard_map/ppermute | solution.py:269
  69.3 8.3 %collective-permute-start.15 = (bf16[32,6144]{1,0:T(8,128)(2,1)S(1)}, bf16[32,6144]{1,0:T(8,128)(2,1)S(1)}, u32[]{:S(2)}, u32[]{:S(2)}) collective-permute-start(bf16[32,6144]{1,0:T(8,128)(2,1)S(1)} %add_convert_fusion.3), channel_id=1, source_target_pairs={{0,4},{5,1},{4,8},{9,5},{8,12},{13,9},{12,14},{15,13},{14,10},{11,... | collective-permute-start | bytes 1179656 | tf_op jit(solution)/shard_map/ppermute | solution.py:269
  73.5 8.3 %collective-permute-start.19 = (bf16[32,6144]{1,0:T(8,128)(2,1)S(1)}, bf16[32,6144]{1,0:T(8,128)(2,1)S(1)}, u32[]{:S(2)}, u32[]{:S(2)}) collective-permute-start(bf16[32,6144]{1,0:T(8,128)(2,1)S(1)} %add_convert_fusion), channel_id=1, source_target_pairs={{0,4},{5,1},{4,8},{9,5},{8,12},{13,9},{12,14},{15,13},{14,10},{11,... | collective-permute-start | bytes 1179656 | tf_op jit(solution)/shard_map/ppermute | solution.py:269
  77.7 8.3 %collective-permute-start.16 = (bf16[32,6144]{1,0:T(8,128)(2,1)S(1)}, bf16[32,6144]{1,0:T(8,128)(2,1)S(1)}, u32[]{:S(2)}, u32[]{:S(2)}) collective-permute-start(bf16[32,6144]{1,0:T(8,128)(2,1)S(1)} %add_convert_fusion.2), channel_id=1, source_target_pairs={{0,4},{5,1},{4,8},{9,5},{8,12},{13,9},{12,14},{15,13},{14,10},{11,... | collective-permute-start | bytes 1179656 | tf_op jit(solution)/shard_map/ppermute | solution.py:269
  82.0 4.1 %collective-permute-start.20 = (bf16[32,6144]{1,0:T(8,128)(2,1)S(1)}, bf16[32,6144]{1,0:T(8,128)(2,1)S(1)}, u32[]{:S(2)}, u32[]{:S(2)}) collective-permute-start(bf16[32,6144]{1,0:T(8,128)(2,1)S(1)} %pad_maximum_fusion.4), channel_id=1, source_target_pairs={{0,1},{1,0},{2,3},{3,2},{4,5},{5,4},{6,7},{7,6},{8,9},{9,8},{10,11... | collective-permute-start | bytes 1179656 | tf_op jit(solution)/shard_map/ppermute | solution.py:25

commit v3 on v2

--- a/solution.py
+++ b/solution.py
@@ -65,7 +65,7 @@
 
 def dispatch(me, expert_ids, route_weights, tokens):
     token_count, width = tokens.shape
-    tile = tile_of(width, 1536)
+    tile = tile_of(width, 3072)
     whole = lambda j, me: (0, 0)
     column = lambda j, me: (0, j)
     return pl.pallas_call(
@@ -130,10 +130,11 @@
     return (gate / (1.0 + jnp.exp(-gate)) * up).astype(jnp.bfloat16)
 
 
-def hold_and_multiply(rows, weights, begin, depth, before, pieces=4):
+def hold_and_multiply(rows, weights, begin, depth, before):
     width = weights.shape[1]
     total = sum(c for _, _, c in rows)
-    step = depth // pieces
+    step = tile_of(depth, 1536)
+    pieces = depth // step
     before = [] if before is None else [before]
 
     def kernel(*refs):
@@ -226,7 +227,7 @@
 def combine(arrived, handed, product, mixer):
     width = arrived.shape[1]
     token_count = mixer.shape[0]
-    tile = tile_of(width, 1536)
+    tile = tile_of(width, 3072)
     column = lambda j: (0, j)
 
     def kernel(arrived_ref, handed_ref, product_ref, mixer_ref, out_ref):
@@ -271,7 +272,7 @@
     own, turned, mixer = dispatch(me, expert_ids, route_weights, tokens)
     units = [own, swap(turned)]
     arriving = [hop(units[0]), hop(units[1])]
-    plan = [(0, 0, 1, 3, 4, 5), (1, 0, 1, 5, 6, 8)] if ept_count == 8 else []
+    plan = [(0, 0, 4, 2, 3, 3), (0, 4, 8, 3, 3, 5), (1, 0, 8, 5, 6, 8)] if ept_count == 8 else []
     weights, held_weights, sums, todo = [w_up, w_gate], [[], []], [None, None], []
     given = [None]
     while len(units) < 2 * reach + 1:
@@ -283,14 +284,16 @@
         units.append(unit)
         if len(arriving) < 2 * reach - 1:
             arriving.append(hop(unit))
-        for i, part, parts, newest, count, before in plan:
+        for i, first, last, newest, count, before in plan:
             if newest == len(units) - 1:
                 units[-1], source = after(units[-1], weights[i])
-                depth = source.shape[0] // parts
+                eighth = source.shape[0] // 8
                 rows = [(u, 0, CAP) for u in units[:count]]
-                if given[-1] is not None and i == 1 and part == 0:
+                if given[-1] is not None and i == 1:
                     source, given[-1] = after(source, given[-1])
-                piece, sums[i] = hold_and_multiply(rows, source, part * depth, depth, sums[i])
+                piece, sums[i] = hold_and_multiply(
+                    rows, source, first * eighth, (last - first) * eighth, sums[i]
+                )
                 held_weights[i].append(piece)
                 todo.append((i, before))
         if len(units) == 2 * reach - 2:
@@ -323,7 +326,9 @@
     handed, kept = [swap(product[:BLOCK])], [product[BLOCK : 2 * BLOCK]]
     a = product[2 * BLOCK :]
     a = hop(jnp.concatenate([a[:CAP], swap(a[CAP:])], axis=0))
-    product = product_of(*mine[:-1], *others[:-2])
+    first = jnp.concatenate([kept[0][:CAP], handed[0][:CAP]], axis=0)
+    first, parts = after(first, (*mine[:-1], *others[:-2]))
+    product = product_of(*parts)
     own = product[:BLOCK]
     if reach > 2:
         more = swap(product[BLOCK : BLOCK * (reach - 1)])
@@ -333,7 +338,7 @@
     b = None
     for mine, theirs in zip(kept, handed):
         unit = jnp.concatenate([mine[:CAP], theirs[:CAP]], axis=0)
-        b = hop(unit if b is None else add(unit, b))
+        b = hop(first if b is None else add(unit, b))
         a = hop(add(jnp.concatenate([mine[CAP:], theirs[CAP:]], axis=0), a))
     handover = swap(jnp.concatenate([b[CAP:], add(b[:CAP], own[CAP:])], axis=0))
     return combine(a, handover, own[:CAP], mixer)

time: 88.6 us -> 83.7 us (0.945)
  waiting for transfers between devices: 34.5 us -> 29.8 us
    ppermute x14, waiting for transfers between devices: 32.5 us -> 27 us  [hop(): return lax.ppermute(value, ('ept', 'exp'), hops)]
    pallas_call x3 -> x4, Pallas kernels: 16.2 us -> 18.2 us  [call(): pl.pallas_call(kernel, in_specs=[pl.BlockSpec(memory_space=m) for _, m in...]
    pallas_call x1, Pallas kernels: 2.95 us -> 1.96 us  [dispatch(): pl.pallas_call(dispatch_kernel, grid_spec=pltpu.PrefetchScalarGridSpec(nu...]
  transfers between devices with their start and end apart: 21 -> 21, of which waited for: 12 -> 13; matrix products, arithmetic and copies ran while one was open for 4% -> 4% of each run, Pallas kernels for 12% -> 15%
where the time goes in v3:
time: 83.7 us; the launch traced here: 83.6 us
  waiting for transfers between devices  29.8 us (36%)
  starting transfers between devices  26.1 us (31%)
  Pallas kernels  21.8 us (26%)
  matrix products  4.34 us (5%)
    ppermute x14, waiting for transfers between devices, hop(): return lax.ppermute(value, ('ept', 'exp'), hops)  27 us
    ppermute x14, starting transfers between devices, hop(): return lax.ppermute(value, ('ept', 'exp'), hops)  24.7 us
    pallas_call x4, Pallas kernels, call(): pl.pallas_call(kernel, in_specs=[pl.BlockSpec(memory_space=m) for _, m in...  18.2 us
    dot_general x2, matrix products, product_of(): jnp.dot(jnp.concatenate(parts, axis=0), w_down, preferred_element_type=jn...  4.34 us
    ppermute x7, waiting for transfers between devices, swap(): return lax.ppermute(value, 'exp', [(0, 1), (1, 0)])  2.83 us
    pallas_call x1, Pallas kernels, dispatch(): pl.pallas_call(dispatch_kernel, grid_spec=pltpu.PrefetchScalarGridSpec(nu...  1.96 us
    pallas_call x1, Pallas kernels, combine(): pl.pallas_call(kernel, grid=(width // tile,), in_specs=[pl.BlockSpec((BLO...  1.7 us
  transfers between devices with their start and end apart: 21, of which 13 were waited for; matrix products, arithmetic and copies ran while one was open for 4% of the time, Pallas kernels for 15%

profile of v3, /device:TPU:0, one launch (start us, length us, event | category | flops | bytes accessed | tf_op | source)
XLA Modules:
  0.0 83.6 jit_solution(4552323712646081696)
XLA Ops:
  0.0 2.0 %dispatch.1 = (bf16[32,6144]{1,0:T(8,128)(2,1)S(1)}, bf16[32,6144]{1,0:T(8,128)(2,1)S(1)}, bf16[128,128]{1,0:T(8,128)(2,1)S(1)}) custom-call(s32[1]{0:T(128)} %bitcast.me_ref, s32[2,128]{1,0:T(2,128)} %bitcast.20, f32[2,128]{1,0:T(2,128)} %bitcast.21, bf16[128,6144]{1,0:T(8,128)(2,1)} %tokens_ref.1), custom_call_target="tpu_custom_call" | custom-call | tf_op jit(solution)/shard_map/dispatch/pallas_call | solution.py:71
  2.5 2.6 %collective-permute-start.1 = (bf16[32,6144]{1,0:T(8,128)(2,1)S(1)}, bf16[32,6144]{1,0:T(8,128)(2,1)S(1)}, u32[]{:S(2)}, u32[]{:S(2)}) collective-permute-start(bf16[32,6144]{1,0:T(8,128)(2,1)S(1)} %get-tuple-element.32.refs_0_), channel_id=1, source_target_pairs={{0,4},{5,1},{4,8},{9,5},{8,12},{13,9},{12,14},{15,13},{14,10},{11,... | collective-permute-start | bytes 1179656 | tf_op jit(solution)/shard_map/ppermute | solution.py:270
  5.1 1.7 %collective-permute-start.2 = (bf16[32,6144]{1,0:T(8,128)(2,1)S(1)}, bf16[32,6144]{1,0:T(8,128)(2,1)S(1)}, u32[]{:S(2)}, u32[]{:S(2)}) collective-permute-start(bf16[32,6144]{1,0:T(8,128)(2,1)S(1)} %collective-permute-done.refs_1_), channel_id=1, source_target_pairs={{0,4},{5,1},{4,8},{9,5},{8,12},{13,9},{12,14},{15,13},{14,10},{11,... | collective-permute-start | bytes 1179656 | tf_op jit(solution)/shard_map/ppermute | solution.py:270
  6.8 4.0 %collective-permute-done.1.refs_2_ = bf16[32,6144]{1,0:T(8,128)(2,1)S(1)} collective-permute-done((bf16[32,6144]{1,0:T(8,128)(2,1)S(1)}, bf16[32,6144]{1,0:T(8,128)(2,1)S(1)}, u32[]{:S(2)}, u32[]{:S(2)}) %collective-permute-start.1) | collective-permute-done | bytes 393248 | tf_op jit(solution)/shard_map/ppermute | solution.py:270
  10.8 2.1 %collective-permute-start.3 = (bf16[32,6144]{1,0:T(8,128)(2,1)S(1)}, bf16[32,6144]{1,0:T(8,128)(2,1)S(1)}, u32[]{:S(2)}, u32[]{:S(2)}) collective-permute-start(bf16[32,6144]{1,0:T(8,128)(2,1)S(1)} %collective-permute-done.1.refs_2_), channel_id=1, source_target_pairs={{0,4},{5,1},{4,8},{9,5},{8,12},{13,9},{12,14},{15,13},{14,10},{11,... | collective-permute-start | bytes 1179656 | tf_op jit(solution)/shard_map/ppermute | solution.py:270
  12.9 3.5 %hold_and_multiply.3 = (bf16[3072,1024]{1,0:T(8,128)(2,1)S(1)}, f32[48,1024]{1,0:T(8,128)S(1)}) custom-call(bf16[32,6144]{1,0:T(8,128)(2,1)S(1)} %get-tuple-element.32.refs_0_, bf16[32,6144]{1,0:T(8,128)(2,1)S(1)} %collective-permute-done.refs_1_, bf16[32,6144]{1,0:T(8,128)(2,1)S(1)} %collective-permute-done.1.refs_2_, bf16[6144,1024]{1,0:T(8,128)(2,1)} %bitcast.17), custom_call_target="tpu_custom_call" | custom-call | flops 301989888 | bytes 6291456 | tf_op jit(solution)/shard_map/hold_and_multiply/pallas_call | solution.py:99
  16.4 1.6 %collective-permute-start.4 = (bf16[32,6144]{1,0:T(8,128)(2,1)S(1)}, bf16[32,6144]{1,0:T(8,128)(2,1)S(1)}, u32[]{:S(2)}, u32[]{:S(2)}) collective-permute-start(bf16[32,6144]{1,0:T(8,128)(2,1)S(1)} %collective-permute-done.2.refs_3_), channel_id=1, source_target_pairs={{0,4},{5,1},{4,8},{9,5},{8,12},{13,9},{12,14},{15,13},{14,10},{11,... | collective-permute-start | bytes 1179656 | tf_op jit(solution)/shard_map/ppermute | solution.py:270
  19.3 2.1 %collective-permute-start.5 = (bf16[32,6144]{1,0:T(8,128)(2,1)S(1)}, bf16[32,6144]{1,0:T(8,128)(2,1)S(1)}, u32[]{:S(2)}, u32[]{:S(2)}) collective-permute-start(bf16[32,6144]{1,0:T(8,128)(2,1)S(1)} %collective-permute-done.3.refs_4_), channel_id=1, source_target_pairs={{0,4},{5,1},{4,8},{9,5},{8,12},{13,9},{12,14},{15,13},{14,10},{11,... | collective-permute-start | bytes 1179656 | tf_op jit(solution)/shard_map/ppermute | solution.py:270
  21.4 3.5 %hold_and_multiply.4 = (bf16[3072,1024]{1,0:T(8,128)(2,1)S(1)}, f32[48,1024]{1,0:T(8,128)S(1)}) custom-call(bf16[32,6144]{1,0:T(8,128)(2,1)S(1)} %get-tuple-element.32.refs_0_, bf16[32,6144]{1,0:T(8,128)(2,1)S(1)} %collective-permute-done.refs_1_, bf16[32,6144]{1,0:T(8,128)(2,1)S(1)} %collective-permute-done.1.refs_2_, bf16[6144,1024]{1,0:T(8,128)(2,1)} %bitcast.18, ...), custom_call_target="tpu_custom_call" | custom-call | flops 301989888 | bytes 6291456 | tf_op jit(solution)/shard_map/hold_and_multiply/pallas_call | solution.py:99
  24.9 1.6 %collective-permute-start.6 = (bf16[32,6144]{1,0:T(8,128)(2,1)S(1)}, bf16[32,6144]{1,0:T(8,128)(2,1)S(1)}, u32[]{:S(2)}, u32[]{:S(2)}) collective-permute-start(bf16[32,6144]{1,0:T(8,128)(2,1)S(1)} %collective-permute-done.4.refs_5_), channel_id=1, source_target_pairs={{0,4},{5,1},{4,8},{9,5},{8,12},{13,9},{12,14},{15,13},{14,10},{11,... | collective-permute-start | bytes 1179656 | tf_op jit(solution)/shard_map/ppermute | solution.py:270
  26.6 1.9 %collective-permute-done.5.refs_6_ = bf16[32,6144]{1,0:T(8,128)(2,1)S(1)} collective-permute-done((bf16[32,6144]{1,0:T(8,128)(2,1)S(1)}, bf16[32,6144]{1,0:T(8,128)(2,1)S(1)}, u32[]{:S(2)}, u32[]{:S(2)}) %collective-permute-start.5) | collective-permute-done | bytes 393248 | tf_op jit(solution)/shard_map/ppermute | solution.py:270
  28.5 1.6 %collective-permute-start.8 = (bf16[32,6144]{1,0:T(8,128)(2,1)S(1)}, bf16[32,6144]{1,0:T(8,128)(2,1)S(1)}, u32[]{:S(2)}, u32[]{:S(2)}) collective-permute-start(bf16[32,6144]{1,0:T(8,128)(2,1)S(1)} %collective-permute-done.5.refs_6_), channel_id=1, source_target_pairs={{0,4},{5,1},{4,8},{9,5},{8,12},{13,9},{12,14},{15,13},{14,10},{11,... | collective-permute-start | bytes 1179656 | tf_op jit(solution)/shard_map/ppermute | solution.py:270
  30.2 5.3 %hold_and_multiply.5 = (bf16[6144,1024]{1,0:T(8,128)(2,1)S(1)}, f32[96,1024]{1,0:T(8,128)S(1)}) custom-call(bf16[32,6144]{1,0:T(8,128)(2,1)S(1)} %get-tuple-element.32.refs_0_, bf16[32,6144]{1,0:T(8,128)(2,1)S(1)} %collective-permute-done.refs_1_, bf16[32,6144]{1,0:T(8,128)(2,1)S(1)} %collective-permute-done.1.refs_2_, ...), custom_call_target="tpu_custom_call" | custom-call | flops 1207959552 | bytes 12582912 | tf_op jit(solution)/shard_map/hold_and_multiply/pallas_call | solution.py:99
  37.2 2.0 %collective-permute-done.9.refs_10_.refs_12_ = bf16[48,6144]{1,0:T(8,128)(2,1)S(1)} collective-permute-done((bf16[48,6144]{1,0:T(8,128)(2,1)S(1)}, bf16[48,6144]{1,0:T(8,128)(2,1)S(1)}, u32[]{:S(2)}, u32[]{:S(2)}) %collective-permute-start.9) | collective-permute-done | bytes 589856 | tf_op jit(solution)/shard_map/ppermute | solution.py:25
  39.2 5.8 %hidden.1 = bf16[256,1024]{1,0:T(8,128)(2,1)S(1)} custom-call(bf16[32,6144]{1,0:T(8,128)(2,1)S(1)} %get-tuple-element.32.refs_0_, bf16[32,6144]{1,0:T(8,128)(2,1)S(1)} %collective-permute-done.refs_1_, bf16[32,6144]{1,0:T(8,128)(2,1)S(1)} %collective-permute-done.1.refs_2_, bf16[32,6144]{1,0:T(8,128)(2,1)S(1)} %collective-permute-done.2.refs_3_, ...), custom_call_target="tpu_custom_call" | custom-call | flops 6442450944 | bytes 25165824 | tf_op jit(solution)/shard_map/hidden/pallas_call | solution.py:99
  45.1 2.1 %fusion.7 = bf16[96,6144]{1,0:T(8,128)(2,1)S(1)} fusion(bf16[1,1024,6144]{2,1,0:T(8,128)(2,1)S(1)} %bitcast.16, bf16[64,1024]{1,0:T(8,128)(2,1)S(1)} %slice.166, bf16[32,1024]{1,0:T(8,128)(2,1)S(1)} %get-tuple-element.77), kind=kOutput, calls=%fused_computation.5 | convolution fusion | flops 1208942592 | bytes 13959168 | tf_op jit(solution)/shard_map/dot_general | solution.py:320
  48.8 1.6 %collective-permute-start.13 = (bf16[32,6144]{1,0:T(8,128)(2,1)S(1)}, bf16[32,6144]{1,0:T(8,128)(2,1)S(1)}, u32[]{:S(2)}, u32[]{:S(2)}) collective-permute-start(bf16[32,6144]{1,0:T(8,128)(2,1)S(1)} %pad_maximum_fusion.3), channel_id=1, source_target_pairs={{0,4},{5,1},{4,8},{9,5},{8,12},{13,9},{12,14},{15,13},{14,10},{11,... | collective-permute-start | bytes 1179656 | tf_op jit(solution)/shard_map/ppermute | solution.py:270
  50.6 2.2 %fusion.4 = bf16[160,6144]{1,0:T(8,128)(2,1)S(1)} fusion(bf16[160,1024]{1,0:T(8,128)(2,1)S(1)} %constant_dynamic-update-slice_fusion, bf16[1,1024,6144]{2,1,0:T(8,128)(2,1)S(1)} %bitcast.16), kind=kOutput, calls=%fused_computation.4 | convolution fusion | flops 2014248960 | bytes 14876672 | tf_op jit(solution)/shard_map/dot_general | solution.py:320
  52.9 1.6 %collective-permute-start.17 = (bf16[32,6144]{1,0:T(8,128)(2,1)S(1)}, bf16[32,6144]{1,0:T(8,128)(2,1)S(1)}, u32[]{:S(2)}, u32[]{:S(2)}) collective-permute-start(bf16[32,6144]{1,0:T(8,128)(2,1)S(1)} %pad_maximum_fusion.2), channel_id=1, source_target_pairs={{0,4},{5,1},{4,8},{9,5},{8,12},{13,9},{12,14},{15,13},{14,10},{11,... | collective-permute-start | bytes 1179656 | tf_op jit(solution)/shard_map/ppermute | solution.py:270
  54.6 2.0 %collective-permute-done.13 = bf16[32,6144]{1,0:T(8,128)(2,1)S(1)} collective-permute-done((bf16[32,6144]{1,0:T(8,128)(2,1)S(1)}, bf16[32,6144]{1,0:T(8,128)(2,1)S(1)}, u32[]{:S(2)}, u32[]{:S(2)}) %collective-permute-start.13) | collective-permute-done | bytes 393248 | tf_op jit(solution)/shard_map/ppermute | solution.py:270
  56.7 1.6 %collective-permute-start.14 = (bf16[32,6144]{1,0:T(8,128)(2,1)S(1)}, bf16[32,6144]{1,0:T(8,128)(2,1)S(1)}, u32[]{:S(2)}, u32[]{:S(2)}) collective-permute-start(bf16[32,6144]{1,0:T(8,128)(2,1)S(1)} %add_convert_fusion.4), channel_id=1, source_target_pairs={{0,4},{5,1},{4,8},{9,5},{8,12},{13,9},{12,14},{15,13},{14,10},{11,... | collective-permute-start | bytes 1179656 | tf_op jit(solution)/shard_map/ppermute | solution.py:270
  58.4 2.4 %collective-permute-done.17 = bf16[32,6144]{1,0:T(8,128)(2,1)S(1)} collective-permute-done((bf16[32,6144]{1,0:T(8,128)(2,1)S(1)}, bf16[32,6144]{1,0:T(8,128)(2,1)S(1)}, u32[]{:S(2)}, u32[]{:S(2)}) %collective-permute-start.17) | collective-permute-done | bytes 393248 | tf_op jit(solution)/shard_map/ppermute | solution.py:270
  60.9 1.6 %collective-permute-start.18 = (bf16[32,6144]{1,0:T(8,128)(2,1)S(1)}, bf16[32,6144]{1,0:T(8,128)(2,1)S(1)}, u32[]{:S(2)}, u32[]{:S(2)}) collective-permute-start(bf16[32,6144]{1,0:T(8,128)(2,1)S(1)} %add_convert_fusion.1), channel_id=1, source_target_pairs={{0,4},{5,1},{4,8},{9,5},{8,12},{13,9},{12,14},{15,13},{14,10},{11,... | collective-permute-start | bytes 1179656 | tf_op jit(solution)/shard_map/ppermute | solution.py:270
  62.5 2.5 %collective-permute-done.14 = bf16[32,6144]{1,0:T(8,128)(2,1)S(1)} collective-permute-done((bf16[32,6144]{1,0:T(8,128)(2,1)S(1)}, bf16[32,6144]{1,0:T(8,128)(2,1)S(1)}, u32[]{:S(2)}, u32[]{:S(2)}) %collective-permute-start.14) | collective-permute-done | bytes 393248 | tf_op jit(solution)/shard_map/ppermute | solution.py:270
  65.1 1.6 %collective-permute-start.15 = (bf16[32,6144]{1,0:T(8,128)(2,1)S(1)}, bf16[32,6144]{1,0:T(8,128)(2,1)S(1)}, u32[]{:S(2)}, u32[]{:S(2)}) collective-permute-start(bf16[32,6144]{1,0:T(8,128)(2,1)S(1)} %add_convert_fusion.3), channel_id=1, source_target_pairs={{0,4},{5,1},{4,8},{9,5},{8,12},{13,9},{12,14},{15,13},{14,10},{11,... | collective-permute-start | bytes 1179656 | tf_op jit(solution)/shard_map/ppermute | solution.py:270
  66.8 2.5 %collective-permute-done.18 = bf16[32,6144]{1,0:T(8,128)(2,1)S(1)} collective-permute-done((bf16[32,6144]{1,0:T(8,128)(2,1)S(1)}, bf16[32,6144]{1,0:T(8,128)(2,1)S(1)}, u32[]{:S(2)}, u32[]{:S(2)}) %collective-permute-start.18) | collective-permute-done | bytes 393248 | tf_op jit(solution)/shard_map/ppermute | solution.py:270
  69.3 1.6 %collective-permute-start.19 = (bf16[32,6144]{1,0:T(8,128)(2,1)S(1)}, bf16[32,6144]{1,0:T(8,128)(2,1)S(1)}, u32[]{:S(2)}, u32[]{:S(2)}) collective-permute-start(bf16[32,6144]{1,0:T(8,128)(2,1)S(1)} %add_convert_fusion), channel_id=1, source_target_pairs={{0,4},{5,1},{4,8},{9,5},{8,12},{13,9},{12,14},{15,13},{14,10},{11,... | collective-permute-start | bytes 1179656 | tf_op jit(solution)/shard_map/ppermute | solution.py:270
  71.0 2.5 %collective-permute-done.15 = bf16[32,6144]{1,0:T(8,128)(2,1)S(1)} collective-permute-done((bf16[32,6144]{1,0:T(8,128)(2,1)S(1)}, bf16[32,6144]{1,0:T(8,128)(2,1)S(1)}, u32[]{:S(2)}, u32[]{:S(2)}) %collective-permute-start.15) | collective-permute-done | bytes 393248 | tf_op jit(solution)/shard_map/ppermute | solution.py:270
  73.6 1.6 %collective-permute-start.16 = (bf16[32,6144]{1,0:T(8,128)(2,1)S(1)}, bf16[32,6144]{1,0:T(8,128)(2,1)S(1)}, u32[]{:S(2)}, u32[]{:S(2)}) collective-permute-start(bf16[32,6144]{1,0:T(8,128)(2,1)S(1)} %add_convert_fusion.2), channel_id=1, source_target_pairs={{0,4},{5,1},{4,8},{9,5},{8,12},{13,9},{12,14},{15,13},{14,10},{11,... | collective-permute-start | bytes 1179656 | tf_op jit(solution)/shard_map/ppermute | solution.py:270
  75.2 2.5 %collective-permute-done.19 = bf16[32,6144]{1,0:T(8,128)(2,1)S(1)} collective-permute-done((bf16[32,6144]{1,0:T(8,128)(2,1)S(1)}, bf16[32,6144]{1,0:T(8,128)(2,1)S(1)}, u32[]{:S(2)}, u32[]{:S(2)}) %collective-permute-start.19) | collective-permute-done | bytes 393248 | tf_op jit(solution)/shard_map/ppermute | solution.py:270
  77.9 4.0 %collective-permute-done.16.arrived_ref = bf16[32,6144]{1,0:T(8,128)(2,1)S(1)} collective-permute-done((bf16[32,6144]{1,0:T(8,128)(2,1)S(1)}, bf16[32,6144]{1,0:T(8,128)(2,1)S(1)}, u32[]{:S(2)}, u32[]{:S(2)}) %collective-permute-start.16) | collective-permute-done | bytes 393248 | tf_op jit(solution)/shard_map/ppermute | solution.py:270
  81.9 1.7 %combine.1 = bf16[128,6144]{1,0:T(8,128)(2,1)} custom-call(bf16[32,6144]{1,0:T(8,128)(2,1)S(1)} %collective-permute-done.16.arrived_ref, bf16[32,6144]{1,0:T(8,128)(2,1)S(1)} %collective-permute-done.20.handed_ref, bf16[16,6144]{1,0:T(8,128)(2,1)S(1)} %get-tuple-element.59.product_ref, bf16[128,128]{1,0:T(8,128)(2,1)S(1)} %get-tuple-element.58.mixer_ref), custom_call_target="tpu_custom_call" | custom-call | tf_op jit(solution)/shard_map/combine/pallas_call | solution.py:242
  (57 shorter events, 6.0 us)
Async XLA Ops:
  2.0 3.2 %collective-permute-start = (bf16[32,6144]{1,0:T(8,128)(2,1)S(1)}, bf16[32,6144]{1,0:T(8,128)(2,1)S(1)}, u32[]{:S(2)}, u32[]{:S(2)}) collective-permute-start(bf16[32,6144]{1,0:T(8,128)(2,1)S(1)} %get-tuple-element.33), channel_id=1, source_target_pairs={{0,1},{1,0},{2,3},{3,2},{4,5},{5,4},{6,7},{7,6},{8,9},{9,8},{10,11... | collective-permute-start | bytes 1179656 | tf_op jit(solution)/shard_map/ppermute | solution.py:25
  2.5 8.3 %collective-permute-start.1 = (bf16[32,6144]{1,0:T(8,128)(2,1)S(1)}, bf16[32,6144]{1,0:T(8,128)(2,1)S(1)}, u32[]{:S(2)}, u32[]{:S(2)}) collective-permute-start(bf16[32,6144]{1,0:T(8,128)(2,1)S(1)} %get-tuple-element.32.refs_0_), channel_id=1, source_target_pairs={{0,4},{5,1},{4,8},{9,5},{8,12},{13,9},{12,14},{15,13},{14,10},{11,... | collective-permute-start | bytes 1179656 | tf_op jit(solution)/shard_map/ppermute | solution.py:270
  5.1 11.3 %collective-permute-start.2 = (bf16[32,6144]{1,0:T(8,128)(2,1)S(1)}, bf16[32,6144]{1,0:T(8,128)(2,1)S(1)}, u32[]{:S(2)}, u32[]{:S(2)}) collective-permute-start(bf16[32,6144]{1,0:T(8,128)(2,1)S(1)} %collective-permute-done.refs_1_), channel_id=1, source_target_pairs={{0,4},{5,1},{4,8},{9,5},{8,12},{13,9},{12,14},{15,13},{14,10},{11,... | collective-permute-start | bytes 1179656 | tf_op jit(solution)/shard_map/ppermute | solution.py:270
  10.8 8.4 %collective-permute-start.3 = (bf16[32,6144]{1,0:T(8,128)(2,1)S(1)}, bf16[32,6144]{1,0:T(8,128)(2,1)S(1)}, u32[]{:S(2)}, u32[]{:S(2)}) collective-permute-start(bf16[32,6144]{1,0:T(8,128)(2,1)S(1)} %collective-permute-done.1.refs_2_), channel_id=1, source_target_pairs={{0,4},{5,1},{4,8},{9,5},{8,12},{13,9},{12,14},{15,13},{14,10},{11,... | collective-permute-start | bytes 1179656 | tf_op jit(solution)/shard_map/ppermute | solution.py:270
  16.4 8.5 %collective-permute-start.4 = (bf16[32,6144]{1,0:T(8,128)(2,1)S(1)}, bf16[32,6144]{1,0:T(8,128)(2,1)S(1)}, u32[]{:S(2)}, u32[]{:S(2)}) collective-permute-start(bf16[32,6144]{1,0:T(8,128)(2,1)S(1)} %collective-permute-done.2.refs_3_), channel_id=1, source_target_pairs={{0,4},{5,1},{4,8},{9,5},{8,12},{13,9},{12,14},{15,13},{14,10},{11,... | collective-permute-start | bytes 1179656 | tf_op jit(solution)/shard_map/ppermute | solution.py:270
  19.3 9.2 %collective-permute-start.5 = (bf16[32,6144]{1,0:T(8,128)(2,1)S(1)}, bf16[32,6144]{1,0:T(8,128)(2,1)S(1)}, u32[]{:S(2)}, u32[]{:S(2)}) collective-permute-start(bf16[32,6144]{1,0:T(8,128)(2,1)S(1)} %collective-permute-done.3.refs_4_), channel_id=1, source_target_pairs={{0,4},{5,1},{4,8},{9,5},{8,12},{13,9},{12,14},{15,13},{14,10},{11,... | collective-permute-start | bytes 1179656 | tf_op jit(solution)/shard_map/ppermute | solution.py:270
  24.9 12.1 %collective-permute-start.6 = (bf16[32,6144]{1,0:T(8,128)(2,1)S(1)}, bf16[32,6144]{1,0:T(8,128)(2,1)S(1)}, u32[]{:S(2)}, u32[]{:S(2)}) collective-permute-start(bf16[32,6144]{1,0:T(8,128)(2,1)S(1)} %collective-permute-done.4.refs_5_), channel_id=1, source_target_pairs={{0,4},{5,1},{4,8},{9,5},{8,12},{13,9},{12,14},{15,13},{14,10},{11,... | collective-permute-start | bytes 1179656 | tf_op jit(solution)/shard_map/ppermute | solution.py:270
  28.5 8.5 %collective-permute-start.8 = (bf16[32,6144]{1,0:T(8,128)(2,1)S(1)}, bf16[32,6144]{1,0:T(8,128)(2,1)S(1)}, u32[]{:S(2)}, u32[]{:S(2)}) collective-permute-start(bf16[32,6144]{1,0:T(8,128)(2,1)S(1)} %collective-permute-done.5.refs_6_), channel_id=1, source_target_pairs={{0,4},{5,1},{4,8},{9,5},{8,12},{13,9},{12,14},{15,13},{14,10},{11,... | collective-permute-start | bytes 1179656 | tf_op jit(solution)/shard_map/ppermute | solution.py:270
  30.1 7.0 %collective-permute-start.7 = (bf16[64,6144]{1,0:T(8,128)(2,1)S(1)}, bf16[64,6144]{1,0:T(8,128)(2,1)S(1)}, u32[]{:S(2)}, u32[]{:S(2)}) collective-permute-start(bf16[64,6144]{1,0:T(8,128)(2,1)S(1)} %pad_maximum_fusion), channel_id=1, source_target_pairs={{0,1},{1,0},{2,3},{3,2},{4,5},{5,4},{6,7},{7,6},{8,9},{9,8},{10,11... | collective-permute-start | bytes 2359304 | tf_op jit(solution)/shard_map/ppermute | solution.py:25
  37.1 2.1 %collective-permute-start.9 = (bf16[48,6144]{1,0:T(8,128)(2,1)S(1)}, bf16[48,6144]{1,0:T(8,128)(2,1)S(1)}, u32[]{:S(2)}, u32[]{:S(2)}) collective-permute-start(bf16[48,6144]{1,0:T(8,128)(2,1)S(1)} %pad_maximum_fusion.1), channel_id=1, source_target_pairs={{0,1},{1,0},{2,3},{3,2},{4,5},{5,4},{6,7},{7,6},{8,9},{9,8},{10,11... | collective-permute-start | bytes 1769480 | tf_op jit(solution)/shard_map/ppermute | solution.py:25
  39.1 5.9 %slice-start = ((s8[12582912]{0:T(1024)(128)(4,1)}), s8[4194304]{0:T(1024)(128)(4,1)S(1)}, s32[]{:S(2)}) async-start(s8[12582912]{0:T(1024)(128)(4,1)} %bitcast.15), calls=%async_computation | async-start | bytes 8388608
  39.1 5.9 %slice-start.1 = ((s8[12582912]{0:T(1024)(128)(4,1)}), s8[4194304]{0:T(1024)(128)(4,1)S(1)}, s32[]{:S(2)}) async-start(s8[12582912]{0:T(1024)(128)(4,1)} %bitcast.15), calls=%async_computation.1 | async-start | bytes 8388608
  39.2 5.9 %slice-start.2 = ((s8[12582912]{0:T(1024)(128)(4,1)}), s8[4194304]{0:T(1024)(128)(4,1)S(1)}, s32[]{:S(2)}) async-start(s8[12582912]{0:T(1024)(128)(4,1)} %bitcast.15), calls=%async_computation.2 | async-start | bytes 8388608
  47.2 1.5 %collective-permute-start.12 = (bf16[16,6144]{1,0:T(8,128)(2,1)S(1)}, bf16[16,6144]{1,0:T(8,128)(2,1)S(1)}, u32[]{:S(2)}, u32[]{:S(2)}) collective-permute-start(bf16[16,6144]{1,0:T(8,128)(2,1)S(1)} %get-tuple-element.65), channel_id=1, source_target_pairs={{0,1},{1,0},{2,3},{3,2},{4,5},{5,4},{6,7},{7,6},{8,9},{9,8},{10,11... | collective-permute-start | bytes 589832 | tf_op jit(solution)/shard_map/ppermute | solution.py:25
  47.5 2.9 %collective-permute-start.10 = (bf16[32,6144]{1,0:T(8,128)(2,1)S(1)}, bf16[32,6144]{1,0:T(8,128)(2,1)S(1)}, u32[]{:S(2)}, u32[]{:S(2)}) collective-permute-start(bf16[32,6144]{1,0:T(8,128)(2,1)S(1)} %slice.168), channel_id=1, source_target_pairs={{0,1},{1,0},{2,3},{3,2},{4,5},{5,4},{6,7},{7,6},{8,9},{9,8},{10,11... | collective-permute-start | bytes 1179656 | tf_op jit(solution)/shard_map/ppermute | solution.py:25
  48.8 7.8 %collective-permute-start.13 = (bf16[32,6144]{1,0:T(8,128)(2,1)S(1)}, bf16[32,6144]{1,0:T(8,128)(2,1)S(1)}, u32[]{:S(2)}, u32[]{:S(2)}) collective-permute-start(bf16[32,6144]{1,0:T(8,128)(2,1)S(1)} %pad_maximum_fusion.3), channel_id=1, source_target_pairs={{0,4},{5,1},{4,8},{9,5},{8,12},{13,9},{12,14},{15,13},{14,10},{11,... | collective-permute-start | bytes 1179656 | tf_op jit(solution)/shard_map/ppermute | solution.py:270
  52.9 7.9 %collective-permute-start.17 = (bf16[32,6144]{1,0:T(8,128)(2,1)S(1)}, bf16[32,6144]{1,0:T(8,128)(2,1)S(1)}, u32[]{:S(2)}, u32[]{:S(2)}) collective-permute-start(bf16[32,6144]{1,0:T(8,128)(2,1)S(1)} %pad_maximum_fusion.2), channel_id=1, source_target_pairs={{0,4},{5,1},{4,8},{9,5},{8,12},{13,9},{12,14},{15,13},{14,10},{11,... | collective-permute-start | bytes 1179656 | tf_op jit(solution)/shard_map/ppermute | solution.py:270
  54.6 3.8 %collective-permute-start.11 = (bf16[64,6144]{1,0:T(8,128)(2,1)S(1)}, bf16[64,6144]{1,0:T(8,128)(2,1)S(1)}, u32[]{:S(2)}, u32[]{:S(2)}) collective-permute-start(bf16[64,6144]{1,0:T(8,128)(2,1)S(1)} %slice.176), channel_id=1, source_target_pairs={{0,1},{1,0},{2,3},{3,2},{4,5},{5,4},{6,7},{7,6},{8,9},{9,8},{10,11... | collective-permute-start | bytes 2359304 | tf_op jit(solution)/shard_map/ppermute | solution.py:25
  56.7 8.3 %collective-permute-start.14 = (bf16[32,6144]{1,0:T(8,128)(2,1)S(1)}, bf16[32,6144]{1,0:T(8,128)(2,1)S(1)}, u32[]{:S(2)}, u32[]{:S(2)}) collective-permute-start(bf16[32,6144]{1,0:T(8,128)(2,1)S(1)} %add_convert_fusion.4), channel_id=1, source_target_pairs={{0,4},{5,1},{4,8},{9,5},{8,12},{13,9},{12,14},{15,13},{14,10},{11,... | collective-permute-start | bytes 1179656 | tf_op jit(solution)/shard_map/ppermute | solution.py:270
  60.9 8.3 %collective-permute-start.18 = (bf16[32,6144]{1,0:T(8,128)(2,1)S(1)}, bf16[32,6144]{1,0:T(8,128)(2,1)S(1)}, u32[]{:S(2)}, u32[]{:S(2)}) collective-permute-start(bf16[32,6144]{1,0:T(8,128)(2,1)S(1)} %add_convert_fusion.1), channel_id=1, source_target_pairs={{0,4},{5,1},{4,8},{9,5},{8,12},{13,9},{12,14},{15,13},{14,10},{11,... | collective-permute-start | bytes 1179656 | tf_op jit(solution)/shard_map/ppermute | solution.py:270
  65.1 8.3 %collective-permute-start.15 = (bf16[32,6144]{1,0:T(8,128)(2,1)S(1)}, bf16[32,6144]{1,0:T(8,128)(2,1)S(1)}, u32[]{:S(2)}, u32[]{:S(2)}) collective-permute-start(bf16[32,6144]{1,0:T(8,128)(2,1)S(1)} %add_convert_fusion.3), channel_id=1, source_target_pairs={{0,4},{5,1},{4,8},{9,5},{8,12},{13,9},{12,14},{15,13},{14,10},{11,... | collective-permute-start | bytes 1179656 | tf_op jit(solution)/shard_map/ppermute | solution.py:270
  69.3 8.3 %collective-permute-start.19 = (bf16[32,6144]{1,0:T(8,128)(2,1)S(1)}, bf16[32,6144]{1,0:T(8,128)(2,1)S(1)}, u32[]{:S(2)}, u32[]{:S(2)}) collective-permute-start(bf16[32,6144]{1,0:T(8,128)(2,1)S(1)} %add_convert_fusion), channel_id=1, source_target_pairs={{0,4},{5,1},{4,8},{9,5},{8,12},{13,9},{12,14},{15,13},{14,10},{11,... | collective-permute-start | bytes 1179656 | tf_op jit(solution)/shard_map/ppermute | solution.py:270
  73.6 8.3 %collective-permute-start.16 = (bf16[32,6144]{1,0:T(8,128)(2,1)S(1)}, bf16[32,6144]{1,0:T(8,128)(2,1)S(1)}, u32[]{:S(2)}, u32[]{:S(2)}) collective-permute-start(bf16[32,6144]{1,0:T(8,128)(2,1)S(1)} %add_convert_fusion.2), channel_id=1, source_target_pairs={{0,4},{5,1},{4,8},{9,5},{8,12},{13,9},{12,14},{15,13},{14,10},{11,... | collective-permute-start | bytes 1179656 | tf_op jit(solution)/shard_map/ppermute | solution.py:270
  77.8 4.1 %collective-permute-start.20 = (bf16[32,6144]{1,0:T(8,128)(2,1)S(1)}, bf16[32,6144]{1,0:T(8,128)(2,1)S(1)}, u32[]{:S(2)}, u32[]{:S(2)}) collective-permute-start(bf16[32,6144]{1,0:T(8,128)(2,1)S(1)} %pad_maximum_fusion.4), channel_id=1, source_target_pairs={{0,1},{1,0},{2,3},{3,2},{4,5},{5,4},{6,7},{7,6},{8,9},{9,8},{10,11... | collective-permute-start | bytes 1179656 | tf_op jit(solution)/shard_map/ppermute | solution.py:25

commit v4 on v3

--- a/solution.py
+++ b/solution.py
@@ -14,11 +14,13 @@
 
 def ring_hops(count, cores):
     cycle = [0, 2, 4, 6, 7, 5, 3, 1] if count == 8 else list(range(count))
-    hops = []
+    hops, across, aside = [], [], []
     for here, there in zip(cycle, cycle[1:] + cycle[:1]):
-        hops.append((here * cores, there * cores))
-        hops.append((there * cores + 1, here * cores + 1))
-    return hops
+        for core, (begin, end) in enumerate(((here, there), (there, here))):
+            hops.append((begin * cores + core, end * cores + core))
+            across.append((begin * cores + core, end * cores + 1 - core))
+            aside.append((begin * cores + 1 - core, end * cores + core))
+    return hops, across, aside
 
 
 def swap(value):
@@ -261,13 +263,13 @@
 
 def body(tokens, expert_ids, route_weights, w_gate, w_up, w_down):
     ept_count = lax.axis_size("ept")
-    hops = ring_hops(ept_count, lax.axis_size("exp"))
+    hops, across, aside = ring_hops(ept_count, lax.axis_size("exp"))
     reach = ept_count // 2
     w_gate, w_up, w_down = w_gate[0], w_up[0], w_down[0]
     me = lax.axis_index("exp").astype(jnp.int32).reshape(1)
 
-    def hop(value):
-        return lax.ppermute(value, ("ept", "exp"), hops)
+    def hop(value, pairs=hops):
+        return lax.ppermute(value, ("ept", "exp"), pairs)
 
     own, turned, mixer = dispatch(me, expert_ids, route_weights, tokens)
     units = [own, swap(turned)]
@@ -324,11 +326,11 @@
 
     product = product_of(mine[reach - 1], *others[-2:])
     handed, kept = [swap(product[:BLOCK])], [product[BLOCK : 2 * BLOCK]]
-    a = product[2 * BLOCK :]
-    a = hop(jnp.concatenate([a[:CAP], swap(a[CAP:])], axis=0))
+    a = [hop(product[2 * BLOCK : 2 * BLOCK + CAP]), hop(product[2 * BLOCK + CAP :], aside)]
     first = jnp.concatenate([kept[0][:CAP], handed[0][:CAP]], axis=0)
     first, parts = after(first, (*mine[:-1], *others[:-2]))
     product = product_of(*parts)
+    a, product = after(a, product)
     own = product[:BLOCK]
     if reach > 2:
         more = swap(product[BLOCK : BLOCK * (reach - 1)])
@@ -339,6 +341,8 @@
     for mine, theirs in zip(kept, handed):
         unit = jnp.concatenate([mine[:CAP], theirs[:CAP]], axis=0)
         b = hop(first if b is None else add(unit, b))
+        if isinstance(a, list):
+            a = jnp.concatenate(a, axis=0)
         a = hop(add(jnp.concatenate([mine[CAP:], theirs[CAP:]], axis=0), a))
     handover = swap(jnp.concatenate([b[CAP:], add(b[:CAP], own[CAP:])], axis=0))
     return combine(a, handover, own[:CAP], mixer)

time: 83.7 us -> 81.9 us (0.978)
  waiting for transfers between devices: 29.8 us -> 27.4 us
    ppermute x14 -> x15, waiting for transfers between devices: 27 us -> 23.2 us  [hop(): return lax.ppermute(value, ('ept', 'exp'), pairs)]
    ppermute x7 -> x6, waiting for transfers between devices: 2.83 us -> 4.19 us  [swap(): return lax.ppermute(value, 'exp', [(0, 1), (1, 0)])]
    ppermute x14 -> x15, starting transfers between devices: 24.7 us -> 25.1 us  [hop(): return lax.ppermute(value, ('ept', 'exp'), pairs)]
where the time goes in v4:
time: 81.9 us; the launch traced here: 81.7 us
  waiting for transfers between devices  27.4 us (33%)
  starting transfers between devices  26.7 us (33%)
  Pallas kernels  21.8 us (27%)
  matrix products  4.34 us (5%)
    ppermute x15, starting transfers between devices, hop(): return lax.ppermute(value, ('ept', 'exp'), pairs)  25.1 us
    ppermute x15, waiting for transfers between devices, hop(): return lax.ppermute(value, ('ept', 'exp'), pairs)  23.2 us
    pallas_call x4, Pallas kernels, call(): pl.pallas_call(kernel, in_specs=[pl.BlockSpec(memory_space=m) for _, m in...  18.2 us
    dot_general x2, matrix products, product_of(): jnp.dot(jnp.concatenate(parts, axis=0), w_down, preferred_element_type=jn...  4.34 us
    ppermute x6, waiting for transfers between devices, swap(): return lax.ppermute(value, 'exp', [(0, 1), (1, 0)])  4.19 us
    pallas_call x1, Pallas kernels, dispatch(): pl.pallas_call(dispatch_kernel, grid_spec=pltpu.PrefetchScalarGridSpec(nu...  1.96 us
    pallas_call x1, Pallas kernels, combine(): pl.pallas_call(kernel, grid=(width // tile,), in_specs=[pl.BlockSpec((BLO...  1.7 us
    ppermute x6, starting transfers between devices, swap(): return lax.ppermute(value, 'exp', [(0, 1), (1, 0)])  1.67 us
  transfers between devices with their start and end apart: 21, of which 13 were waited for; matrix products, arithmetic and copies ran while one was open for 4% of the time, Pallas kernels for 15%

profile of v4, /device:TPU:0, one launch (start us, length us, event | category | flops | bytes accessed | tf_op | source)
XLA Modules:
  0.0 81.7 jit_solution(1143120827244615689)
XLA Ops:
  0.0 2.0 %dispatch.1 = (bf16[32,6144]{1,0:T(8,128)(2,1)S(1)}, bf16[32,6144]{1,0:T(8,128)(2,1)S(1)}, bf16[128,128]{1,0:T(8,128)(2,1)S(1)}) custom-call(s32[1]{0:T(128)} %bitcast.me_ref, s32[2,128]{1,0:T(2,128)} %bitcast.20, f32[2,128]{1,0:T(2,128)} %bitcast.21, bf16[128,6144]{1,0:T(8,128)(2,1)} %tokens_ref.1), custom_call_target="tpu_custom_call" | custom-call | tf_op jit(solution)/shard_map/dispatch/pallas_call | solution.py:73
  2.5 2.6 %collective-permute-start.1 = (bf16[32,6144]{1,0:T(8,128)(2,1)S(1)}, bf16[32,6144]{1,0:T(8,128)(2,1)S(1)}, u32[]{:S(2)}, u32[]{:S(2)}) collective-permute-start(bf16[32,6144]{1,0:T(8,128)(2,1)S(1)} %get-tuple-element.35.refs_0_), channel_id=1, source_target_pairs={{0,4},{5,1},{4,8},{9,5},{8,12},{13,9},{12,14},{15,13},{14,10},{11,... | collective-permute-start | bytes 1179656 | tf_op jit(solution)/shard_map/ppermute | solution.py:272
  5.1 1.7 %collective-permute-start.2 = (bf16[32,6144]{1,0:T(8,128)(2,1)S(1)}, bf16[32,6144]{1,0:T(8,128)(2,1)S(1)}, u32[]{:S(2)}, u32[]{:S(2)}) collective-permute-start(bf16[32,6144]{1,0:T(8,128)(2,1)S(1)} %collective-permute-done.refs_1_), channel_id=1, source_target_pairs={{0,4},{5,1},{4,8},{9,5},{8,12},{13,9},{12,14},{15,13},{14,10},{11,... | collective-permute-start | bytes 1179656 | tf_op jit(solution)/shard_map/ppermute | solution.py:272
  6.8 4.0 %collective-permute-done.1.refs_2_ = bf16[32,6144]{1,0:T(8,128)(2,1)S(1)} collective-permute-done((bf16[32,6144]{1,0:T(8,128)(2,1)S(1)}, bf16[32,6144]{1,0:T(8,128)(2,1)S(1)}, u32[]{:S(2)}, u32[]{:S(2)}) %collective-permute-start.1) | collective-permute-done | bytes 393248 | tf_op jit(solution)/shard_map/ppermute | solution.py:272
  10.8 2.1 %collective-permute-start.3 = (bf16[32,6144]{1,0:T(8,128)(2,1)S(1)}, bf16[32,6144]{1,0:T(8,128)(2,1)S(1)}, u32[]{:S(2)}, u32[]{:S(2)}) collective-permute-start(bf16[32,6144]{1,0:T(8,128)(2,1)S(1)} %collective-permute-done.1.refs_2_), channel_id=1, source_target_pairs={{0,4},{5,1},{4,8},{9,5},{8,12},{13,9},{12,14},{15,13},{14,10},{11,... | collective-permute-start | bytes 1179656 | tf_op jit(solution)/shard_map/ppermute | solution.py:272
  12.9 3.5 %hold_and_multiply.3 = (bf16[3072,1024]{1,0:T(8,128)(2,1)S(1)}, f32[48,1024]{1,0:T(8,128)S(1)}) custom-call(bf16[32,6144]{1,0:T(8,128)(2,1)S(1)} %get-tuple-element.35.refs_0_, bf16[32,6144]{1,0:T(8,128)(2,1)S(1)} %collective-permute-done.refs_1_, bf16[32,6144]{1,0:T(8,128)(2,1)S(1)} %collective-permute-done.1.refs_2_, bf16[6144,1024]{1,0:T(8,128)(2,1)} %bitcast.17), custom_call_target="tpu_custom_call" | custom-call | flops 301989888 | bytes 6291456 | tf_op jit(solution)/shard_map/hold_and_multiply/pallas_call | solution.py:101
  16.4 1.6 %collective-permute-start.4 = (bf16[32,6144]{1,0:T(8,128)(2,1)S(1)}, bf16[32,6144]{1,0:T(8,128)(2,1)S(1)}, u32[]{:S(2)}, u32[]{:S(2)}) collective-permute-start(bf16[32,6144]{1,0:T(8,128)(2,1)S(1)} %collective-permute-done.2.refs_3_), channel_id=1, source_target_pairs={{0,4},{5,1},{4,8},{9,5},{8,12},{13,9},{12,14},{15,13},{14,10},{11,... | collective-permute-start | bytes 1179656 | tf_op jit(solution)/shard_map/ppermute | solution.py:272
  19.3 2.1 %collective-permute-start.5 = (bf16[32,6144]{1,0:T(8,128)(2,1)S(1)}, bf16[32,6144]{1,0:T(8,128)(2,1)S(1)}, u32[]{:S(2)}, u32[]{:S(2)}) collective-permute-start(bf16[32,6144]{1,0:T(8,128)(2,1)S(1)} %collective-permute-done.3.refs_4_), channel_id=1, source_target_pairs={{0,4},{5,1},{4,8},{9,5},{8,12},{13,9},{12,14},{15,13},{14,10},{11,... | collective-permute-start | bytes 1179656 | tf_op jit(solution)/shard_map/ppermute | solution.py:272
  21.4 3.5 %hold_and_multiply.4 = (bf16[3072,1024]{1,0:T(8,128)(2,1)S(1)}, f32[48,1024]{1,0:T(8,128)S(1)}) custom-call(bf16[32,6144]{1,0:T(8,128)(2,1)S(1)} %get-tuple-element.35.refs_0_, bf16[32,6144]{1,0:T(8,128)(2,1)S(1)} %collective-permute-done.refs_1_, bf16[32,6144]{1,0:T(8,128)(2,1)S(1)} %collective-permute-done.1.refs_2_, bf16[6144,1024]{1,0:T(8,128)(2,1)} %bitcast.18, ...), custom_call_target="tpu_custom_call" | custom-call | flops 301989888 | bytes 6291456 | tf_op jit(solution)/shard_map/hold_and_multiply/pallas_call | solution.py:101
  24.9 1.6 %collective-permute-start.6 = (bf16[32,6144]{1,0:T(8,128)(2,1)S(1)}, bf16[32,6144]{1,0:T(8,128)(2,1)S(1)}, u32[]{:S(2)}, u32[]{:S(2)}) collective-permute-start(bf16[32,6144]{1,0:T(8,128)(2,1)S(1)} %collective-permute-done.4.refs_5_), channel_id=1, source_target_pairs={{0,4},{5,1},{4,8},{9,5},{8,12},{13,9},{12,14},{15,13},{14,10},{11,... | collective-permute-start | bytes 1179656 | tf_op jit(solution)/shard_map/ppermute | solution.py:272
  26.6 1.9 %collective-permute-done.5.refs_6_ = bf16[32,6144]{1,0:T(8,128)(2,1)S(1)} collective-permute-done((bf16[32,6144]{1,0:T(8,128)(2,1)S(1)}, bf16[32,6144]{1,0:T(8,128)(2,1)S(1)}, u32[]{:S(2)}, u32[]{:S(2)}) %collective-permute-start.5) | collective-permute-done | bytes 393248 | tf_op jit(solution)/shard_map/ppermute | solution.py:272
  28.5 1.6 %collective-permute-start.8 = (bf16[32,6144]{1,0:T(8,128)(2,1)S(1)}, bf16[32,6144]{1,0:T(8,128)(2,1)S(1)}, u32[]{:S(2)}, u32[]{:S(2)}) collective-permute-start(bf16[32,6144]{1,0:T(8,128)(2,1)S(1)} %collective-permute-done.5.refs_6_), channel_id=1, source_target_pairs={{0,4},{5,1},{4,8},{9,5},{8,12},{13,9},{12,14},{15,13},{14,10},{11,... | collective-permute-start | bytes 1179656 | tf_op jit(solution)/shard_map/ppermute | solution.py:272
  30.2 5.3 %hold_and_multiply.5 = (bf16[6144,1024]{1,0:T(8,128)(2,1)S(1)}, f32[96,1024]{1,0:T(8,128)S(1)}) custom-call(bf16[32,6144]{1,0:T(8,128)(2,1)S(1)} %get-tuple-element.35.refs_0_, bf16[32,6144]{1,0:T(8,128)(2,1)S(1)} %collective-permute-done.refs_1_, bf16[32,6144]{1,0:T(8,128)(2,1)S(1)} %collective-permute-done.1.refs_2_, ...), custom_call_target="tpu_custom_call" | custom-call | flops 1207959552 | bytes 12582912 | tf_op jit(solution)/shard_map/hold_and_multiply/pallas_call | solution.py:101
  35.5 1.4 %collective-permute-done.8.refs_11_ = bf16[32,6144]{1,0:T(8,128)(2,1)S(1)} collective-permute-done((bf16[32,6144]{1,0:T(8,128)(2,1)S(1)}, bf16[32,6144]{1,0:T(8,128)(2,1)S(1)}, u32[]{:S(2)}, u32[]{:S(2)}) %collective-permute-start.8) | collective-permute-done | bytes 393248 | tf_op jit(solution)/shard_map/ppermute | solution.py:272
  37.2 2.0 %collective-permute-done.9.refs_10_.refs_12_ = bf16[48,6144]{1,0:T(8,128)(2,1)S(1)} collective-permute-done((bf16[48,6144]{1,0:T(8,128)(2,1)S(1)}, bf16[48,6144]{1,0:T(8,128)(2,1)S(1)}, u32[]{:S(2)}, u32[]{:S(2)}) %collective-permute-start.9) | collective-permute-done | bytes 589856 | tf_op jit(solution)/shard_map/ppermute | solution.py:27
  39.2 5.8 %hidden.1 = bf16[256,1024]{1,0:T(8,128)(2,1)S(1)} custom-call(bf16[32,6144]{1,0:T(8,128)(2,1)S(1)} %get-tuple-element.35.refs_0_, bf16[32,6144]{1,0:T(8,128)(2,1)S(1)} %collective-permute-done.refs_1_, bf16[32,6144]{1,0:T(8,128)(2,1)S(1)} %collective-permute-done.1.refs_2_, bf16[32,6144]{1,0:T(8,128)(2,1)S(1)} %collective-permute-done.2.refs_3_, ...), custom_call_target="tpu_custom_call" | custom-call | flops 6442450944 | bytes 25165824 | tf_op jit(solution)/shard_map/hidden/pallas_call | solution.py:101
  45.1 2.1 %fusion.7 = bf16[96,6144]{1,0:T(8,128)(2,1)S(1)} fusion(bf16[1,1024,6144]{2,1,0:T(8,128)(2,1)S(1)} %bitcast.16, bf16[64,1024]{1,0:T(8,128)(2,1)S(1)} %slice.163, bf16[32,1024]{1,0:T(8,128)(2,1)S(1)} %get-tuple-element.83), kind=kOutput, calls=%fused_computation.5 | convolution fusion | flops 1208942592 | bytes 13959168 | tf_op jit(solution)/shard_map/dot_general | solution.py:322
  47.5 1.2 %collective-permute-start.11 = (bf16[16,6144]{1,0:T(8,128)(2,1)S(1)}, bf16[16,6144]{1,0:T(8,128)(2,1)S(1)}, u32[]{:S(2)}, u32[]{:S(2)}) collective-permute-start(bf16[16,6144]{1,0:T(8,128)(2,1)S(1)} %get-tuple-element.72), channel_id=1, source_target_pairs={{1,4},{4,1},{5,8},{8,5},{9,12},{12,9},{13,14},{14,13},{15,10},{10,... | collective-permute-start | bytes 589832 | tf_op jit(solution)/shard_map/ppermute | solution.py:272
  49.6 1.6 %collective-permute-start.17 = (bf16[32,6144]{1,0:T(8,128)(2,1)S(1)}, bf16[32,6144]{1,0:T(8,128)(2,1)S(1)}, u32[]{:S(2)}, u32[]{:S(2)}) collective-permute-start(bf16[32,6144]{1,0:T(8,128)(2,1)S(1)} %pad_maximum_fusion.2), channel_id=1, source_target_pairs={{0,4},{5,1},{4,8},{9,5},{8,12},{13,9},{12,14},{15,13},{14,10},{11,... | collective-permute-start | bytes 1179656 | tf_op jit(solution)/shard_map/ppermute | solution.py:272
  51.3 2.2 %fusion.4 = bf16[160,6144]{1,0:T(8,128)(2,1)S(1)} fusion(bf16[160,1024]{1,0:T(8,128)(2,1)S(1)} %constant_dynamic-update-slice_fusion, bf16[1,1024,6144]{2,1,0:T(8,128)(2,1)S(1)} %bitcast.16), kind=kOutput, calls=%fused_computation.4 | convolution fusion | flops 2014248960 | bytes 14876672 | tf_op jit(solution)/shard_map/dot_general | solution.py:322
  54.8 1.6 %collective-permute-start.14 = (bf16[32,6144]{1,0:T(8,128)(2,1)S(1)}, bf16[32,6144]{1,0:T(8,128)(2,1)S(1)}, u32[]{:S(2)}, u32[]{:S(2)}) collective-permute-start(bf16[32,6144]{1,0:T(8,128)(2,1)S(1)} %add_convert_fusion.4), channel_id=1, source_target_pairs={{0,4},{5,1},{4,8},{9,5},{8,12},{13,9},{12,14},{15,13},{14,10},{11,... | collective-permute-start | bytes 1179656 | tf_op jit(solution)/shard_map/ppermute | solution.py:272
  56.7 2.2 %collective-permute-done.13 = bf16[64,6144]{1,0:T(8,128)(2,1)S(1)} collective-permute-done((bf16[64,6144]{1,0:T(8,128)(2,1)S(1)}, bf16[64,6144]{1,0:T(8,128)(2,1)S(1)}, u32[]{:S(2)}, u32[]{:S(2)}) %collective-permute-start.13) | collective-permute-done | bytes 786464 | tf_op jit(solution)/shard_map/ppermute | solution.py:27
  59.1 1.6 %collective-permute-start.18 = (bf16[32,6144]{1,0:T(8,128)(2,1)S(1)}, bf16[32,6144]{1,0:T(8,128)(2,1)S(1)}, u32[]{:S(2)}, u32[]{:S(2)}) collective-permute-start(bf16[32,6144]{1,0:T(8,128)(2,1)S(1)} %add_convert_fusion.1), channel_id=1, source_target_pairs={{0,4},{5,1},{4,8},{9,5},{8,12},{13,9},{12,14},{15,13},{14,10},{11,... | collective-permute-start | bytes 1179656 | tf_op jit(solution)/shard_map/ppermute | solution.py:272
  60.7 2.5 %collective-permute-done.14 = bf16[32,6144]{1,0:T(8,128)(2,1)S(1)} collective-permute-done((bf16[32,6144]{1,0:T(8,128)(2,1)S(1)}, bf16[32,6144]{1,0:T(8,128)(2,1)S(1)}, u32[]{:S(2)}, u32[]{:S(2)}) %collective-permute-start.14) | collective-permute-done | bytes 393248 | tf_op jit(solution)/shard_map/ppermute | solution.py:272
  63.3 1.6 %collective-permute-start.15 = (bf16[32,6144]{1,0:T(8,128)(2,1)S(1)}, bf16[32,6144]{1,0:T(8,128)(2,1)S(1)}, u32[]{:S(2)}, u32[]{:S(2)}) collective-permute-start(bf16[32,6144]{1,0:T(8,128)(2,1)S(1)} %add_convert_fusion.3), channel_id=1, source_target_pairs={{0,4},{5,1},{4,8},{9,5},{8,12},{13,9},{12,14},{15,13},{14,10},{11,... | collective-permute-start | bytes 1179656 | tf_op jit(solution)/shard_map/ppermute | solution.py:272
  64.9 2.5 %collective-permute-done.18 = bf16[32,6144]{1,0:T(8,128)(2,1)S(1)} collective-permute-done((bf16[32,6144]{1,0:T(8,128)(2,1)S(1)}, bf16[32,6144]{1,0:T(8,128)(2,1)S(1)}, u32[]{:S(2)}, u32[]{:S(2)}) %collective-permute-start.18) | collective-permute-done | bytes 393248 | tf_op jit(solution)/shard_map/ppermute | solution.py:272
  67.5 1.6 %collective-permute-start.19 = (bf16[32,6144]{1,0:T(8,128)(2,1)S(1)}, bf16[32,6144]{1,0:T(8,128)(2,1)S(1)}, u32[]{:S(2)}, u32[]{:S(2)}) collective-permute-start(bf16[32,6144]{1,0:T(8,128)(2,1)S(1)} %add_convert_fusion), channel_id=1, source_target_pairs={{0,4},{5,1},{4,8},{9,5},{8,12},{13,9},{12,14},{15,13},{14,10},{11,... | collective-permute-start | bytes 1179656 | tf_op jit(solution)/shard_map/ppermute | solution.py:272
  69.1 2.5 %collective-permute-done.15 = bf16[32,6144]{1,0:T(8,128)(2,1)S(1)} collective-permute-done((bf16[32,6144]{1,0:T(8,128)(2,1)S(1)}, bf16[32,6144]{1,0:T(8,128)(2,1)S(1)}, u32[]{:S(2)}, u32[]{:S(2)}) %collective-permute-start.15) | collective-permute-done | bytes 393248 | tf_op jit(solution)/shard_map/ppermute | solution.py:272
  71.7 1.6 %collective-permute-start.16 = (bf16[32,6144]{1,0:T(8,128)(2,1)S(1)}, bf16[32,6144]{1,0:T(8,128)(2,1)S(1)}, u32[]{:S(2)}, u32[]{:S(2)}) collective-permute-start(bf16[32,6144]{1,0:T(8,128)(2,1)S(1)} %add_convert_fusion.2), channel_id=1, source_target_pairs={{0,4},{5,1},{4,8},{9,5},{8,12},{13,9},{12,14},{15,13},{14,10},{11,... | collective-permute-start | bytes 1179656 | tf_op jit(solution)/shard_map/ppermute | solution.py:272
  73.3 2.5 %collective-permute-done.19 = bf16[32,6144]{1,0:T(8,128)(2,1)S(1)} collective-permute-done((bf16[32,6144]{1,0:T(8,128)(2,1)S(1)}, bf16[32,6144]{1,0:T(8,128)(2,1)S(1)}, u32[]{:S(2)}, u32[]{:S(2)}) %collective-permute-start.19) | collective-permute-done | bytes 393248 | tf_op jit(solution)/shard_map/ppermute | solution.py:272
  76.6 3.4 %collective-permute-done.16.arrived_ref = bf16[32,6144]{1,0:T(8,128)(2,1)S(1)} collective-permute-done((bf16[32,6144]{1,0:T(8,128)(2,1)S(1)}, bf16[32,6144]{1,0:T(8,128)(2,1)S(1)}, u32[]{:S(2)}, u32[]{:S(2)}) %collective-permute-start.16) | collective-permute-done | bytes 393248 | tf_op jit(solution)/shard_map/ppermute | solution.py:272
  80.0 1.7 %combine.1 = bf16[128,6144]{1,0:T(8,128)(2,1)} custom-call(bf16[32,6144]{1,0:T(8,128)(2,1)S(1)} %collective-permute-done.16.arrived_ref, bf16[32,6144]{1,0:T(8,128)(2,1)S(1)} %collective-permute-done.20.handed_ref, bf16[16,6144]{1,0:T(8,128)(2,1)S(1)} %get-tuple-element.65.product_ref, bf16[128,128]{1,0:T(8,128)(2,1)S(1)} %get-tuple-element.64.mixer_ref), custom_call_target="tpu_custom_call" | custom-call | tf_op jit(solution)/shard_map/combine/pallas_call | solution.py:244
  (56 shorter events, 6.1 us)
Async XLA Ops:
  2.0 3.2 %collective-permute-start = (bf16[32,6144]{1,0:T(8,128)(2,1)S(1)}, bf16[32,6144]{1,0:T(8,128)(2,1)S(1)}, u32[]{:S(2)}, u32[]{:S(2)}) collective-permute-start(bf16[32,6144]{1,0:T(8,128)(2,1)S(1)} %get-tuple-element.36), channel_id=1, source_target_pairs={{0,1},{1,0},{2,3},{3,2},{4,5},{5,4},{6,7},{7,6},{8,9},{9,8},{10,11... | collective-permute-start | bytes 1179656 | tf_op jit(solution)/shard_map/ppermute | solution.py:27
  2.5 8.3 %collective-permute-start.1 = (bf16[32,6144]{1,0:T(8,128)(2,1)S(1)}, bf16[32,6144]{1,0:T(8,128)(2,1)S(1)}, u32[]{:S(2)}, u32[]{:S(2)}) collective-permute-start(bf16[32,6144]{1,0:T(8,128)(2,1)S(1)} %get-tuple-element.35.refs_0_), channel_id=1, source_target_pairs={{0,4},{5,1},{4,8},{9,5},{8,12},{13,9},{12,14},{15,13},{14,10},{11,... | collective-permute-start | bytes 1179656 | tf_op jit(solution)/shard_map/ppermute | solution.py:272
  5.1 11.3 %collective-permute-start.2 = (bf16[32,6144]{1,0:T(8,128)(2,1)S(1)}, bf16[32,6144]{1,0:T(8,128)(2,1)S(1)}, u32[]{:S(2)}, u32[]{:S(2)}) collective-permute-start(bf16[32,6144]{1,0:T(8,128)(2,1)S(1)} %collective-permute-done.refs_1_), channel_id=1, source_target_pairs={{0,4},{5,1},{4,8},{9,5},{8,12},{13,9},{12,14},{15,13},{14,10},{11,... | collective-permute-start | bytes 1179656 | tf_op jit(solution)/shard_map/ppermute | solution.py:272
  10.8 8.4 %collective-permute-start.3 = (bf16[32,6144]{1,0:T(8,128)(2,1)S(1)}, bf16[32,6144]{1,0:T(8,128)(2,1)S(1)}, u32[]{:S(2)}, u32[]{:S(2)}) collective-permute-start(bf16[32,6144]{1,0:T(8,128)(2,1)S(1)} %collective-permute-done.1.refs_2_), channel_id=1, source_target_pairs={{0,4},{5,1},{4,8},{9,5},{8,12},{13,9},{12,14},{15,13},{14,10},{11,... | collective-permute-start | bytes 1179656 | tf_op jit(solution)/shard_map/ppermute | solution.py:272
  16.4 8.5 %collective-permute-start.4 = (bf16[32,6144]{1,0:T(8,128)(2,1)S(1)}, bf16[32,6144]{1,0:T(8,128)(2,1)S(1)}, u32[]{:S(2)}, u32[]{:S(2)}) collective-permute-start(bf16[32,6144]{1,0:T(8,128)(2,1)S(1)} %collective-permute-done.2.refs_3_), channel_id=1, source_target_pairs={{0,4},{5,1},{4,8},{9,5},{8,12},{13,9},{12,14},{15,13},{14,10},{11,... | collective-permute-start | bytes 1179656 | tf_op jit(solution)/shard_map/ppermute | solution.py:272
  19.3 9.2 %collective-permute-start.5 = (bf16[32,6144]{1,0:T(8,128)(2,1)S(1)}, bf16[32,6144]{1,0:T(8,128)(2,1)S(1)}, u32[]{:S(2)}, u32[]{:S(2)}) collective-permute-start(bf16[32,6144]{1,0:T(8,128)(2,1)S(1)} %collective-permute-done.3.refs_4_), channel_id=1, source_target_pairs={{0,4},{5,1},{4,8},{9,5},{8,12},{13,9},{12,14},{15,13},{14,10},{11,... | collective-permute-start | bytes 1179656 | tf_op jit(solution)/shard_map/ppermute | solution.py:272
  24.9 12.1 %collective-permute-start.6 = (bf16[32,6144]{1,0:T(8,128)(2,1)S(1)}, bf16[32,6144]{1,0:T(8,128)(2,1)S(1)}, u32[]{:S(2)}, u32[]{:S(2)}) collective-permute-start(bf16[32,6144]{1,0:T(8,128)(2,1)S(1)} %collective-permute-done.4.refs_5_), channel_id=1, source_target_pairs={{0,4},{5,1},{4,8},{9,5},{8,12},{13,9},{12,14},{15,13},{14,10},{11,... | collective-permute-start | bytes 1179656 | tf_op jit(solution)/shard_map/ppermute | solution.py:272
  28.5 8.5 %collective-permute-start.8 = (bf16[32,6144]{1,0:T(8,128)(2,1)S(1)}, bf16[32,6144]{1,0:T(8,128)(2,1)S(1)}, u32[]{:S(2)}, u32[]{:S(2)}) collective-permute-start(bf16[32,6144]{1,0:T(8,128)(2,1)S(1)} %collective-permute-done.5.refs_6_), channel_id=1, source_target_pairs={{0,4},{5,1},{4,8},{9,5},{8,12},{13,9},{12,14},{15,13},{14,10},{11,... | collective-permute-start | bytes 1179656 | tf_op jit(solution)/shard_map/ppermute | solution.py:272
  30.1 7.0 %collective-permute-start.7 = (bf16[64,6144]{1,0:T(8,128)(2,1)S(1)}, bf16[64,6144]{1,0:T(8,128)(2,1)S(1)}, u32[]{:S(2)}, u32[]{:S(2)}) collective-permute-start(bf16[64,6144]{1,0:T(8,128)(2,1)S(1)} %pad_maximum_fusion), channel_id=1, source_target_pairs={{0,1},{1,0},{2,3},{3,2},{4,5},{5,4},{6,7},{7,6},{8,9},{9,8},{10,11... | collective-permute-start | bytes 2359304 | tf_op jit(solution)/shard_map/ppermute | solution.py:27
  37.1 2.1 %collective-permute-start.9 = (bf16[48,6144]{1,0:T(8,128)(2,1)S(1)}, bf16[48,6144]{1,0:T(8,128)(2,1)S(1)}, u32[]{:S(2)}, u32[]{:S(2)}) collective-permute-start(bf16[48,6144]{1,0:T(8,128)(2,1)S(1)} %pad_maximum_fusion.1), channel_id=1, source_target_pairs={{0,1},{1,0},{2,3},{3,2},{4,5},{5,4},{6,7},{7,6},{8,9},{9,8},{10,11... | collective-permute-start | bytes 1769480 | tf_op jit(solution)/shard_map/ppermute | solution.py:27
  39.1 5.9 %slice-start = ((s8[12582912]{0:T(1024)(128)(4,1)}), s8[4194304]{0:T(1024)(128)(4,1)S(1)}, s32[]{:S(2)}) async-start(s8[12582912]{0:T(1024)(128)(4,1)} %bitcast.15), calls=%async_computation | async-start | bytes 8388608
  39.1 5.9 %slice-start.1 = ((s8[12582912]{0:T(1024)(128)(4,1)}), s8[4194304]{0:T(1024)(128)(4,1)S(1)}, s32[]{:S(2)}) async-start(s8[12582912]{0:T(1024)(128)(4,1)} %bitcast.15), calls=%async_computation.1 | async-start | bytes 8388608
  39.2 5.9 %slice-start.2 = ((s8[12582912]{0:T(1024)(128)(4,1)}), s8[4194304]{0:T(1024)(128)(4,1)S(1)}, s32[]{:S(2)}) async-start(s8[12582912]{0:T(1024)(128)(4,1)} %bitcast.15), calls=%async_computation.2 | async-start | bytes 8388608
  47.2 2.3 %collective-permute-start.12 = (bf16[32,6144]{1,0:T(8,128)(2,1)S(1)}, bf16[32,6144]{1,0:T(8,128)(2,1)S(1)}, u32[]{:S(2)}, u32[]{:S(2)}) collective-permute-start(bf16[32,6144]{1,0:T(8,128)(2,1)S(1)} %slice.167), channel_id=1, source_target_pairs={{0,1},{1,0},{2,3},{3,2},{4,5},{5,4},{6,7},{7,6},{8,9},{9,8},{10,11... | collective-permute-start | bytes 1179656 | tf_op jit(solution)/shard_map/ppermute | solution.py:27
  47.5 6.4 %collective-permute-start.11 = (bf16[16,6144]{1,0:T(8,128)(2,1)S(1)}, bf16[16,6144]{1,0:T(8,128)(2,1)S(1)}, u32[]{:S(2)}, u32[]{:S(2)}) collective-permute-start(bf16[16,6144]{1,0:T(8,128)(2,1)S(1)} %get-tuple-element.72), channel_id=1, source_target_pairs={{1,4},{4,1},{5,8},{8,5},{9,12},{12,9},{13,14},{14,13},{15,10},{10,... | collective-permute-start | bytes 589832 | tf_op jit(solution)/shard_map/ppermute | solution.py:272
  48.7 6.1 %collective-permute-start.10 = (bf16[16,6144]{1,0:T(8,128)(2,1)S(1)}, bf16[16,6144]{1,0:T(8,128)(2,1)S(1)}, u32[]{:S(2)}, u32[]{:S(2)}) collective-permute-start(bf16[16,6144]{1,0:T(8,128)(2,1)S(1)} %get-tuple-element.73), channel_id=1, source_target_pairs={{0,4},{5,1},{4,8},{9,5},{8,12},{13,9},{12,14},{15,13},{14,10},{11,... | collective-permute-start | bytes 589832 | tf_op jit(solution)/shard_map/ppermute | solution.py:272
  49.6 9.3 %collective-permute-start.17 = (bf16[32,6144]{1,0:T(8,128)(2,1)S(1)}, bf16[32,6144]{1,0:T(8,128)(2,1)S(1)}, u32[]{:S(2)}, u32[]{:S(2)}) collective-permute-start(bf16[32,6144]{1,0:T(8,128)(2,1)S(1)} %pad_maximum_fusion.2), channel_id=1, source_target_pairs={{0,4},{5,1},{4,8},{9,5},{8,12},{13,9},{12,14},{15,13},{14,10},{11,... | collective-permute-start | bytes 1179656 | tf_op jit(solution)/shard_map/ppermute | solution.py:272
  54.8 8.3 %collective-permute-start.14 = (bf16[32,6144]{1,0:T(8,128)(2,1)S(1)}, bf16[32,6144]{1,0:T(8,128)(2,1)S(1)}, u32[]{:S(2)}, u32[]{:S(2)}) collective-permute-start(bf16[32,6144]{1,0:T(8,128)(2,1)S(1)} %add_convert_fusion.4), channel_id=1, source_target_pairs={{0,4},{5,1},{4,8},{9,5},{8,12},{13,9},{12,14},{15,13},{14,10},{11,... | collective-permute-start | bytes 1179656 | tf_op jit(solution)/shard_map/ppermute | solution.py:272
  56.5 2.4 %collective-permute-start.13 = (bf16[64,6144]{1,0:T(8,128)(2,1)S(1)}, bf16[64,6144]{1,0:T(8,128)(2,1)S(1)}, u32[]{:S(2)}, u32[]{:S(2)}) collective-permute-start(bf16[64,6144]{1,0:T(8,128)(2,1)S(1)} %slice.145), channel_id=1, source_target_pairs={{0,1},{1,0},{2,3},{3,2},{4,5},{5,4},{6,7},{7,6},{8,9},{9,8},{10,11... | collective-permute-start | bytes 2359304 | tf_op jit(solution)/shard_map/ppermute | solution.py:27
  59.1 8.3 %collective-permute-start.18 = (bf16[32,6144]{1,0:T(8,128)(2,1)S(1)}, bf16[32,6144]{1,0:T(8,128)(2,1)S(1)}, u32[]{:S(2)}, u32[]{:S(2)}) collective-permute-start(bf16[32,6144]{1,0:T(8,128)(2,1)S(1)} %add_convert_fusion.1), channel_id=1, source_target_pairs={{0,4},{5,1},{4,8},{9,5},{8,12},{13,9},{12,14},{15,13},{14,10},{11,... | collective-permute-start | bytes 1179656 | tf_op jit(solution)/shard_map/ppermute | solution.py:272
  63.3 8.3 %collective-permute-start.15 = (bf16[32,6144]{1,0:T(8,128)(2,1)S(1)}, bf16[32,6144]{1,0:T(8,128)(2,1)S(1)}, u32[]{:S(2)}, u32[]{:S(2)}) collective-permute-start(bf16[32,6144]{1,0:T(8,128)(2,1)S(1)} %add_convert_fusion.3), channel_id=1, source_target_pairs={{0,4},{5,1},{4,8},{9,5},{8,12},{13,9},{12,14},{15,13},{14,10},{11,... | collective-permute-start | bytes 1179656 | tf_op jit(solution)/shard_map/ppermute | solution.py:272
  67.5 8.3 %collective-permute-start.19 = (bf16[32,6144]{1,0:T(8,128)(2,1)S(1)}, bf16[32,6144]{1,0:T(8,128)(2,1)S(1)}, u32[]{:S(2)}, u32[]{:S(2)}) collective-permute-start(bf16[32,6144]{1,0:T(8,128)(2,1)S(1)} %add_convert_fusion), channel_id=1, source_target_pairs={{0,4},{5,1},{4,8},{9,5},{8,12},{13,9},{12,14},{15,13},{14,10},{11,... | collective-permute-start | bytes 1179656 | tf_op jit(solution)/shard_map/ppermute | solution.py:272
  71.7 8.3 %collective-permute-start.16 = (bf16[32,6144]{1,0:T(8,128)(2,1)S(1)}, bf16[32,6144]{1,0:T(8,128)(2,1)S(1)}, u32[]{:S(2)}, u32[]{:S(2)}) collective-permute-start(bf16[32,6144]{1,0:T(8,128)(2,1)S(1)} %add_convert_fusion.2), channel_id=1, source_target_pairs={{0,4},{5,1},{4,8},{9,5},{8,12},{13,9},{12,14},{15,13},{14,10},{11,... | collective-permute-start | bytes 1179656 | tf_op jit(solution)/shard_map/ppermute | solution.py:272
  75.9 4.1 %collective-permute-start.20 = (bf16[32,6144]{1,0:T(8,128)(2,1)S(1)}, bf16[32,6144]{1,0:T(8,128)(2,1)S(1)}, u32[]{:S(2)}, u32[]{:S(2)}) collective-permute-start(bf16[32,6144]{1,0:T(8,128)(2,1)S(1)} %pad_maximum_fusion.3), channel_id=1, source_target_pairs={{0,1},{1,0},{2,3},{3,2},{4,5},{5,4},{6,7},{7,6},{8,9},{9,8},{10,11... | collective-permute-start | bytes 1179656 | tf_op jit(solution)/shard_map/ppermute | solution.py:27

commit v5 on v4

--- a/solution.py
+++ b/solution.py
@@ -135,7 +135,7 @@
 def hold_and_multiply(rows, weights, begin, depth, before):
     width = weights.shape[1]
     total = sum(c for _, _, c in rows)
-    step = tile_of(depth, 1536)
+    step = tile_of(depth, 768)
     pieces = depth // step
     before = [] if before is None else [before]
 
@@ -181,7 +181,7 @@
 def hidden_of(rows, gates, ups, gate_done=None, up_done=None):
     total = sum(c for _, _, c in rows)
     width = gates[0].shape[1]
-    tile = tile_of(width, 256)
+    tile = tile_of(width, 1024)
     before = [] if gate_done is None else [gate_done, up_done]
 
     def kernel(*refs):
@@ -229,29 +229,43 @@
 def combine(arrived, handed, product, mixer):
     width = arrived.shape[1]
     token_count = mixer.shape[0]
-    tile = tile_of(width, 3072)
-    column = lambda j: (0, j)
-
-    def kernel(arrived_ref, handed_ref, product_ref, mixer_ref, out_ref):
-        rows = arrived_ref[...].astype(jnp.float32) + handed_ref[...].astype(jnp.float32)
-        mine = (rows[:CAP] + product_ref[...].astype(jnp.float32)).astype(jnp.bfloat16)
-        theirs = rows[CAP:].astype(jnp.bfloat16)
-        rows = jnp.concatenate([mine, theirs, mine, theirs], axis=0)
-        out_ref[...] = jnp.dot(
-            mixer_ref[:, : 2 * BLOCK], rows, preferred_element_type=jnp.float32
-        ).astype(jnp.bfloat16)
-
+    tile = tile_of(width, 1536)
+    steps = width // tile
+
+    def kernel(arrived_ref, handed_ref, product_ref, mixer_ref, out_hbm, mixed_ref, done):
+        copies = []
+        for i in range(steps):
+            here = slice(i * tile, (i + 1) * tile)
+            rows = arrived_ref[:, here].astype(jnp.float32) + handed_ref[:, here].astype(
+                jnp.float32
+            )
+            mine = (rows[:CAP] + product_ref[:CAP, here].astype(jnp.float32)).astype(jnp.bfloat16)
+            theirs = rows[CAP:].astype(jnp.bfloat16)
+            rows = jnp.concatenate([mine, theirs, mine, theirs], axis=0)
+            mixed_ref[:, here] = jnp.dot(
+                mixer_ref[:, : 2 * BLOCK], rows, preferred_element_type=jnp.float32
+            ).astype(jnp.bfloat16)
+            copies.append(
+                pltpu.make_async_copy(
+                    mixed_ref.at[:, pl.ds(i * tile, tile)],
+                    out_hbm.at[:, pl.ds(i * tile, tile)],
+                    done.at[i],
+                )
+            )
+            copies[i].start()
+        for copy in copies:
+            copy.wait()
+
+    local_spec = pl.BlockSpec(memory_space=pltpu.VMEM)
     return pl.pallas_call(
         kernel,
-        grid=(width // tile,),
-        in_specs=[
-            pl.BlockSpec((BLOCK, tile), column),
-            pl.BlockSpec((BLOCK, tile), column),
-            pl.BlockSpec((CAP, tile), column),
-            pl.BlockSpec(mixer.shape, lambda j: (0, 0)),
+        in_specs=[local_spec] * 4,
+        out_specs=pl.BlockSpec(memory_space=pltpu.HBM),
+        out_shape=array(token_count, width),
+        scratch_shapes=[
+            pltpu.VMEM((token_count, width), jnp.bfloat16),
+            pltpu.SemaphoreType.DMA((steps,)),
         ],
-        out_specs=pl.BlockSpec((token_count, tile), column),
-        out_shape=array(token_count, width),
         compiler_params=pltpu.CompilerParams(vmem_limit_bytes=VMEM_LIMIT),
         name="combine",
     )(arrived, handed, product, mixer)

time: 81.9 us -> 80.5 us (0.983)
  Pallas kernels: 21.8 us -> 19.9 us
    pallas_call x4, Pallas kernels: 18.2 us -> 16.5 us  [call(): pl.pallas_call(kernel, in_specs=[pl.BlockSpec(memory_space=m) for _, m in...]
  transfers between devices with their start and end apart: 21 -> 21, of which waited for: 13 -> 13; matrix products, arithmetic and copies ran while one was open for 4% -> 4% of each run, Pallas kernels for 15% -> 14%
where the time goes in v5:
time: 80.5 us; the launch traced here: 80.4 us
  waiting for transfers between devices  27.4 us (34%)
  starting transfers between devices  27.2 us (34%)
  Pallas kernels  19.9 us (25%)
  matrix products  4.34 us (5%)
    ppermute x15, starting transfers between devices, hop(): return lax.ppermute(value, ('ept', 'exp'), pairs)  25.3 us
    ppermute x15, waiting for transfers between devices, hop(): return lax.ppermute(value, ('ept', 'exp'), pairs)  23.4 us
    pallas_call x4, Pallas kernels, call(): pl.pallas_call(kernel, in_specs=[pl.BlockSpec(memory_space=m) for _, m in...  16.5 us
    dot_general x2, matrix products, product_of(): jnp.dot(jnp.concatenate(parts, axis=0), w_down, preferred_element_type=jn...  4.34 us
    ppermute x6, waiting for transfers between devices, swap(): return lax.ppermute(value, 'exp', [(0, 1), (1, 0)])  3.97 us
    pallas_call x1, Pallas kernels, dispatch(): pl.pallas_call(dispatch_kernel, grid_spec=pltpu.PrefetchScalarGridSpec(nu...  1.97 us
    ppermute x6, starting transfers between devices, swap(): return lax.ppermute(value, 'exp', [(0, 1), (1, 0)])  1.89 us
  transfers between devices with their start and end apart: 21, of which 13 were waited for; matrix products, arithmetic and copies ran while one was open for 4% of the time, Pallas kernels for 14%

profile of v5, /device:TPU:0, one launch (start us, length us, event | category | flops | bytes accessed | tf_op | source)
XLA Modules:
  0.0 80.4 jit_solution(4259882775027228400)
XLA Ops:
  0.0 2.0 %dispatch.1 = (bf16[32,6144]{1,0:T(8,128)(2,1)S(1)}, bf16[32,6144]{1,0:T(8,128)(2,1)S(1)}, bf16[128,128]{1,0:T(8,128)(2,1)S(1)}) custom-call(s32[1]{0:T(128)} %bitcast.me_ref, s32[2,128]{1,0:T(2,128)} %bitcast.20, f32[2,128]{1,0:T(2,128)} %bitcast.21, bf16[128,6144]{1,0:T(8,128)(2,1)} %tokens_ref.1), custom_call_target="tpu_custom_call" | custom-call | tf_op jit(solution)/shard_map/dispatch/pallas_call | solution.py:73
  2.5 2.6 %collective-permute-start.1 = (bf16[32,6144]{1,0:T(8,128)(2,1)S(1)}, bf16[32,6144]{1,0:T(8,128)(2,1)S(1)}, u32[]{:S(2)}, u32[]{:S(2)}) collective-permute-start(bf16[32,6144]{1,0:T(8,128)(2,1)S(1)} %get-tuple-element.35.refs_0_), channel_id=1, source_target_pairs={{0,4},{5,1},{4,8},{9,5},{8,12},{13,9},{12,14},{15,13},{14,10},{11,... | collective-permute-start | bytes 1179656 | tf_op jit(solution)/shard_map/ppermute | solution.py:286
  5.1 1.7 %collective-permute-start.2 = (bf16[32,6144]{1,0:T(8,128)(2,1)S(1)}, bf16[32,6144]{1,0:T(8,128)(2,1)S(1)}, u32[]{:S(2)}, u32[]{:S(2)}) collective-permute-start(bf16[32,6144]{1,0:T(8,128)(2,1)S(1)} %collective-permute-done.refs_1_), channel_id=1, source_target_pairs={{0,4},{5,1},{4,8},{9,5},{8,12},{13,9},{12,14},{15,13},{14,10},{11,... | collective-permute-start | bytes 1179656 | tf_op jit(solution)/shard_map/ppermute | solution.py:286
  6.8 4.0 %collective-permute-done.1.refs_2_ = bf16[32,6144]{1,0:T(8,128)(2,1)S(1)} collective-permute-done((bf16[32,6144]{1,0:T(8,128)(2,1)S(1)}, bf16[32,6144]{1,0:T(8,128)(2,1)S(1)}, u32[]{:S(2)}, u32[]{:S(2)}) %collective-permute-start.1) | collective-permute-done | bytes 393248 | tf_op jit(solution)/shard_map/ppermute | solution.py:286
  10.8 2.1 %collective-permute-start.3 = (bf16[32,6144]{1,0:T(8,128)(2,1)S(1)}, bf16[32,6144]{1,0:T(8,128)(2,1)S(1)}, u32[]{:S(2)}, u32[]{:S(2)}) collective-permute-start(bf16[32,6144]{1,0:T(8,128)(2,1)S(1)} %collective-permute-done.1.refs_2_), channel_id=1, source_target_pairs={{0,4},{5,1},{4,8},{9,5},{8,12},{13,9},{12,14},{15,13},{14,10},{11,... | collective-permute-start | bytes 1179656 | tf_op jit(solution)/shard_map/ppermute | solution.py:286
  12.9 3.2 %hold_and_multiply.3 = (bf16[3072,1024]{1,0:T(8,128)(2,1)S(1)}, f32[48,1024]{1,0:T(8,128)S(1)}) custom-call(bf16[32,6144]{1,0:T(8,128)(2,1)S(1)} %get-tuple-element.35.refs_0_, bf16[32,6144]{1,0:T(8,128)(2,1)S(1)} %collective-permute-done.refs_1_, bf16[32,6144]{1,0:T(8,128)(2,1)S(1)} %collective-permute-done.1.refs_2_, bf16[6144,1024]{1,0:T(8,128)(2,1)} %bitcast.17), custom_call_target="tpu_custom_call" | custom-call | flops 301989888 | bytes 6291456 | tf_op jit(solution)/shard_map/hold_and_multiply/pallas_call | solution.py:101
  16.2 1.6 %collective-permute-start.4 = (bf16[32,6144]{1,0:T(8,128)(2,1)S(1)}, bf16[32,6144]{1,0:T(8,128)(2,1)S(1)}, u32[]{:S(2)}, u32[]{:S(2)}) collective-permute-start(bf16[32,6144]{1,0:T(8,128)(2,1)S(1)} %collective-permute-done.2.refs_3_), channel_id=1, source_target_pairs={{0,4},{5,1},{4,8},{9,5},{8,12},{13,9},{12,14},{15,13},{14,10},{11,... | collective-permute-start | bytes 1179656 | tf_op jit(solution)/shard_map/ppermute | solution.py:286
  17.8 1.5 %collective-permute-done.3.refs_4_ = bf16[32,6144]{1,0:T(8,128)(2,1)S(1)} collective-permute-done((bf16[32,6144]{1,0:T(8,128)(2,1)S(1)}, bf16[32,6144]{1,0:T(8,128)(2,1)S(1)}, u32[]{:S(2)}, u32[]{:S(2)}) %collective-permute-start.3) | collective-permute-done | bytes 393248 | tf_op jit(solution)/shard_map/ppermute | solution.py:286
  19.3 2.1 %collective-permute-start.5 = (bf16[32,6144]{1,0:T(8,128)(2,1)S(1)}, bf16[32,6144]{1,0:T(8,128)(2,1)S(1)}, u32[]{:S(2)}, u32[]{:S(2)}) collective-permute-start(bf16[32,6144]{1,0:T(8,128)(2,1)S(1)} %collective-permute-done.3.refs_4_), channel_id=1, source_target_pairs={{0,4},{5,1},{4,8},{9,5},{8,12},{13,9},{12,14},{15,13},{14,10},{11,... | collective-permute-start | bytes 1179656 | tf_op jit(solution)/shard_map/ppermute | solution.py:286
  21.4 3.3 %hold_and_multiply.4 = (bf16[3072,1024]{1,0:T(8,128)(2,1)S(1)}, f32[48,1024]{1,0:T(8,128)S(1)}) custom-call(bf16[32,6144]{1,0:T(8,128)(2,1)S(1)} %get-tuple-element.35.refs_0_, bf16[32,6144]{1,0:T(8,128)(2,1)S(1)} %collective-permute-done.refs_1_, bf16[32,6144]{1,0:T(8,128)(2,1)S(1)} %collective-permute-done.1.refs_2_, bf16[6144,1024]{1,0:T(8,128)(2,1)} %bitcast.18, ...), custom_call_target="tpu_custom_call" | custom-call | flops 301989888 | bytes 6291456 | tf_op jit(solution)/shard_map/hold_and_multiply/pallas_call | solution.py:101
  24.7 1.6 %collective-permute-start.6 = (bf16[32,6144]{1,0:T(8,128)(2,1)S(1)}, bf16[32,6144]{1,0:T(8,128)(2,1)S(1)}, u32[]{:S(2)}, u32[]{:S(2)}) collective-permute-start(bf16[32,6144]{1,0:T(8,128)(2,1)S(1)} %collective-permute-done.4.refs_5_), channel_id=1, source_target_pairs={{0,4},{5,1},{4,8},{9,5},{8,12},{13,9},{12,14},{15,13},{14,10},{11,... | collective-permute-start | bytes 1179656 | tf_op jit(solution)/shard_map/ppermute | solution.py:286
  26.3 1.9 %collective-permute-done.5.refs_6_ = bf16[32,6144]{1,0:T(8,128)(2,1)S(1)} collective-permute-done((bf16[32,6144]{1,0:T(8,128)(2,1)S(1)}, bf16[32,6144]{1,0:T(8,128)(2,1)S(1)}, u32[]{:S(2)}, u32[]{:S(2)}) %collective-permute-start.5) | collective-permute-done | bytes 393248 | tf_op jit(solution)/shard_map/ppermute | solution.py:286
  28.2 1.6 %collective-permute-start.8 = (bf16[32,6144]{1,0:T(8,128)(2,1)S(1)}, bf16[32,6144]{1,0:T(8,128)(2,1)S(1)}, u32[]{:S(2)}, u32[]{:S(2)}) collective-permute-start(bf16[32,6144]{1,0:T(8,128)(2,1)S(1)} %collective-permute-done.5.refs_6_), channel_id=1, source_target_pairs={{0,4},{5,1},{4,8},{9,5},{8,12},{13,9},{12,14},{15,13},{14,10},{11,... | collective-permute-start | bytes 1179656 | tf_op jit(solution)/shard_map/ppermute | solution.py:286
  30.0 5.1 %hold_and_multiply.5 = (bf16[6144,1024]{1,0:T(8,128)(2,1)S(1)}, f32[96,1024]{1,0:T(8,128)S(1)}) custom-call(bf16[32,6144]{1,0:T(8,128)(2,1)S(1)} %get-tuple-element.35.refs_0_, bf16[32,6144]{1,0:T(8,128)(2,1)S(1)} %collective-permute-done.refs_1_, bf16[32,6144]{1,0:T(8,128)(2,1)S(1)} %collective-permute-done.1.refs_2_, ...), custom_call_target="tpu_custom_call" | custom-call | flops 1207959552 | bytes 12582912 | tf_op jit(solution)/shard_map/hold_and_multiply/pallas_call | solution.py:101
  35.1 1.7 %collective-permute-done.8.refs_11_ = bf16[32,6144]{1,0:T(8,128)(2,1)S(1)} collective-permute-done((bf16[32,6144]{1,0:T(8,128)(2,1)S(1)}, bf16[32,6144]{1,0:T(8,128)(2,1)S(1)}, u32[]{:S(2)}, u32[]{:S(2)}) %collective-permute-start.8) | collective-permute-done | bytes 393248 | tf_op jit(solution)/shard_map/ppermute | solution.py:286
  36.9 2.0 %collective-permute-done.9.refs_10_.refs_12_ = bf16[48,6144]{1,0:T(8,128)(2,1)S(1)} collective-permute-done((bf16[48,6144]{1,0:T(8,128)(2,1)S(1)}, bf16[48,6144]{1,0:T(8,128)(2,1)S(1)}, u32[]{:S(2)}, u32[]{:S(2)}) %collective-permute-start.9) | collective-permute-done | bytes 589856 | tf_op jit(solution)/shard_map/ppermute | solution.py:27
  38.9 4.9 %hidden.1 = bf16[256,1024]{1,0:T(8,128)(2,1)S(1)} custom-call(bf16[32,6144]{1,0:T(8,128)(2,1)S(1)} %get-tuple-element.35.refs_0_, bf16[32,6144]{1,0:T(8,128)(2,1)S(1)} %collective-permute-done.refs_1_, bf16[32,6144]{1,0:T(8,128)(2,1)S(1)} %collective-permute-done.1.refs_2_, bf16[32,6144]{1,0:T(8,128)(2,1)S(1)} %collective-permute-done.2.refs_3_, ...), custom_call_target="tpu_custom_call" | custom-call | flops 6442450944 | bytes 25165824 | tf_op jit(solution)/shard_map/hidden/pallas_call | solution.py:101
  43.9 2.1 %fusion.7 = bf16[96,6144]{1,0:T(8,128)(2,1)S(1)} fusion(bf16[1,1024,6144]{2,1,0:T(8,128)(2,1)S(1)} %bitcast.16, bf16[64,1024]{1,0:T(8,128)(2,1)S(1)} %slice.163, bf16[32,1024]{1,0:T(8,128)(2,1)S(1)} %get-tuple-element.83), kind=kOutput, calls=%fused_computation.5 | convolution fusion | flops 1208942592 | bytes 13959168 | tf_op jit(solution)/shard_map/dot_general | solution.py:336
  46.3 1.5 %collective-permute-start.11 = (bf16[16,6144]{1,0:T(8,128)(2,1)S(1)}, bf16[16,6144]{1,0:T(8,128)(2,1)S(1)}, u32[]{:S(2)}, u32[]{:S(2)}) collective-permute-start(bf16[16,6144]{1,0:T(8,128)(2,1)S(1)} %get-tuple-element.72), channel_id=1, source_target_pairs={{1,4},{4,1},{5,8},{8,5},{9,12},{12,9},{13,14},{14,13},{15,10},{10,... | collective-permute-start | bytes 589832 | tf_op jit(solution)/shard_map/ppermute | solution.py:286
  48.4 1.8 %collective-permute-start.17 = (bf16[32,6144]{1,0:T(8,128)(2,1)S(1)}, bf16[32,6144]{1,0:T(8,128)(2,1)S(1)}, u32[]{:S(2)}, u32[]{:S(2)}) collective-permute-start(bf16[32,6144]{1,0:T(8,128)(2,1)S(1)} %pad_maximum_fusion.2), channel_id=1, source_target_pairs={{0,4},{5,1},{4,8},{9,5},{8,12},{13,9},{12,14},{15,13},{14,10},{11,... | collective-permute-start | bytes 1179656 | tf_op jit(solution)/shard_map/ppermute | solution.py:286
  50.3 2.2 %fusion.4 = bf16[160,6144]{1,0:T(8,128)(2,1)S(1)} fusion(bf16[160,1024]{1,0:T(8,128)(2,1)S(1)} %constant_dynamic-update-slice_fusion, bf16[1,1024,6144]{2,1,0:T(8,128)(2,1)S(1)} %bitcast.16), kind=kOutput, calls=%fused_computation.4 | convolution fusion | flops 2014248960 | bytes 14876672 | tf_op jit(solution)/shard_map/dot_general | solution.py:336
  53.6 1.6 %collective-permute-start.14 = (bf16[32,6144]{1,0:T(8,128)(2,1)S(1)}, bf16[32,6144]{1,0:T(8,128)(2,1)S(1)}, u32[]{:S(2)}, u32[]{:S(2)}) collective-permute-start(bf16[32,6144]{1,0:T(8,128)(2,1)S(1)} %add_convert_fusion.4), channel_id=1, source_target_pairs={{0,4},{5,1},{4,8},{9,5},{8,12},{13,9},{12,14},{15,13},{14,10},{11,... | collective-permute-start | bytes 1179656 | tf_op jit(solution)/shard_map/ppermute | solution.py:286
  55.7 2.0 %collective-permute-done.13 = bf16[64,6144]{1,0:T(8,128)(2,1)S(1)} collective-permute-done((bf16[64,6144]{1,0:T(8,128)(2,1)S(1)}, bf16[64,6144]{1,0:T(8,128)(2,1)S(1)}, u32[]{:S(2)}, u32[]{:S(2)}) %collective-permute-start.13) | collective-permute-done | bytes 786464 | tf_op jit(solution)/shard_map/ppermute | solution.py:27
  57.8 1.6 %collective-permute-start.18 = (bf16[32,6144]{1,0:T(8,128)(2,1)S(1)}, bf16[32,6144]{1,0:T(8,128)(2,1)S(1)}, u32[]{:S(2)}, u32[]{:S(2)}) collective-permute-start(bf16[32,6144]{1,0:T(8,128)(2,1)S(1)} %add_convert_fusion.1), channel_id=1, source_target_pairs={{0,4},{5,1},{4,8},{9,5},{8,12},{13,9},{12,14},{15,13},{14,10},{11,... | collective-permute-start | bytes 1179656 | tf_op jit(solution)/shard_map/ppermute | solution.py:286
  59.5 2.5 %collective-permute-done.14 = bf16[32,6144]{1,0:T(8,128)(2,1)S(1)} collective-permute-done((bf16[32,6144]{1,0:T(8,128)(2,1)S(1)}, bf16[32,6144]{1,0:T(8,128)(2,1)S(1)}, u32[]{:S(2)}, u32[]{:S(2)}) %collective-permute-start.14) | collective-permute-done | bytes 393248 | tf_op jit(solution)/shard_map/ppermute | solution.py:286
  62.0 1.6 %collective-permute-start.15 = (bf16[32,6144]{1,0:T(8,128)(2,1)S(1)}, bf16[32,6144]{1,0:T(8,128)(2,1)S(1)}, u32[]{:S(2)}, u32[]{:S(2)}) collective-permute-start(bf16[32,6144]{1,0:T(8,128)(2,1)S(1)} %add_convert_fusion.3), channel_id=1, source_target_pairs={{0,4},{5,1},{4,8},{9,5},{8,12},{13,9},{12,14},{15,13},{14,10},{11,... | collective-permute-start | bytes 1179656 | tf_op jit(solution)/shard_map/ppermute | solution.py:286
  63.7 2.5 %collective-permute-done.18 = bf16[32,6144]{1,0:T(8,128)(2,1)S(1)} collective-permute-done((bf16[32,6144]{1,0:T(8,128)(2,1)S(1)}, bf16[32,6144]{1,0:T(8,128)(2,1)S(1)}, u32[]{:S(2)}, u32[]{:S(2)}) %collective-permute-start.18) | collective-permute-done | bytes 393248 | tf_op jit(solution)/shard_map/ppermute | solution.py:286
  66.3 1.6 %collective-permute-start.19 = (bf16[32,6144]{1,0:T(8,128)(2,1)S(1)}, bf16[32,6144]{1,0:T(8,128)(2,1)S(1)}, u32[]{:S(2)}, u32[]{:S(2)}) collective-permute-start(bf16[32,6144]{1,0:T(8,128)(2,1)S(1)} %add_convert_fusion), channel_id=1, source_target_pairs={{0,4},{5,1},{4,8},{9,5},{8,12},{13,9},{12,14},{15,13},{14,10},{11,... | collective-permute-start | bytes 1179656 | tf_op jit(solution)/shard_map/ppermute | solution.py:286
  67.9 2.5 %collective-permute-done.15 = bf16[32,6144]{1,0:T(8,128)(2,1)S(1)} collective-permute-done((bf16[32,6144]{1,0:T(8,128)(2,1)S(1)}, bf16[32,6144]{1,0:T(8,128)(2,1)S(1)}, u32[]{:S(2)}, u32[]{:S(2)}) %collective-permute-start.15) | collective-permute-done | bytes 393248 | tf_op jit(solution)/shard_map/ppermute | solution.py:286
  70.5 1.6 %collective-permute-start.16 = (bf16[32,6144]{1,0:T(8,128)(2,1)S(1)}, bf16[32,6144]{1,0:T(8,128)(2,1)S(1)}, u32[]{:S(2)}, u32[]{:S(2)}) collective-permute-start(bf16[32,6144]{1,0:T(8,128)(2,1)S(1)} %add_convert_fusion.2), channel_id=1, source_target_pairs={{0,4},{5,1},{4,8},{9,5},{8,12},{13,9},{12,14},{15,13},{14,10},{11,... | collective-permute-start | bytes 1179656 | tf_op jit(solution)/shard_map/ppermute | solution.py:286
  72.1 2.5 %collective-permute-done.19 = bf16[32,6144]{1,0:T(8,128)(2,1)S(1)} collective-permute-done((bf16[32,6144]{1,0:T(8,128)(2,1)S(1)}, bf16[32,6144]{1,0:T(8,128)(2,1)S(1)}, u32[]{:S(2)}, u32[]{:S(2)}) %collective-permute-start.19) | collective-permute-done | bytes 393248 | tf_op jit(solution)/shard_map/ppermute | solution.py:286
  75.4 3.4 %collective-permute-done.16.arrived_ref = bf16[32,6144]{1,0:T(8,128)(2,1)S(1)} collective-permute-done((bf16[32,6144]{1,0:T(8,128)(2,1)S(1)}, bf16[32,6144]{1,0:T(8,128)(2,1)S(1)}, u32[]{:S(2)}, u32[]{:S(2)}) %collective-permute-start.16) | collective-permute-done | bytes 393248 | tf_op jit(solution)/shard_map/ppermute | solution.py:286
  (56 shorter events, 6.1 us)
Async XLA Ops:
  2.0 3.2 %collective-permute-start = (bf16[32,6144]{1,0:T(8,128)(2,1)S(1)}, bf16[32,6144]{1,0:T(8,128)(2,1)S(1)}, u32[]{:S(2)}, u32[]{:S(2)}) collective-permute-start(bf16[32,6144]{1,0:T(8,128)(2,1)S(1)} %get-tuple-element.36), channel_id=1, source_target_pairs={{0,1},{1,0},{2,3},{3,2},{4,5},{5,4},{6,7},{7,6},{8,9},{9,8},{10,11... | collective-permute-start | bytes 1179656 | tf_op jit(solution)/shard_map/ppermute | solution.py:27
  2.5 8.3 %collective-permute-start.1 = (bf16[32,6144]{1,0:T(8,128)(2,1)S(1)}, bf16[32,6144]{1,0:T(8,128)(2,1)S(1)}, u32[]{:S(2)}, u32[]{:S(2)}) collective-permute-start(bf16[32,6144]{1,0:T(8,128)(2,1)S(1)} %get-tuple-element.35.refs_0_), channel_id=1, source_target_pairs={{0,4},{5,1},{4,8},{9,5},{8,12},{13,9},{12,14},{15,13},{14,10},{11,... | collective-permute-start | bytes 1179656 | tf_op jit(solution)/shard_map/ppermute | solution.py:286
  5.1 11.0 %collective-permute-start.2 = (bf16[32,6144]{1,0:T(8,128)(2,1)S(1)}, bf16[32,6144]{1,0:T(8,128)(2,1)S(1)}, u32[]{:S(2)}, u32[]{:S(2)}) collective-permute-start(bf16[32,6144]{1,0:T(8,128)(2,1)S(1)} %collective-permute-done.refs_1_), channel_id=1, source_target_pairs={{0,4},{5,1},{4,8},{9,5},{8,12},{13,9},{12,14},{15,13},{14,10},{11,... | collective-permute-start | bytes 1179656 | tf_op jit(solution)/shard_map/ppermute | solution.py:286
  10.8 8.4 %collective-permute-start.3 = (bf16[32,6144]{1,0:T(8,128)(2,1)S(1)}, bf16[32,6144]{1,0:T(8,128)(2,1)S(1)}, u32[]{:S(2)}, u32[]{:S(2)}) collective-permute-start(bf16[32,6144]{1,0:T(8,128)(2,1)S(1)} %collective-permute-done.1.refs_2_), channel_id=1, source_target_pairs={{0,4},{5,1},{4,8},{9,5},{8,12},{13,9},{12,14},{15,13},{14,10},{11,... | collective-permute-start | bytes 1179656 | tf_op jit(solution)/shard_map/ppermute | solution.py:286
  16.2 8.5 %collective-permute-start.4 = (bf16[32,6144]{1,0:T(8,128)(2,1)S(1)}, bf16[32,6144]{1,0:T(8,128)(2,1)S(1)}, u32[]{:S(2)}, u32[]{:S(2)}) collective-permute-start(bf16[32,6144]{1,0:T(8,128)(2,1)S(1)} %collective-permute-done.2.refs_3_), channel_id=1, source_target_pairs={{0,4},{5,1},{4,8},{9,5},{8,12},{13,9},{12,14},{15,13},{14,10},{11,... | collective-permute-start | bytes 1179656 | tf_op jit(solution)/shard_map/ppermute | solution.py:286
  19.3 9.0 %collective-permute-start.5 = (bf16[32,6144]{1,0:T(8,128)(2,1)S(1)}, bf16[32,6144]{1,0:T(8,128)(2,1)S(1)}, u32[]{:S(2)}, u32[]{:S(2)}) collective-permute-start(bf16[32,6144]{1,0:T(8,128)(2,1)S(1)} %collective-permute-done.3.refs_4_), channel_id=1, source_target_pairs={{0,4},{5,1},{4,8},{9,5},{8,12},{13,9},{12,14},{15,13},{14,10},{11,... | collective-permute-start | bytes 1179656 | tf_op jit(solution)/shard_map/ppermute | solution.py:286
  24.7 12.1 %collective-permute-start.6 = (bf16[32,6144]{1,0:T(8,128)(2,1)S(1)}, bf16[32,6144]{1,0:T(8,128)(2,1)S(1)}, u32[]{:S(2)}, u32[]{:S(2)}) collective-permute-start(bf16[32,6144]{1,0:T(8,128)(2,1)S(1)} %collective-permute-done.4.refs_5_), channel_id=1, source_target_pairs={{0,4},{5,1},{4,8},{9,5},{8,12},{13,9},{12,14},{15,13},{14,10},{11,... | collective-permute-start | bytes 1179656 | tf_op jit(solution)/shard_map/ppermute | solution.py:286
  28.2 8.5 %collective-permute-start.8 = (bf16[32,6144]{1,0:T(8,128)(2,1)S(1)}, bf16[32,6144]{1,0:T(8,128)(2,1)S(1)}, u32[]{:S(2)}, u32[]{:S(2)}) collective-permute-start(bf16[32,6144]{1,0:T(8,128)(2,1)S(1)} %collective-permute-done.5.refs_6_), channel_id=1, source_target_pairs={{0,4},{5,1},{4,8},{9,5},{8,12},{13,9},{12,14},{15,13},{14,10},{11,... | collective-permute-start | bytes 1179656 | tf_op jit(solution)/shard_map/ppermute | solution.py:286
  29.8 7.0 %collective-permute-start.7 = (bf16[64,6144]{1,0:T(8,128)(2,1)S(1)}, bf16[64,6144]{1,0:T(8,128)(2,1)S(1)}, u32[]{:S(2)}, u32[]{:S(2)}) collective-permute-start(bf16[64,6144]{1,0:T(8,128)(2,1)S(1)} %pad_maximum_fusion), channel_id=1, source_target_pairs={{0,1},{1,0},{2,3},{3,2},{4,5},{5,4},{6,7},{7,6},{8,9},{9,8},{10,11... | collective-permute-start | bytes 2359304 | tf_op jit(solution)/shard_map/ppermute | solution.py:27
  36.8 2.1 %collective-permute-start.9 = (bf16[48,6144]{1,0:T(8,128)(2,1)S(1)}, bf16[48,6144]{1,0:T(8,128)(2,1)S(1)}, u32[]{:S(2)}, u32[]{:S(2)}) collective-permute-start(bf16[48,6144]{1,0:T(8,128)(2,1)S(1)} %pad_maximum_fusion.1), channel_id=1, source_target_pairs={{0,1},{1,0},{2,3},{3,2},{4,5},{5,4},{6,7},{7,6},{8,9},{9,8},{10,11... | collective-permute-start | bytes 1769480 | tf_op jit(solution)/shard_map/ppermute | solution.py:27
  38.9 4.9 %slice-start = ((s8[12582912]{0:T(1024)(128)(4,1)}), s8[4194304]{0:T(1024)(128)(4,1)S(1)}, s32[]{:S(2)}) async-start(s8[12582912]{0:T(1024)(128)(4,1)} %bitcast.15), calls=%async_computation | async-start | bytes 8388608
  38.9 4.9 %slice-start.1 = ((s8[12582912]{0:T(1024)(128)(4,1)}), s8[4194304]{0:T(1024)(128)(4,1)S(1)}, s32[]{:S(2)}) async-start(s8[12582912]{0:T(1024)(128)(4,1)} %bitcast.15), calls=%async_computation.1 | async-start | bytes 8388608
  38.9 4.9 %slice-start.2 = ((s8[12582912]{0:T(1024)(128)(4,1)}), s8[4194304]{0:T(1024)(128)(4,1)S(1)}, s32[]{:S(2)}) async-start(s8[12582912]{0:T(1024)(128)(4,1)} %bitcast.15), calls=%async_computation.2 | async-start | bytes 8388608
  46.0 2.3 %collective-permute-start.12 = (bf16[32,6144]{1,0:T(8,128)(2,1)S(1)}, bf16[32,6144]{1,0:T(8,128)(2,1)S(1)}, u32[]{:S(2)}, u32[]{:S(2)}) collective-permute-start(bf16[32,6144]{1,0:T(8,128)(2,1)S(1)} %slice.167), channel_id=1, source_target_pairs={{0,1},{1,0},{2,3},{3,2},{4,5},{5,4},{6,7},{7,6},{8,9},{9,8},{10,11... | collective-permute-start | bytes 1179656 | tf_op jit(solution)/shard_map/ppermute | solution.py:27
  46.3 6.8 %collective-permute-start.11 = (bf16[16,6144]{1,0:T(8,128)(2,1)S(1)}, bf16[16,6144]{1,0:T(8,128)(2,1)S(1)}, u32[]{:S(2)}, u32[]{:S(2)}) collective-permute-start(bf16[16,6144]{1,0:T(8,128)(2,1)S(1)} %get-tuple-element.72), channel_id=1, source_target_pairs={{1,4},{4,1},{5,8},{8,5},{9,12},{12,9},{13,14},{14,13},{15,10},{10,... | collective-permute-start | bytes 589832 | tf_op jit(solution)/shard_map/ppermute | solution.py:286
  47.7 5.8 %collective-permute-start.10 = (bf16[16,6144]{1,0:T(8,128)(2,1)S(1)}, bf16[16,6144]{1,0:T(8,128)(2,1)S(1)}, u32[]{:S(2)}, u32[]{:S(2)}) collective-permute-start(bf16[16,6144]{1,0:T(8,128)(2,1)S(1)} %get-tuple-element.73), channel_id=1, source_target_pairs={{0,4},{5,1},{4,8},{9,5},{8,12},{13,9},{12,14},{15,13},{14,10},{11,... | collective-permute-start | bytes 589832 | tf_op jit(solution)/shard_map/ppermute | solution.py:286
  48.4 9.3 %collective-permute-start.17 = (bf16[32,6144]{1,0:T(8,128)(2,1)S(1)}, bf16[32,6144]{1,0:T(8,128)(2,1)S(1)}, u32[]{:S(2)}, u32[]{:S(2)}) collective-permute-start(bf16[32,6144]{1,0:T(8,128)(2,1)S(1)} %pad_maximum_fusion.2), channel_id=1, source_target_pairs={{0,4},{5,1},{4,8},{9,5},{8,12},{13,9},{12,14},{15,13},{14,10},{11,... | collective-permute-start | bytes 1179656 | tf_op jit(solution)/shard_map/ppermute | solution.py:286
  53.6 8.3 %collective-permute-start.14 = (bf16[32,6144]{1,0:T(8,128)(2,1)S(1)}, bf16[32,6144]{1,0:T(8,128)(2,1)S(1)}, u32[]{:S(2)}, u32[]{:S(2)}) collective-permute-start(bf16[32,6144]{1,0:T(8,128)(2,1)S(1)} %add_convert_fusion.4), channel_id=1, source_target_pairs={{0,4},{5,1},{4,8},{9,5},{8,12},{13,9},{12,14},{15,13},{14,10},{11,... | collective-permute-start | bytes 1179656 | tf_op jit(solution)/shard_map/ppermute | solution.py:286
  55.3 2.4 %collective-permute-start.13 = (bf16[64,6144]{1,0:T(8,128)(2,1)S(1)}, bf16[64,6144]{1,0:T(8,128)(2,1)S(1)}, u32[]{:S(2)}, u32[]{:S(2)}) collective-permute-start(bf16[64,6144]{1,0:T(8,128)(2,1)S(1)} %slice.145), channel_id=1, source_target_pairs={{0,1},{1,0},{2,3},{3,2},{4,5},{5,4},{6,7},{7,6},{8,9},{9,8},{10,11... | collective-permute-start | bytes 2359304 | tf_op jit(solution)/shard_map/ppermute | solution.py:27
  57.8 8.3 %collective-permute-start.18 = (bf16[32,6144]{1,0:T(8,128)(2,1)S(1)}, bf16[32,6144]{1,0:T(8,128)(2,1)S(1)}, u32[]{:S(2)}, u32[]{:S(2)}) collective-permute-start(bf16[32,6144]{1,0:T(8,128)(2,1)S(1)} %add_convert_fusion.1), channel_id=1, source_target_pairs={{0,4},{5,1},{4,8},{9,5},{8,12},{13,9},{12,14},{15,13},{14,10},{11,... | collective-permute-start | bytes 1179656 | tf_op jit(solution)/shard_map/ppermute | solution.py:286
  62.0 8.3 %collective-permute-start.15 = (bf16[32,6144]{1,0:T(8,128)(2,1)S(1)}, bf16[32,6144]{1,0:T(8,128)(2,1)S(1)}, u32[]{:S(2)}, u32[]{:S(2)}) collective-permute-start(bf16[32,6144]{1,0:T(8,128)(2,1)S(1)} %add_convert_fusion.3), channel_id=1, source_target_pairs={{0,4},{5,1},{4,8},{9,5},{8,12},{13,9},{12,14},{15,13},{14,10},{11,... | collective-permute-start | bytes 1179656 | tf_op jit(solution)/shard_map/ppermute | solution.py:286
  66.3 8.3 %collective-permute-start.19 = (bf16[32,6144]{1,0:T(8,128)(2,1)S(1)}, bf16[32,6144]{1,0:T(8,128)(2,1)S(1)}, u32[]{:S(2)}, u32[]{:S(2)}) collective-permute-start(bf16[32,6144]{1,0:T(8,128)(2,1)S(1)} %add_convert_fusion), channel_id=1, source_target_pairs={{0,4},{5,1},{4,8},{9,5},{8,12},{13,9},{12,14},{15,13},{14,10},{11,... | collective-permute-start | bytes 1179656 | tf_op jit(solution)/shard_map/ppermute | solution.py:286
  70.5 8.3 %collective-permute-start.16 = (bf16[32,6144]{1,0:T(8,128)(2,1)S(1)}, bf16[32,6144]{1,0:T(8,128)(2,1)S(1)}, u32[]{:S(2)}, u32[]{:S(2)}) collective-permute-start(bf16[32,6144]{1,0:T(8,128)(2,1)S(1)} %add_convert_fusion.2), channel_id=1, source_target_pairs={{0,4},{5,1},{4,8},{9,5},{8,12},{13,9},{12,14},{15,13},{14,10},{11,... | collective-permute-start | bytes 1179656 | tf_op jit(solution)/shard_map/ppermute | solution.py:286
  74.7 4.1 %collective-permute-start.20 = (bf16[32,6144]{1,0:T(8,128)(2,1)S(1)}, bf16[32,6144]{1,0:T(8,128)(2,1)S(1)}, u32[]{:S(2)}, u32[]{:S(2)}) collective-permute-start(bf16[32,6144]{1,0:T(8,128)(2,1)S(1)} %pad_maximum_fusion.3), channel_id=1, source_target_pairs={{0,1},{1,0},{2,3},{3,2},{4,5},{5,4},{6,7},{7,6},{8,9},{9,8},{10,11... | collective-permute-start | bytes 1179656 | tf_op jit(solution)/shard_map/ppermute | solution.py:27

commit v6 on v5

--- a/solution.py
+++ b/solution.py
@@ -135,7 +135,7 @@
 def hold_and_multiply(rows, weights, begin, depth, before):
     width = weights.shape[1]
     total = sum(c for _, _, c in rows)
-    step = tile_of(depth, 768)
+    step = tile_of(depth, 384)
     pieces = depth // step
     before = [] if before is None else [before]
 
@@ -288,7 +288,7 @@
     own, turned, mixer = dispatch(me, expert_ids, route_weights, tokens)
     units = [own, swap(turned)]
     arriving = [hop(units[0]), hop(units[1])]
-    plan = [(0, 0, 4, 2, 3, 3), (0, 4, 8, 3, 3, 5), (1, 0, 8, 5, 6, 8)] if ept_count == 8 else []
+    plan = [(0, 0, 3, 2, 3, 3), (0, 3, 6, 3, 3, 4), (0, 6, 8, 4, 3, 5), (1, 0, 3, 5, 6, 6), (1, 3, 8, 6, 6, 8)] if ept_count == 8 else []
     weights, held_weights, sums, todo = [w_up, w_gate], [[], []], [None, None], []
     given = [None]
     while len(units) < 2 * reach + 1:
@@ -314,13 +314,14 @@
                 todo.append((i, before))
         if len(units) == 2 * reach - 2:
             given = [swap(jnp.concatenate([u[CAP:] for u in units[2:]], axis=0))]
-    far = swap(jnp.concatenate([u[CAP:] for u in units[-3:]], axis=0))
+    given.append(swap(jnp.concatenate([u[CAP:] for u in units[-3:-1]], axis=0)))
+    far = swap(units[-1][CAP:])
     ups, gates = (h if h else [w] for h, w in zip(held_weights, weights))
     up_done, gate_done = sums
 
     rows = [(u, 0, CAP) for u in units[:-1]]
-    rows += [(given[0], BLOCK * k, BLOCK) for k in range(reach - 2)] + [(far, 0, BLOCK)]
-    rows += [(units[-1], 0, CAP), (far, BLOCK, CAP)]
+    rows += [(given[0], BLOCK * k, BLOCK) for k in range(reach - 2)] + [(given[1], 0, BLOCK)]
+    rows += [(units[-1], 0, CAP), (far, 0, CAP)]
     groups = [[]]
     for row in rows:
         if sum(c for _, _, c in groups[-1]) + row[2] > ROWS:

time: 80.5 us -> 79.8 us (level)
  waiting for transfers between devices: 27.4 us -> 23.8 us
  Pallas kernels: 19.9 us -> 22.1 us
    ppermute x15, waiting for transfers between devices: 23.4 us -> 20.3 us  [hop(): return lax.ppermute(value, ('ept', 'exp'), pairs)]
    pallas_call x4 -> x6, Pallas kernels: 16.5 us -> 18.7 us  [call(): pl.pallas_call(kernel, in_specs=[pl.BlockSpec(memory_space=m) for _, m in...]
    ppermute x6 -> x7, waiting for transfers between devices: 3.97 us -> 3.51 us  [swap(): return lax.ppermute(value, 'exp', [(0, 1), (1, 0)])]
    ppermute x6 -> x7, starting transfers between devices: 1.89 us -> 1.85 us  [swap(): return lax.ppermute(value, 'exp', [(0, 1), (1, 0)])]
  transfers between devices with their start and end apart: 21 -> 22, of which waited for: 13 -> 13; matrix products, arithmetic and copies ran while one was open for 4% -> 4% of each run, Pallas kernels for 14% -> 17%
where the time goes in v6:
time: 79.8 us; the launch traced here: 79.6 us
  starting transfers between devices  27.8 us (35%)
  waiting for transfers between devices  23.8 us (30%)
  Pallas kernels  22.1 us (28%)
  matrix products  4.34 us (5%)
    ppermute x15, starting transfers between devices, hop(): return lax.ppermute(value, ('ept', 'exp'), pairs)  25.9 us
    ppermute x15, waiting for transfers between devices, hop(): return lax.ppermute(value, ('ept', 'exp'), pairs)  20.3 us
    pallas_call x6, Pallas kernels, call(): pl.pallas_call(kernel, in_specs=[pl.BlockSpec(memory_space=m) for _, m in...  18.7 us
    dot_general x2, matrix products, product_of(): jnp.dot(jnp.concatenate(parts, axis=0), w_down, preferred_element_type=jn...  4.34 us
    ppermute x7, waiting for transfers between devices, swap(): return lax.ppermute(value, 'exp', [(0, 1), (1, 0)])  3.51 us
    pallas_call x1, Pallas kernels, dispatch(): pl.pallas_call(dispatch_kernel, grid_spec=pltpu.PrefetchScalarGridSpec(nu...  1.97 us
    ppermute x7, starting transfers between devices, swap(): return lax.ppermute(value, 'exp', [(0, 1), (1, 0)])  1.85 us
  transfers between devices with their start and end apart: 22, of which 13 were waited for; matrix products, arithmetic and copies ran while one was open for 4% of the time, Pallas kernels for 17%

profile of v6, /device:TPU:0, one launch (start us, length us, event | category | flops | bytes accessed | tf_op | source)
XLA Modules:
  0.0 79.6 jit_solution(15145785484130189898)
XLA Ops:
  0.0 2.0 %dispatch.1 = (bf16[32,6144]{1,0:T(8,128)(2,1)S(1)}, bf16[32,6144]{1,0:T(8,128)(2,1)S(1)}, bf16[128,128]{1,0:T(8,128)(2,1)S(1)}) custom-call(s32[1]{0:T(128)} %bitcast.me_ref, s32[2,128]{1,0:T(2,128)} %bitcast.22, f32[2,128]{1,0:T(2,128)} %bitcast.23, bf16[128,6144]{1,0:T(8,128)(2,1)} %tokens_ref.1), custom_call_target="tpu_custom_call" | custom-call | tf_op jit(solution)/shard_map/dispatch/pallas_call | solution.py:73
  2.5 2.6 %collective-permute-start.1 = (bf16[32,6144]{1,0:T(8,128)(2,1)S(1)}, bf16[32,6144]{1,0:T(8,128)(2,1)S(1)}, u32[]{:S(2)}, u32[]{:S(2)}) collective-permute-start(bf16[32,6144]{1,0:T(8,128)(2,1)S(1)} %get-tuple-element.49.refs_0_), channel_id=1, source_target_pairs={{0,4},{5,1},{4,8},{9,5},{8,12},{13,9},{12,14},{15,13},{14,10},{11,... | collective-permute-start | bytes 1179656 | tf_op jit(solution)/shard_map/ppermute | solution.py:286
  5.1 1.7 %collective-permute-start.2 = (bf16[32,6144]{1,0:T(8,128)(2,1)S(1)}, bf16[32,6144]{1,0:T(8,128)(2,1)S(1)}, u32[]{:S(2)}, u32[]{:S(2)}) collective-permute-start(bf16[32,6144]{1,0:T(8,128)(2,1)S(1)} %collective-permute-done.refs_1_), channel_id=1, source_target_pairs={{0,4},{5,1},{4,8},{9,5},{8,12},{13,9},{12,14},{15,13},{14,10},{11,... | collective-permute-start | bytes 1179656 | tf_op jit(solution)/shard_map/ppermute | solution.py:286
  6.8 4.0 %collective-permute-done.1.refs_2_ = bf16[32,6144]{1,0:T(8,128)(2,1)S(1)} collective-permute-done((bf16[32,6144]{1,0:T(8,128)(2,1)S(1)}, bf16[32,6144]{1,0:T(8,128)(2,1)S(1)}, u32[]{:S(2)}, u32[]{:S(2)}) %collective-permute-start.1) | collective-permute-done | bytes 393248 | tf_op jit(solution)/shard_map/ppermute | solution.py:286
  10.8 2.1 %collective-permute-start.3 = (bf16[32,6144]{1,0:T(8,128)(2,1)S(1)}, bf16[32,6144]{1,0:T(8,128)(2,1)S(1)}, u32[]{:S(2)}, u32[]{:S(2)}) collective-permute-start(bf16[32,6144]{1,0:T(8,128)(2,1)S(1)} %collective-permute-done.1.refs_2_), channel_id=1, source_target_pairs={{0,4},{5,1},{4,8},{9,5},{8,12},{13,9},{12,14},{15,13},{14,10},{11,... | collective-permute-start | bytes 1179656 | tf_op jit(solution)/shard_map/ppermute | solution.py:286
  12.9 2.6 %hold_and_multiply.5 = (bf16[2304,1024]{1,0:T(8,128)(2,1)S(1)}, f32[48,1024]{1,0:T(8,128)S(1)}) custom-call(bf16[32,6144]{1,0:T(8,128)(2,1)S(1)} %get-tuple-element.49.refs_0_, bf16[32,6144]{1,0:T(8,128)(2,1)S(1)} %collective-permute-done.refs_1_, bf16[32,6144]{1,0:T(8,128)(2,1)S(1)} %collective-permute-done.1.refs_2_, bf16[6144,1024]{1,0:T(8,128)(2,1)} %bitcast.15), custom_call_target="tpu_custom_call" | custom-call | flops 226492416 | bytes 4718592 | tf_op jit(solution)/shard_map/hold_and_multiply/pallas_call | solution.py:101
  15.5 1.6 %collective-permute-start.4 = (bf16[32,6144]{1,0:T(8,128)(2,1)S(1)}, bf16[32,6144]{1,0:T(8,128)(2,1)S(1)}, u32[]{:S(2)}, u32[]{:S(2)}) collective-permute-start(bf16[32,6144]{1,0:T(8,128)(2,1)S(1)} %collective-permute-done.2.refs_3_), channel_id=1, source_target_pairs={{0,4},{5,1},{4,8},{9,5},{8,12},{13,9},{12,14},{15,13},{14,10},{11,... | collective-permute-start | bytes 1179656 | tf_op jit(solution)/shard_map/ppermute | solution.py:286
  17.2 2.6 %hold_and_multiply.6 = (bf16[2304,1024]{1,0:T(8,128)(2,1)S(1)}, f32[48,1024]{1,0:T(8,128)S(1)}) custom-call(bf16[32,6144]{1,0:T(8,128)(2,1)S(1)} %get-tuple-element.49.refs_0_, bf16[32,6144]{1,0:T(8,128)(2,1)S(1)} %collective-permute-done.refs_1_, bf16[32,6144]{1,0:T(8,128)(2,1)S(1)} %collective-permute-done.1.refs_2_, bf16[6144,1024]{1,0:T(8,128)(2,1)} %bitcast.16, ...), custom_call_target="tpu_custom_call" | custom-call | flops 226492416 | bytes 4718592 | tf_op jit(solution)/shard_map/hold_and_multiply/pallas_call | solution.py:101
  19.8 1.6 %collective-permute-start.5 = (bf16[32,6144]{1,0:T(8,128)(2,1)S(1)}, bf16[32,6144]{1,0:T(8,128)(2,1)S(1)}, u32[]{:S(2)}, u32[]{:S(2)}) collective-permute-start(bf16[32,6144]{1,0:T(8,128)(2,1)S(1)} %collective-permute-done.3.refs_4_), channel_id=1, source_target_pairs={{0,4},{5,1},{4,8},{9,5},{8,12},{13,9},{12,14},{15,13},{14,10},{11,... | collective-permute-start | bytes 1179656 | tf_op jit(solution)/shard_map/ppermute | solution.py:286
  21.5 2.1 %hold_and_multiply.7 = (bf16[1536,1024]{1,0:T(8,128)(2,1)S(1)}, f32[48,1024]{1,0:T(8,128)S(1)}) custom-call(bf16[32,6144]{1,0:T(8,128)(2,1)S(1)} %get-tuple-element.49.refs_0_, bf16[32,6144]{1,0:T(8,128)(2,1)S(1)} %collective-permute-done.refs_1_, bf16[32,6144]{1,0:T(8,128)(2,1)S(1)} %collective-permute-done.1.refs_2_, bf16[6144,1024]{1,0:T(8,128)(2,1)} %bitcast.17, ...), custom_call_target="tpu_custom_call" | custom-call | flops 150994944 | bytes 3145728 | tf_op jit(solution)/shard_map/hold_and_multiply/pallas_call | solution.py:101
  23.7 1.9 %collective-permute-start.6 = (bf16[32,6144]{1,0:T(8,128)(2,1)S(1)}, bf16[32,6144]{1,0:T(8,128)(2,1)S(1)}, u32[]{:S(2)}, u32[]{:S(2)}) collective-permute-start(bf16[32,6144]{1,0:T(8,128)(2,1)S(1)} %collective-permute-done.4.refs_5_), channel_id=1, source_target_pairs={{0,4},{5,1},{4,8},{9,5},{8,12},{13,9},{12,14},{15,13},{14,10},{11,... | collective-permute-start | bytes 1179656 | tf_op jit(solution)/shard_map/ppermute | solution.py:286
  25.6 2.7 %hold_and_multiply.8 = (bf16[2304,1024]{1,0:T(8,128)(2,1)S(1)}, f32[96,1024]{1,0:T(8,128)S(1)}) custom-call(bf16[32,6144]{1,0:T(8,128)(2,1)S(1)} %get-tuple-element.49.refs_0_, bf16[32,6144]{1,0:T(8,128)(2,1)S(1)} %collective-permute-done.refs_1_, bf16[32,6144]{1,0:T(8,128)(2,1)S(1)} %collective-permute-done.1.refs_2_, ...), custom_call_target="tpu_custom_call" | custom-call | flops 452984832 | bytes 4718592 | tf_op jit(solution)/shard_map/hold_and_multiply/pallas_call | solution.py:101
  28.2 1.6 %collective-permute-start.9 = (bf16[32,6144]{1,0:T(8,128)(2,1)S(1)}, bf16[32,6144]{1,0:T(8,128)(2,1)S(1)}, u32[]{:S(2)}, u32[]{:S(2)}) collective-permute-start(bf16[32,6144]{1,0:T(8,128)(2,1)S(1)} %collective-permute-done.5.refs_6_), channel_id=1, source_target_pairs={{0,4},{5,1},{4,8},{9,5},{8,12},{13,9},{12,14},{15,13},{14,10},{11,... | collective-permute-start | bytes 1179656 | tf_op jit(solution)/shard_map/ppermute | solution.py:286
  30.0 1.9 %collective-permute-done.6.refs_7_ = bf16[32,6144]{1,0:T(8,128)(2,1)S(1)} collective-permute-done((bf16[32,6144]{1,0:T(8,128)(2,1)S(1)}, bf16[32,6144]{1,0:T(8,128)(2,1)S(1)}, u32[]{:S(2)}, u32[]{:S(2)}) %collective-permute-start.6) | collective-permute-done | bytes 393248 | tf_op jit(solution)/shard_map/ppermute | solution.py:286
  32.3 3.8 %hold_and_multiply.9 = (bf16[3840,1024]{1,0:T(8,128)(2,1)S(1)}, f32[96,1024]{1,0:T(8,128)S(1)}) custom-call(bf16[32,6144]{1,0:T(8,128)(2,1)S(1)} %get-tuple-element.49.refs_0_, bf16[32,6144]{1,0:T(8,128)(2,1)S(1)} %collective-permute-done.refs_1_, bf16[32,6144]{1,0:T(8,128)(2,1)S(1)} %collective-permute-done.1.refs_2_, ...), custom_call_target="tpu_custom_call" | custom-call | flops 754974720 | bytes 7864320 | tf_op jit(solution)/shard_map/hold_and_multiply/pallas_call | solution.py:101
  37.6 4.9 %hidden.1 = bf16[256,1024]{1,0:T(8,128)(2,1)S(1)} custom-call(bf16[32,6144]{1,0:T(8,128)(2,1)S(1)} %get-tuple-element.49.refs_0_, bf16[32,6144]{1,0:T(8,128)(2,1)S(1)} %collective-permute-done.refs_1_, bf16[32,6144]{1,0:T(8,128)(2,1)S(1)} %collective-permute-done.1.refs_2_, bf16[32,6144]{1,0:T(8,128)(2,1)S(1)} %collective-permute-done.2.refs_3_, ...), custom_call_target="tpu_custom_call" | custom-call | flops 6442450944 | bytes 25165824 | tf_op jit(solution)/shard_map/hidden/pallas_call | solution.py:101
  42.6 2.1 %fusion.7 = bf16[96,6144]{1,0:T(8,128)(2,1)S(1)} fusion(bf16[1,1024,6144]{2,1,0:T(8,128)(2,1)S(1)} %bitcast.19, bf16[64,1024]{1,0:T(8,128)(2,1)S(1)} %slice.161, bf16[32,1024]{1,0:T(8,128)(2,1)S(1)} %get-tuple-element.111), kind=kOutput, calls=%fused_computation.5 | convolution fusion | flops 1208942592 | bytes 13959168 | tf_op jit(solution)/shard_map/dot_general | solution.py:337
  45.1 2.0 %collective-permute-start.12 = (bf16[16,6144]{1,0:T(8,128)(2,1)S(1)}, bf16[16,6144]{1,0:T(8,128)(2,1)S(1)}, u32[]{:S(2)}, u32[]{:S(2)}) collective-permute-start(bf16[16,6144]{1,0:T(8,128)(2,1)S(1)} %get-tuple-element.100), channel_id=1, source_target_pairs={{1,4},{4,1},{5,8},{8,5},{9,12},{12,9},{13,14},{14,13},{15,10},{10,... | collective-permute-start | bytes 589832 | tf_op jit(solution)/shard_map/ppermute | solution.py:286
  47.4 2.1 %collective-permute-start.18 = (bf16[32,6144]{1,0:T(8,128)(2,1)S(1)}, bf16[32,6144]{1,0:T(8,128)(2,1)S(1)}, u32[]{:S(2)}, u32[]{:S(2)}) collective-permute-start(bf16[32,6144]{1,0:T(8,128)(2,1)S(1)} %pad_maximum_fusion.2), channel_id=1, source_target_pairs={{0,4},{5,1},{4,8},{9,5},{8,12},{13,9},{12,14},{15,13},{14,10},{11,... | collective-permute-start | bytes 1179656 | tf_op jit(solution)/shard_map/ppermute | solution.py:286
  49.5 2.2 %fusion.4 = bf16[160,6144]{1,0:T(8,128)(2,1)S(1)} fusion(bf16[160,1024]{1,0:T(8,128)(2,1)S(1)} %constant_dynamic-update-slice_fusion, bf16[1,1024,6144]{2,1,0:T(8,128)(2,1)S(1)} %bitcast.19), kind=kOutput, calls=%fused_computation.4 | convolution fusion | flops 2014248960 | bytes 14876672 | tf_op jit(solution)/shard_map/dot_general | solution.py:337
  52.9 1.7 %collective-permute-start.15 = (bf16[32,6144]{1,0:T(8,128)(2,1)S(1)}, bf16[32,6144]{1,0:T(8,128)(2,1)S(1)}, u32[]{:S(2)}, u32[]{:S(2)}) collective-permute-start(bf16[32,6144]{1,0:T(8,128)(2,1)S(1)} %add_convert_fusion.4), channel_id=1, source_target_pairs={{0,4},{5,1},{4,8},{9,5},{8,12},{13,9},{12,14},{15,13},{14,10},{11,... | collective-permute-start | bytes 1179656 | tf_op jit(solution)/shard_map/ppermute | solution.py:286
  55.0 2.0 %collective-permute-done.14 = bf16[64,6144]{1,0:T(8,128)(2,1)S(1)} collective-permute-done((bf16[64,6144]{1,0:T(8,128)(2,1)S(1)}, bf16[64,6144]{1,0:T(8,128)(2,1)S(1)}, u32[]{:S(2)}, u32[]{:S(2)}) %collective-permute-start.14) | collective-permute-done | bytes 786464 | tf_op jit(solution)/shard_map/ppermute | solution.py:27
  57.2 1.6 %collective-permute-start.19 = (bf16[32,6144]{1,0:T(8,128)(2,1)S(1)}, bf16[32,6144]{1,0:T(8,128)(2,1)S(1)}, u32[]{:S(2)}, u32[]{:S(2)}) collective-permute-start(bf16[32,6144]{1,0:T(8,128)(2,1)S(1)} %add_convert_fusion.1), channel_id=1, source_target_pairs={{0,4},{5,1},{4,8},{9,5},{8,12},{13,9},{12,14},{15,13},{14,10},{11,... | collective-permute-start | bytes 1179656 | tf_op jit(solution)/shard_map/ppermute | solution.py:286
  58.8 2.4 %collective-permute-done.15 = bf16[32,6144]{1,0:T(8,128)(2,1)S(1)} collective-permute-done((bf16[32,6144]{1,0:T(8,128)(2,1)S(1)}, bf16[32,6144]{1,0:T(8,128)(2,1)S(1)}, u32[]{:S(2)}, u32[]{:S(2)}) %collective-permute-start.15) | collective-permute-done | bytes 393248 | tf_op jit(solution)/shard_map/ppermute | solution.py:286
  61.3 1.7 %collective-permute-start.16 = (bf16[32,6144]{1,0:T(8,128)(2,1)S(1)}, bf16[32,6144]{1,0:T(8,128)(2,1)S(1)}, u32[]{:S(2)}, u32[]{:S(2)}) collective-permute-start(bf16[32,6144]{1,0:T(8,128)(2,1)S(1)} %add_convert_fusion.3), channel_id=1, source_target_pairs={{0,4},{5,1},{4,8},{9,5},{8,12},{13,9},{12,14},{15,13},{14,10},{11,... | collective-permute-start | bytes 1179656 | tf_op jit(solution)/shard_map/ppermute | solution.py:286
  63.0 2.4 %collective-permute-done.19 = bf16[32,6144]{1,0:T(8,128)(2,1)S(1)} collective-permute-done((bf16[32,6144]{1,0:T(8,128)(2,1)S(1)}, bf16[32,6144]{1,0:T(8,128)(2,1)S(1)}, u32[]{:S(2)}, u32[]{:S(2)}) %collective-permute-start.19) | collective-permute-done | bytes 393248 | tf_op jit(solution)/shard_map/ppermute | solution.py:286
  65.5 1.7 %collective-permute-start.20 = (bf16[32,6144]{1,0:T(8,128)(2,1)S(1)}, bf16[32,6144]{1,0:T(8,128)(2,1)S(1)}, u32[]{:S(2)}, u32[]{:S(2)}) collective-permute-start(bf16[32,6144]{1,0:T(8,128)(2,1)S(1)} %add_convert_fusion), channel_id=1, source_target_pairs={{0,4},{5,1},{4,8},{9,5},{8,12},{13,9},{12,14},{15,13},{14,10},{11,... | collective-permute-start | bytes 1179656 | tf_op jit(solution)/shard_map/ppermute | solution.py:286
  67.2 2.4 %collective-permute-done.16 = bf16[32,6144]{1,0:T(8,128)(2,1)S(1)} collective-permute-done((bf16[32,6144]{1,0:T(8,128)(2,1)S(1)}, bf16[32,6144]{1,0:T(8,128)(2,1)S(1)}, u32[]{:S(2)}, u32[]{:S(2)}) %collective-permute-start.16) | collective-permute-done | bytes 393248 | tf_op jit(solution)/shard_map/ppermute | solution.py:286
  69.7 1.7 %collective-permute-start.17 = (bf16[32,6144]{1,0:T(8,128)(2,1)S(1)}, bf16[32,6144]{1,0:T(8,128)(2,1)S(1)}, u32[]{:S(2)}, u32[]{:S(2)}) collective-permute-start(bf16[32,6144]{1,0:T(8,128)(2,1)S(1)} %add_convert_fusion.2), channel_id=1, source_target_pairs={{0,4},{5,1},{4,8},{9,5},{8,12},{13,9},{12,14},{15,13},{14,10},{11,... | collective-permute-start | bytes 1179656 | tf_op jit(solution)/shard_map/ppermute | solution.py:286
  71.4 2.4 %collective-permute-done.20 = bf16[32,6144]{1,0:T(8,128)(2,1)S(1)} collective-permute-done((bf16[32,6144]{1,0:T(8,128)(2,1)S(1)}, bf16[32,6144]{1,0:T(8,128)(2,1)S(1)}, u32[]{:S(2)}, u32[]{:S(2)}) %collective-permute-start.20) | collective-permute-done | bytes 393248 | tf_op jit(solution)/shard_map/ppermute | solution.py:286
  74.3 3.7 %collective-permute-done.17.arrived_ref = bf16[32,6144]{1,0:T(8,128)(2,1)S(1)} collective-permute-done((bf16[32,6144]{1,0:T(8,128)(2,1)S(1)}, bf16[32,6144]{1,0:T(8,128)(2,1)S(1)}, u32[]{:S(2)}, u32[]{:S(2)}) %collective-permute-start.17) | collective-permute-done | bytes 393248 | tf_op jit(solution)/shard_map/ppermute | solution.py:286
  78.1 1.4 %combine.1 = bf16[128,6144]{1,0:T(8,128)(2,1)} custom-call(bf16[32,6144]{1,0:T(8,128)(2,1)S(1)} %collective-permute-done.17.arrived_ref, bf16[32,6144]{1,0:T(8,128)(2,1)S(1)} %collective-permute-done.21.handed_ref, bf16[16,6144]{1,0:T(8,128)(2,1)S(1)} %get-tuple-element.93.product_ref, bf16[128,128]{1,0:T(8,128)(2,1)S(1)} %get-tuple-element.92.mixer_ref), custom_call_target="tpu_custom_call" | custom-call | tf_op jit(solution)/shard_map/combine/pallas_call | solution.py:260
  (60 shorter events, 5.7 us)
Async XLA Ops:
  2.0 3.2 %collective-permute-start = (bf16[32,6144]{1,0:T(8,128)(2,1)S(1)}, bf16[32,6144]{1,0:T(8,128)(2,1)S(1)}, u32[]{:S(2)}, u32[]{:S(2)}) collective-permute-start(bf16[32,6144]{1,0:T(8,128)(2,1)S(1)} %get-tuple-element.50), channel_id=1, source_target_pairs={{0,1},{1,0},{2,3},{3,2},{4,5},{5,4},{6,7},{7,6},{8,9},{9,8},{10,11... | collective-permute-start | bytes 1179656 | tf_op jit(solution)/shard_map/ppermute | solution.py:27
  2.5 8.3 %collective-permute-start.1 = (bf16[32,6144]{1,0:T(8,128)(2,1)S(1)}, bf16[32,6144]{1,0:T(8,128)(2,1)S(1)}, u32[]{:S(2)}, u32[]{:S(2)}) collective-permute-start(bf16[32,6144]{1,0:T(8,128)(2,1)S(1)} %get-tuple-element.49.refs_0_), channel_id=1, source_target_pairs={{0,4},{5,1},{4,8},{9,5},{8,12},{13,9},{12,14},{15,13},{14,10},{11,... | collective-permute-start | bytes 1179656 | tf_op jit(solution)/shard_map/ppermute | solution.py:286
  5.1 10.4 %collective-permute-start.2 = (bf16[32,6144]{1,0:T(8,128)(2,1)S(1)}, bf16[32,6144]{1,0:T(8,128)(2,1)S(1)}, u32[]{:S(2)}, u32[]{:S(2)}) collective-permute-start(bf16[32,6144]{1,0:T(8,128)(2,1)S(1)} %collective-permute-done.refs_1_), channel_id=1, source_target_pairs={{0,4},{5,1},{4,8},{9,5},{8,12},{13,9},{12,14},{15,13},{14,10},{11,... | collective-permute-start | bytes 1179656 | tf_op jit(solution)/shard_map/ppermute | solution.py:286
  10.8 9.0 %collective-permute-start.3 = (bf16[32,6144]{1,0:T(8,128)(2,1)S(1)}, bf16[32,6144]{1,0:T(8,128)(2,1)S(1)}, u32[]{:S(2)}, u32[]{:S(2)}) collective-permute-start(bf16[32,6144]{1,0:T(8,128)(2,1)S(1)} %collective-permute-done.1.refs_2_), channel_id=1, source_target_pairs={{0,4},{5,1},{4,8},{9,5},{8,12},{13,9},{12,14},{15,13},{14,10},{11,... | collective-permute-start | bytes 1179656 | tf_op jit(solution)/shard_map/ppermute | solution.py:286
  15.5 8.1 %collective-permute-start.4 = (bf16[32,6144]{1,0:T(8,128)(2,1)S(1)}, bf16[32,6144]{1,0:T(8,128)(2,1)S(1)}, u32[]{:S(2)}, u32[]{:S(2)}) collective-permute-start(bf16[32,6144]{1,0:T(8,128)(2,1)S(1)} %collective-permute-done.2.refs_3_), channel_id=1, source_target_pairs={{0,4},{5,1},{4,8},{9,5},{8,12},{13,9},{12,14},{15,13},{14,10},{11,... | collective-permute-start | bytes 1179656 | tf_op jit(solution)/shard_map/ppermute | solution.py:286
  19.8 8.4 %collective-permute-start.5 = (bf16[32,6144]{1,0:T(8,128)(2,1)S(1)}, bf16[32,6144]{1,0:T(8,128)(2,1)S(1)}, u32[]{:S(2)}, u32[]{:S(2)}) collective-permute-start(bf16[32,6144]{1,0:T(8,128)(2,1)S(1)} %collective-permute-done.3.refs_4_), channel_id=1, source_target_pairs={{0,4},{5,1},{4,8},{9,5},{8,12},{13,9},{12,14},{15,13},{14,10},{11,... | collective-permute-start | bytes 1179656 | tf_op jit(solution)/shard_map/ppermute | solution.py:286
  23.7 8.2 %collective-permute-start.6 = (bf16[32,6144]{1,0:T(8,128)(2,1)S(1)}, bf16[32,6144]{1,0:T(8,128)(2,1)S(1)}, u32[]{:S(2)}, u32[]{:S(2)}) collective-permute-start(bf16[32,6144]{1,0:T(8,128)(2,1)S(1)} %collective-permute-done.4.refs_5_), channel_id=1, source_target_pairs={{0,4},{5,1},{4,8},{9,5},{8,12},{13,9},{12,14},{15,13},{14,10},{11,... | collective-permute-start | bytes 1179656 | tf_op jit(solution)/shard_map/ppermute | solution.py:286
  28.2 7.9 %collective-permute-start.9 = (bf16[32,6144]{1,0:T(8,128)(2,1)S(1)}, bf16[32,6144]{1,0:T(8,128)(2,1)S(1)}, u32[]{:S(2)}, u32[]{:S(2)}) collective-permute-start(bf16[32,6144]{1,0:T(8,128)(2,1)S(1)} %collective-permute-done.5.refs_6_), channel_id=1, source_target_pairs={{0,4},{5,1},{4,8},{9,5},{8,12},{13,9},{12,14},{15,13},{14,10},{11,... | collective-permute-start | bytes 1179656 | tf_op jit(solution)/shard_map/ppermute | solution.py:286
  29.9 2.4 %collective-permute-start.7 = (bf16[64,6144]{1,0:T(8,128)(2,1)S(1)}, bf16[64,6144]{1,0:T(8,128)(2,1)S(1)}, u32[]{:S(2)}, u32[]{:S(2)}) collective-permute-start(bf16[64,6144]{1,0:T(8,128)(2,1)S(1)} %pad_maximum_fusion), channel_id=1, source_target_pairs={{0,1},{1,0},{2,3},{3,2},{4,5},{5,4},{6,7},{7,6},{8,9},{9,8},{10,11... | collective-permute-start | bytes 2359304 | tf_op jit(solution)/shard_map/ppermute | solution.py:27
  32.0 4.4 %collective-permute-start.8 = (bf16[32,6144]{1,0:T(8,128)(2,1)S(1)}, bf16[32,6144]{1,0:T(8,128)(2,1)S(1)}, u32[]{:S(2)}, u32[]{:S(2)}) collective-permute-start(bf16[32,6144]{1,0:T(8,128)(2,1)S(1)} %pad_maximum_fusion.1), channel_id=1, source_target_pairs={{0,1},{1,0},{2,3},{3,2},{4,5},{5,4},{6,7},{7,6},{8,9},{9,8},{10,11... | collective-permute-start | bytes 1179656 | tf_op jit(solution)/shard_map/ppermute | solution.py:27
  32.3 10.3 %slice-start = ((s8[12582912]{0:T(1024)(128)(4,1)}), s8[4194304]{0:T(1024)(128)(4,1)S(1)}, s32[]{:S(2)}) async-start(s8[12582912]{0:T(1024)(128)(4,1)} %bitcast.18), calls=%async_computation | async-start | bytes 8388608
  36.1 1.5 %collective-permute-start.10 = (bf16[16,6144]{1,0:T(8,128)(2,1)S(1)}, bf16[16,6144]{1,0:T(8,128)(2,1)S(1)}, u32[]{:S(2)}, u32[]{:S(2)}) collective-permute-start(bf16[16,6144]{1,0:T(8,128)(2,1)S(1)} %slice.131), channel_id=1, source_target_pairs={{0,1},{1,0},{2,3},{3,2},{4,5},{5,4},{6,7},{7,6},{8,9},{9,8},{10,11... | collective-permute-start | bytes 589832 | tf_op jit(solution)/shard_map/ppermute | solution.py:27
  37.6 5.0 %slice-start.1 = ((s8[12582912]{0:T(1024)(128)(4,1)}), s8[4194304]{0:T(1024)(128)(4,1)S(1)}, s32[]{:S(2)}) async-start(s8[12582912]{0:T(1024)(128)(4,1)} %bitcast.18), calls=%async_computation.1 | async-start | bytes 8388608
  37.6 5.0 %slice-start.2 = ((s8[12582912]{0:T(1024)(128)(4,1)}), s8[4194304]{0:T(1024)(128)(4,1)S(1)}, s32[]{:S(2)}) async-start(s8[12582912]{0:T(1024)(128)(4,1)} %bitcast.18), calls=%async_computation.2 | async-start | bytes 8388608
  44.8 2.5 %collective-permute-start.13 = (bf16[32,6144]{1,0:T(8,128)(2,1)S(1)}, bf16[32,6144]{1,0:T(8,128)(2,1)S(1)}, u32[]{:S(2)}, u32[]{:S(2)}) collective-permute-start(bf16[32,6144]{1,0:T(8,128)(2,1)S(1)} %slice.165), channel_id=1, source_target_pairs={{0,1},{1,0},{2,3},{3,2},{4,5},{5,4},{6,7},{7,6},{8,9},{9,8},{10,11... | collective-permute-start | bytes 1179656 | tf_op jit(solution)/shard_map/ppermute | solution.py:27
  45.1 7.2 %collective-permute-start.12 = (bf16[16,6144]{1,0:T(8,128)(2,1)S(1)}, bf16[16,6144]{1,0:T(8,128)(2,1)S(1)}, u32[]{:S(2)}, u32[]{:S(2)}) collective-permute-start(bf16[16,6144]{1,0:T(8,128)(2,1)S(1)} %get-tuple-element.100), channel_id=1, source_target_pairs={{1,4},{4,1},{5,8},{8,5},{9,12},{12,9},{13,14},{14,13},{15,10},{10,... | collective-permute-start | bytes 589832 | tf_op jit(solution)/shard_map/ppermute | solution.py:286
  47.1 5.7 %collective-permute-start.11 = (bf16[16,6144]{1,0:T(8,128)(2,1)S(1)}, bf16[16,6144]{1,0:T(8,128)(2,1)S(1)}, u32[]{:S(2)}, u32[]{:S(2)}) collective-permute-start(bf16[16,6144]{1,0:T(8,128)(2,1)S(1)} %get-tuple-element.101), channel_id=1, source_target_pairs={{0,4},{5,1},{4,8},{9,5},{8,12},{13,9},{12,14},{15,13},{14,10},{11,... | collective-permute-start | bytes 589832 | tf_op jit(solution)/shard_map/ppermute | solution.py:286
  47.4 9.7 %collective-permute-start.18 = (bf16[32,6144]{1,0:T(8,128)(2,1)S(1)}, bf16[32,6144]{1,0:T(8,128)(2,1)S(1)}, u32[]{:S(2)}, u32[]{:S(2)}) collective-permute-start(bf16[32,6144]{1,0:T(8,128)(2,1)S(1)} %pad_maximum_fusion.2), channel_id=1, source_target_pairs={{0,4},{5,1},{4,8},{9,5},{8,12},{13,9},{12,14},{15,13},{14,10},{11,... | collective-permute-start | bytes 1179656 | tf_op jit(solution)/shard_map/ppermute | solution.py:286
  52.9 8.3 %collective-permute-start.15 = (bf16[32,6144]{1,0:T(8,128)(2,1)S(1)}, bf16[32,6144]{1,0:T(8,128)(2,1)S(1)}, u32[]{:S(2)}, u32[]{:S(2)}) collective-permute-start(bf16[32,6144]{1,0:T(8,128)(2,1)S(1)} %add_convert_fusion.4), channel_id=1, source_target_pairs={{0,4},{5,1},{4,8},{9,5},{8,12},{13,9},{12,14},{15,13},{14,10},{11,... | collective-permute-start | bytes 1179656 | tf_op jit(solution)/shard_map/ppermute | solution.py:286
  54.6 2.4 %collective-permute-start.14 = (bf16[64,6144]{1,0:T(8,128)(2,1)S(1)}, bf16[64,6144]{1,0:T(8,128)(2,1)S(1)}, u32[]{:S(2)}, u32[]{:S(2)}) collective-permute-start(bf16[64,6144]{1,0:T(8,128)(2,1)S(1)} %slice.145), channel_id=1, source_target_pairs={{0,1},{1,0},{2,3},{3,2},{4,5},{5,4},{6,7},{7,6},{8,9},{9,8},{10,11... | collective-permute-start | bytes 2359304 | tf_op jit(solution)/shard_map/ppermute | solution.py:27
  57.2 8.3 %collective-permute-start.19 = (bf16[32,6144]{1,0:T(8,128)(2,1)S(1)}, bf16[32,6144]{1,0:T(8,128)(2,1)S(1)}, u32[]{:S(2)}, u32[]{:S(2)}) collective-permute-start(bf16[32,6144]{1,0:T(8,128)(2,1)S(1)} %add_convert_fusion.1), channel_id=1, source_target_pairs={{0,4},{5,1},{4,8},{9,5},{8,12},{13,9},{12,14},{15,13},{14,10},{11,... | collective-permute-start | bytes 1179656 | tf_op jit(solution)/shard_map/ppermute | solution.py:286
  61.3 8.3 %collective-permute-start.16 = (bf16[32,6144]{1,0:T(8,128)(2,1)S(1)}, bf16[32,6144]{1,0:T(8,128)(2,1)S(1)}, u32[]{:S(2)}, u32[]{:S(2)}) collective-permute-start(bf16[32,6144]{1,0:T(8,128)(2,1)S(1)} %add_convert_fusion.3), channel_id=1, source_target_pairs={{0,4},{5,1},{4,8},{9,5},{8,12},{13,9},{12,14},{15,13},{14,10},{11,... | collective-permute-start | bytes 1179656 | tf_op jit(solution)/shard_map/ppermute | solution.py:286
  65.5 8.3 %collective-permute-start.20 = (bf16[32,6144]{1,0:T(8,128)(2,1)S(1)}, bf16[32,6144]{1,0:T(8,128)(2,1)S(1)}, u32[]{:S(2)}, u32[]{:S(2)}) collective-permute-start(bf16[32,6144]{1,0:T(8,128)(2,1)S(1)} %add_convert_fusion), channel_id=1, source_target_pairs={{0,4},{5,1},{4,8},{9,5},{8,12},{13,9},{12,14},{15,13},{14,10},{11,... | collective-permute-start | bytes 1179656 | tf_op jit(solution)/shard_map/ppermute | solution.py:286
  69.7 8.3 %collective-permute-start.17 = (bf16[32,6144]{1,0:T(8,128)(2,1)S(1)}, bf16[32,6144]{1,0:T(8,128)(2,1)S(1)}, u32[]{:S(2)}, u32[]{:S(2)}) collective-permute-start(bf16[32,6144]{1,0:T(8,128)(2,1)S(1)} %add_convert_fusion.2), channel_id=1, source_target_pairs={{0,4},{5,1},{4,8},{9,5},{8,12},{13,9},{12,14},{15,13},{14,10},{11,... | collective-permute-start | bytes 1179656 | tf_op jit(solution)/shard_map/ppermute | solution.py:286
  74.0 4.1 %collective-permute-start.21 = (bf16[32,6144]{1,0:T(8,128)(2,1)S(1)}, bf16[32,6144]{1,0:T(8,128)(2,1)S(1)}, u32[]{:S(2)}, u32[]{:S(2)}) collective-permute-start(bf16[32,6144]{1,0:T(8,128)(2,1)S(1)} %pad_maximum_fusion.3), channel_id=1, source_target_pairs={{0,1},{1,0},{2,3},{3,2},{4,5},{5,4},{6,7},{7,6},{8,9},{9,8},{10,11... | collective-permute-start | bytes 1179656 | tf_op jit(solution)/shard_map/ppermute | solution.py:27

commit v7 on v6

--- a/solution.py
+++ b/solution.py
@@ -35,66 +35,69 @@
     return pltpu.with_memory_space_constraint(value, pltpu.HBM)
 
 
-def dispatch_kernel(me_ref, ids_ref, weights_ref, tokens_ref, rows_ref, turned_ref, mixer_ref, picker):
-    @pl.when(pl.program_id(0) == 0)
-    def _():
-        token_count = ids_ref.shape[1]
+def dispatch(me, expert_ids, route_weights, tokens):
+    token_count, width = tokens.shape
+    tile = tile_of(width, 3072)
+    steps = width // tile
+
+    def kernel(me_ref, ids_hbm, weights_hbm, tokens_hbm, rows_ref, turned_ref, mixer_ref, *scratch):
+        ids_ref, weights_ref, held_ref, done = scratch
+        copies = [
+            pltpu.make_async_copy(ids_hbm, ids_ref, done.at[0]),
+            pltpu.make_async_copy(weights_hbm, weights_ref, done.at[1]),
+        ]
+        for i in range(steps):
+            here = pl.ds(i * tile, tile)
+            copies.append(
+                pltpu.make_async_copy(
+                    tokens_hbm.at[:, here], held_ref.at[:, here], done.at[2 + i]
+                )
+            )
+        for copy in copies:
+            copy.start()
         line = lax.broadcasted_iota(jnp.int32, (BLOCK, token_count), 0)
         expert = (line // CAP + me_ref[0]) % 2
+        slot = (line % CAP).astype(jnp.float32)
+        row = lax.broadcasted_iota(jnp.int32, (token_count, token_count), 0)
+        column = lax.broadcasted_iota(jnp.int32, (token_count, token_count), 1)
+        earlier = (row < column).astype(jnp.bfloat16)
+        copies[0].wait()
         first = ids_ref[0:1, :] == expert
         second = ids_ref[1:2, :] == expert
         named = first.astype(jnp.float32) + second.astype(jnp.float32)
-        row = lax.broadcasted_iota(jnp.int32, (token_count, token_count), 0)
-        column = lax.broadcasted_iota(jnp.int32, (token_count, token_count), 1)
-        earlier = (row < column).astype(jnp.bfloat16)
         before = jnp.dot(named.astype(jnp.bfloat16), earlier, preferred_element_type=jnp.float32)
-        slot = (line % CAP).astype(jnp.float32)
         hit_first = jnp.where(first & (before == slot), 1.0, 0.0)
-        after = before + first.astype(jnp.float32)
-        hit_second = jnp.where(second & (after == slot), 1.0, 0.0)
-        picker[...] = (hit_first + hit_second).astype(jnp.bfloat16)
+        after_first = before + first.astype(jnp.float32)
+        hit_second = jnp.where(second & (after_first == slot), 1.0, 0.0)
+        picker = (hit_first + hit_second).astype(jnp.bfloat16)
+        copies[1].wait()
+        for i in range(steps):
+            here = slice(i * tile, (i + 1) * tile)
+            copies[2 + i].wait()
+            rows = jnp.dot(
+                picker, held_ref[:, here], preferred_element_type=jnp.float32
+            ).astype(jnp.bfloat16)
+            rows_ref[:, here] = rows
+            turned_ref[:CAP, here] = rows[CAP:]
+            turned_ref[CAP:, here] = rows[:CAP]
         mixer = hit_first * weights_ref[0:1, :] + hit_second * weights_ref[1:2, :]
         high = mixer.astype(jnp.bfloat16).astype(jnp.float32)
         empty = jnp.zeros((LANES - 2 * BLOCK, token_count), jnp.float32)
         stacked = jnp.concatenate([high, mixer - high, empty], axis=0)
         mixer_ref[...] = stacked.T.astype(jnp.bfloat16)
 
-    rows = jnp.dot(picker[...], tokens_ref[...], preferred_element_type=jnp.float32)
-    rows_ref[...] = rows.astype(jnp.bfloat16)
-    turned_ref[:CAP, :] = rows[CAP:].astype(jnp.bfloat16)
-    turned_ref[CAP:, :] = rows[:CAP].astype(jnp.bfloat16)
-
-
-def dispatch(me, expert_ids, route_weights, tokens):
-    token_count, width = tokens.shape
-    tile = tile_of(width, 3072)
-    whole = lambda j, me: (0, 0)
-    column = lambda j, me: (0, j)
-    return pl.pallas_call(
-        dispatch_kernel,
-        grid_spec=pltpu.PrefetchScalarGridSpec(
-            num_scalar_prefetch=1,
-            grid=(width // tile,),
-            in_specs=[
-                pl.BlockSpec((2, token_count), whole),
-                pl.BlockSpec((2, token_count), whole),
-                pl.BlockSpec((token_count, tile), column),
-            ],
-            out_specs=[
-                pl.BlockSpec((BLOCK, tile), column),
-                pl.BlockSpec((BLOCK, tile), column),
-                pl.BlockSpec((token_count, LANES), whole),
-            ],
-            scratch_shapes=[pltpu.VMEM((BLOCK, token_count), jnp.bfloat16)],
-        ),
-        out_shape=[
-            jax.ShapeDtypeStruct((BLOCK, width), jnp.bfloat16),
-            jax.ShapeDtypeStruct((BLOCK, width), jnp.bfloat16),
-            jax.ShapeDtypeStruct((token_count, LANES), jnp.bfloat16),
+    return call(
+        kernel,
+        "dispatch",
+        [(me, pltpu.SMEM)] + remote(expert_ids.T, route_weights.T, tokens),
+        [array(BLOCK, width), array(BLOCK, width), array(token_count, LANES)],
+        [
+            pltpu.VMEM((2, token_count), expert_ids.dtype),
+            pltpu.VMEM((2, token_count), route_weights.dtype),
+            pltpu.VMEM((token_count, width), tokens.dtype),
+            pltpu.SemaphoreType.DMA((2 + steps,)),
         ],
-        compiler_params=pltpu.CompilerParams(vmem_limit_bytes=VMEM_LIMIT),
-        name="dispatch",
-    )(me, in_hbm(expert_ids.T), in_hbm(route_weights.T), in_hbm(tokens))
+    )
 
 
 def call(kernel, name, operands, outs, scratch=(), flops=0, bytes_accessed=0):

time: 79.8 us -> 79.5 us (level)
    pallas_call x1 -> x0, Pallas kernels: 1.97 us -> none  [dispatch(): pl.pallas_call(dispatch_kernel, grid_spec=pltpu.PrefetchScalarGridSpec(nu...]
    pallas_call x6 -> x7, Pallas kernels: 18.7 us -> 20.4 us  [call(): pl.pallas_call(kernel, in_specs=[pl.BlockSpec(memory_space=m) for _, m in...]
where the time goes in v7:
time: 79.5 us; the launch traced here: 79.4 us
  starting transfers between devices  27.8 us (35%)
  waiting for transfers between devices  23.8 us (30%)
  Pallas kernels  21.8 us (27%)
  matrix products  4.34 us (5%)
    ppermute x15, starting transfers between devices, hop(): return lax.ppermute(value, ('ept', 'exp'), pairs)  25.8 us
    pallas_call x7, Pallas kernels, call(): pl.pallas_call(kernel, in_specs=[pl.BlockSpec(memory_space=m) for _, m in...  20.4 us
    ppermute x15, waiting for transfers between devices, hop(): return lax.ppermute(value, ('ept', 'exp'), pairs)  20.4 us
    dot_general x2, matrix products, product_of(): jnp.dot(jnp.concatenate(parts, axis=0), w_down, preferred_element_type=jn...  4.34 us
    ppermute x7, waiting for transfers between devices, swap(): return lax.ppermute(value, 'exp', [(0, 1), (1, 0)])  3.45 us
    ppermute x7, starting transfers between devices, swap(): return lax.ppermute(value, 'exp', [(0, 1), (1, 0)])  1.94 us
  transfers between devices with their start and end apart: 22, of which 13 were waited for; matrix products, arithmetic and copies ran while one was open for 4% of the time, Pallas kernels for 17%

profile of v7, /device:TPU:0, one launch (start us, length us, event | category | flops | bytes accessed | tf_op | source)
XLA Modules:
  0.0 79.4 jit_solution(7451526932891817214)
XLA Ops:
  0.0 1.7 %dispatch.1 = (bf16[32,6144]{1,0:T(8,128)(2,1)S(1)}, bf16[32,6144]{1,0:T(8,128)(2,1)S(1)}, bf16[128,128]{1,0:T(8,128)(2,1)S(1)}) custom-call(s32[1]{0:T(128)} %bitcast.me_ref, s32[2,128]{1,0:T(2,128)} %bitcast.22, f32[2,128]{1,0:T(2,128)} %bitcast.23, bf16[128,6144]{1,0:T(8,128)(2,1)} %tokens_hbm.1), custom_call_target="tpu_custom_call" | custom-call | tf_op jit(solution)/shard_map/dispatch/pallas_call | solution.py:104
  2.2 2.6 %collective-permute-start.1 = (bf16[32,6144]{1,0:T(8,128)(2,1)S(1)}, bf16[32,6144]{1,0:T(8,128)(2,1)S(1)}, u32[]{:S(2)}, u32[]{:S(2)}) collective-permute-start(bf16[32,6144]{1,0:T(8,128)(2,1)S(1)} %get-tuple-element.49.refs_0_), channel_id=1, source_target_pairs={{0,4},{5,1},{4,8},{9,5},{8,12},{13,9},{12,14},{15,13},{14,10},{11,... | collective-permute-start | bytes 1179656 | tf_op jit(solution)/shard_map/ppermute | solution.py:289
  4.9 1.7 %collective-permute-start.2 = (bf16[32,6144]{1,0:T(8,128)(2,1)S(1)}, bf16[32,6144]{1,0:T(8,128)(2,1)S(1)}, u32[]{:S(2)}, u32[]{:S(2)}) collective-permute-start(bf16[32,6144]{1,0:T(8,128)(2,1)S(1)} %collective-permute-done.refs_1_), channel_id=1, source_target_pairs={{0,4},{5,1},{4,8},{9,5},{8,12},{13,9},{12,14},{15,13},{14,10},{11,... | collective-permute-start | bytes 1179656 | tf_op jit(solution)/shard_map/ppermute | solution.py:289
  6.5 4.0 %collective-permute-done.1.refs_2_ = bf16[32,6144]{1,0:T(8,128)(2,1)S(1)} collective-permute-done((bf16[32,6144]{1,0:T(8,128)(2,1)S(1)}, bf16[32,6144]{1,0:T(8,128)(2,1)S(1)}, u32[]{:S(2)}, u32[]{:S(2)}) %collective-permute-start.1) | collective-permute-done | bytes 393248 | tf_op jit(solution)/shard_map/ppermute | solution.py:289
  10.6 2.1 %collective-permute-start.3 = (bf16[32,6144]{1,0:T(8,128)(2,1)S(1)}, bf16[32,6144]{1,0:T(8,128)(2,1)S(1)}, u32[]{:S(2)}, u32[]{:S(2)}) collective-permute-start(bf16[32,6144]{1,0:T(8,128)(2,1)S(1)} %collective-permute-done.1.refs_2_), channel_id=1, source_target_pairs={{0,4},{5,1},{4,8},{9,5},{8,12},{13,9},{12,14},{15,13},{14,10},{11,... | collective-permute-start | bytes 1179656 | tf_op jit(solution)/shard_map/ppermute | solution.py:289
  12.6 2.6 %hold_and_multiply.5 = (bf16[2304,1024]{1,0:T(8,128)(2,1)S(1)}, f32[48,1024]{1,0:T(8,128)S(1)}) custom-call(bf16[32,6144]{1,0:T(8,128)(2,1)S(1)} %get-tuple-element.49.refs_0_, bf16[32,6144]{1,0:T(8,128)(2,1)S(1)} %collective-permute-done.refs_1_, bf16[32,6144]{1,0:T(8,128)(2,1)S(1)} %collective-permute-done.1.refs_2_, bf16[6144,1024]{1,0:T(8,128)(2,1)} %bitcast.15), custom_call_target="tpu_custom_call" | custom-call | flops 226492416 | bytes 4718592 | tf_op jit(solution)/shard_map/hold_and_multiply/pallas_call | solution.py:104
  15.3 1.6 %collective-permute-start.4 = (bf16[32,6144]{1,0:T(8,128)(2,1)S(1)}, bf16[32,6144]{1,0:T(8,128)(2,1)S(1)}, u32[]{:S(2)}, u32[]{:S(2)}) collective-permute-start(bf16[32,6144]{1,0:T(8,128)(2,1)S(1)} %collective-permute-done.2.refs_3_), channel_id=1, source_target_pairs={{0,4},{5,1},{4,8},{9,5},{8,12},{13,9},{12,14},{15,13},{14,10},{11,... | collective-permute-start | bytes 1179656 | tf_op jit(solution)/shard_map/ppermute | solution.py:289
  16.9 2.6 %hold_and_multiply.6 = (bf16[2304,1024]{1,0:T(8,128)(2,1)S(1)}, f32[48,1024]{1,0:T(8,128)S(1)}) custom-call(bf16[32,6144]{1,0:T(8,128)(2,1)S(1)} %get-tuple-element.49.refs_0_, bf16[32,6144]{1,0:T(8,128)(2,1)S(1)} %collective-permute-done.refs_1_, bf16[32,6144]{1,0:T(8,128)(2,1)S(1)} %collective-permute-done.1.refs_2_, bf16[6144,1024]{1,0:T(8,128)(2,1)} %bitcast.16, ...), custom_call_target="tpu_custom_call" | custom-call | flops 226492416 | bytes 4718592 | tf_op jit(solution)/shard_map/hold_and_multiply/pallas_call | solution.py:104
  19.6 1.6 %collective-permute-start.5 = (bf16[32,6144]{1,0:T(8,128)(2,1)S(1)}, bf16[32,6144]{1,0:T(8,128)(2,1)S(1)}, u32[]{:S(2)}, u32[]{:S(2)}) collective-permute-start(bf16[32,6144]{1,0:T(8,128)(2,1)S(1)} %collective-permute-done.3.refs_4_), channel_id=1, source_target_pairs={{0,4},{5,1},{4,8},{9,5},{8,12},{13,9},{12,14},{15,13},{14,10},{11,... | collective-permute-start | bytes 1179656 | tf_op jit(solution)/shard_map/ppermute | solution.py:289
  21.2 2.1 %hold_and_multiply.7 = (bf16[1536,1024]{1,0:T(8,128)(2,1)S(1)}, f32[48,1024]{1,0:T(8,128)S(1)}) custom-call(bf16[32,6144]{1,0:T(8,128)(2,1)S(1)} %get-tuple-element.49.refs_0_, bf16[32,6144]{1,0:T(8,128)(2,1)S(1)} %collective-permute-done.refs_1_, bf16[32,6144]{1,0:T(8,128)(2,1)S(1)} %collective-permute-done.1.refs_2_, bf16[6144,1024]{1,0:T(8,128)(2,1)} %bitcast.17, ...), custom_call_target="tpu_custom_call" | custom-call | flops 150994944 | bytes 3145728 | tf_op jit(solution)/shard_map/hold_and_multiply/pallas_call | solution.py:104
  23.4 1.9 %collective-permute-start.6 = (bf16[32,6144]{1,0:T(8,128)(2,1)S(1)}, bf16[32,6144]{1,0:T(8,128)(2,1)S(1)}, u32[]{:S(2)}, u32[]{:S(2)}) collective-permute-start(bf16[32,6144]{1,0:T(8,128)(2,1)S(1)} %collective-permute-done.4.refs_5_), channel_id=1, source_target_pairs={{0,4},{5,1},{4,8},{9,5},{8,12},{13,9},{12,14},{15,13},{14,10},{11,... | collective-permute-start | bytes 1179656 | tf_op jit(solution)/shard_map/ppermute | solution.py:289
  25.3 2.7 %hold_and_multiply.8 = (bf16[2304,1024]{1,0:T(8,128)(2,1)S(1)}, f32[96,1024]{1,0:T(8,128)S(1)}) custom-call(bf16[32,6144]{1,0:T(8,128)(2,1)S(1)} %get-tuple-element.49.refs_0_, bf16[32,6144]{1,0:T(8,128)(2,1)S(1)} %collective-permute-done.refs_1_, bf16[32,6144]{1,0:T(8,128)(2,1)S(1)} %collective-permute-done.1.refs_2_, ...), custom_call_target="tpu_custom_call" | custom-call | flops 452984832 | bytes 4718592 | tf_op jit(solution)/shard_map/hold_and_multiply/pallas_call | solution.py:104
  28.0 1.6 %collective-permute-start.9 = (bf16[32,6144]{1,0:T(8,128)(2,1)S(1)}, bf16[32,6144]{1,0:T(8,128)(2,1)S(1)}, u32[]{:S(2)}, u32[]{:S(2)}) collective-permute-start(bf16[32,6144]{1,0:T(8,128)(2,1)S(1)} %collective-permute-done.5.refs_6_), channel_id=1, source_target_pairs={{0,4},{5,1},{4,8},{9,5},{8,12},{13,9},{12,14},{15,13},{14,10},{11,... | collective-permute-start | bytes 1179656 | tf_op jit(solution)/shard_map/ppermute | solution.py:289
  29.8 1.9 %collective-permute-done.6.refs_7_ = bf16[32,6144]{1,0:T(8,128)(2,1)S(1)} collective-permute-done((bf16[32,6144]{1,0:T(8,128)(2,1)S(1)}, bf16[32,6144]{1,0:T(8,128)(2,1)S(1)}, u32[]{:S(2)}, u32[]{:S(2)}) %collective-permute-start.6) | collective-permute-done | bytes 393248 | tf_op jit(solution)/shard_map/ppermute | solution.py:289
  32.0 3.8 %hold_and_multiply.9 = (bf16[3840,1024]{1,0:T(8,128)(2,1)S(1)}, f32[96,1024]{1,0:T(8,128)S(1)}) custom-call(bf16[32,6144]{1,0:T(8,128)(2,1)S(1)} %get-tuple-element.49.refs_0_, bf16[32,6144]{1,0:T(8,128)(2,1)S(1)} %collective-permute-done.refs_1_, bf16[32,6144]{1,0:T(8,128)(2,1)S(1)} %collective-permute-done.1.refs_2_, ...), custom_call_target="tpu_custom_call" | custom-call | flops 754974720 | bytes 7864320 | tf_op jit(solution)/shard_map/hold_and_multiply/pallas_call | solution.py:104
  37.4 4.9 %hidden.1 = bf16[256,1024]{1,0:T(8,128)(2,1)S(1)} custom-call(bf16[32,6144]{1,0:T(8,128)(2,1)S(1)} %get-tuple-element.49.refs_0_, bf16[32,6144]{1,0:T(8,128)(2,1)S(1)} %collective-permute-done.refs_1_, bf16[32,6144]{1,0:T(8,128)(2,1)S(1)} %collective-permute-done.1.refs_2_, bf16[32,6144]{1,0:T(8,128)(2,1)S(1)} %collective-permute-done.2.refs_3_, ...), custom_call_target="tpu_custom_call" | custom-call | flops 6442450944 | bytes 25165824 | tf_op jit(solution)/shard_map/hidden/pallas_call | solution.py:104
  42.4 2.1 %fusion.7 = bf16[96,6144]{1,0:T(8,128)(2,1)S(1)} fusion(bf16[1,1024,6144]{2,1,0:T(8,128)(2,1)S(1)} %bitcast.19, bf16[64,1024]{1,0:T(8,128)(2,1)S(1)} %slice.161, bf16[32,1024]{1,0:T(8,128)(2,1)S(1)} %get-tuple-element.111), kind=kOutput, calls=%fused_computation.5 | convolution fusion | flops 1208942592 | bytes 13959168 | tf_op jit(solution)/shard_map/dot_general | solution.py:340
  44.8 2.0 %collective-permute-start.12 = (bf16[16,6144]{1,0:T(8,128)(2,1)S(1)}, bf16[16,6144]{1,0:T(8,128)(2,1)S(1)}, u32[]{:S(2)}, u32[]{:S(2)}) collective-permute-start(bf16[16,6144]{1,0:T(8,128)(2,1)S(1)} %get-tuple-element.100), channel_id=1, source_target_pairs={{1,4},{4,1},{5,8},{8,5},{9,12},{12,9},{13,14},{14,13},{15,10},{10,... | collective-permute-start | bytes 589832 | tf_op jit(solution)/shard_map/ppermute | solution.py:289
  47.3 1.7 %collective-permute-start.18 = (bf16[32,6144]{1,0:T(8,128)(2,1)S(1)}, bf16[32,6144]{1,0:T(8,128)(2,1)S(1)}, u32[]{:S(2)}, u32[]{:S(2)}) collective-permute-start(bf16[32,6144]{1,0:T(8,128)(2,1)S(1)} %pad_maximum_fusion.2), channel_id=1, source_target_pairs={{0,4},{5,1},{4,8},{9,5},{8,12},{13,9},{12,14},{15,13},{14,10},{11,... | collective-permute-start | bytes 1179656 | tf_op jit(solution)/shard_map/ppermute | solution.py:289
  49.1 2.2 %fusion.4 = bf16[160,6144]{1,0:T(8,128)(2,1)S(1)} fusion(bf16[160,1024]{1,0:T(8,128)(2,1)S(1)} %constant_dynamic-update-slice_fusion, bf16[1,1024,6144]{2,1,0:T(8,128)(2,1)S(1)} %bitcast.19), kind=kOutput, calls=%fused_computation.4 | convolution fusion | flops 2014248960 | bytes 14876672 | tf_op jit(solution)/shard_map/dot_general | solution.py:340
  52.6 1.7 %collective-permute-start.15 = (bf16[32,6144]{1,0:T(8,128)(2,1)S(1)}, bf16[32,6144]{1,0:T(8,128)(2,1)S(1)}, u32[]{:S(2)}, u32[]{:S(2)}) collective-permute-start(bf16[32,6144]{1,0:T(8,128)(2,1)S(1)} %add_convert_fusion.4), channel_id=1, source_target_pairs={{0,4},{5,1},{4,8},{9,5},{8,12},{13,9},{12,14},{15,13},{14,10},{11,... | collective-permute-start | bytes 1179656 | tf_op jit(solution)/shard_map/ppermute | solution.py:289
  54.8 2.0 %collective-permute-done.14 = bf16[64,6144]{1,0:T(8,128)(2,1)S(1)} collective-permute-done((bf16[64,6144]{1,0:T(8,128)(2,1)S(1)}, bf16[64,6144]{1,0:T(8,128)(2,1)S(1)}, u32[]{:S(2)}, u32[]{:S(2)}) %collective-permute-start.14) | collective-permute-done | bytes 786464 | tf_op jit(solution)/shard_map/ppermute | solution.py:27
  56.9 1.6 %collective-permute-start.19 = (bf16[32,6144]{1,0:T(8,128)(2,1)S(1)}, bf16[32,6144]{1,0:T(8,128)(2,1)S(1)}, u32[]{:S(2)}, u32[]{:S(2)}) collective-permute-start(bf16[32,6144]{1,0:T(8,128)(2,1)S(1)} %add_convert_fusion.1), channel_id=1, source_target_pairs={{0,4},{5,1},{4,8},{9,5},{8,12},{13,9},{12,14},{15,13},{14,10},{11,... | collective-permute-start | bytes 1179656 | tf_op jit(solution)/shard_map/ppermute | solution.py:289
  58.5 2.4 %collective-permute-done.15 = bf16[32,6144]{1,0:T(8,128)(2,1)S(1)} collective-permute-done((bf16[32,6144]{1,0:T(8,128)(2,1)S(1)}, bf16[32,6144]{1,0:T(8,128)(2,1)S(1)}, u32[]{:S(2)}, u32[]{:S(2)}) %collective-permute-start.15) | collective-permute-done | bytes 393248 | tf_op jit(solution)/shard_map/ppermute | solution.py:289
  61.0 1.7 %collective-permute-start.16 = (bf16[32,6144]{1,0:T(8,128)(2,1)S(1)}, bf16[32,6144]{1,0:T(8,128)(2,1)S(1)}, u32[]{:S(2)}, u32[]{:S(2)}) collective-permute-start(bf16[32,6144]{1,0:T(8,128)(2,1)S(1)} %add_convert_fusion.3), channel_id=1, source_target_pairs={{0,4},{5,1},{4,8},{9,5},{8,12},{13,9},{12,14},{15,13},{14,10},{11,... | collective-permute-start | bytes 1179656 | tf_op jit(solution)/shard_map/ppermute | solution.py:289
  62.8 2.4 %collective-permute-done.19 = bf16[32,6144]{1,0:T(8,128)(2,1)S(1)} collective-permute-done((bf16[32,6144]{1,0:T(8,128)(2,1)S(1)}, bf16[32,6144]{1,0:T(8,128)(2,1)S(1)}, u32[]{:S(2)}, u32[]{:S(2)}) %collective-permute-start.19) | collective-permute-done | bytes 393248 | tf_op jit(solution)/shard_map/ppermute | solution.py:289
  65.2 1.7 %collective-permute-start.20 = (bf16[32,6144]{1,0:T(8,128)(2,1)S(1)}, bf16[32,6144]{1,0:T(8,128)(2,1)S(1)}, u32[]{:S(2)}, u32[]{:S(2)}) collective-permute-start(bf16[32,6144]{1,0:T(8,128)(2,1)S(1)} %add_convert_fusion), channel_id=1, source_target_pairs={{0,4},{5,1},{4,8},{9,5},{8,12},{13,9},{12,14},{15,13},{14,10},{11,... | collective-permute-start | bytes 1179656 | tf_op jit(solution)/shard_map/ppermute | solution.py:289
  67.0 2.4 %collective-permute-done.16 = bf16[32,6144]{1,0:T(8,128)(2,1)S(1)} collective-permute-done((bf16[32,6144]{1,0:T(8,128)(2,1)S(1)}, bf16[32,6144]{1,0:T(8,128)(2,1)S(1)}, u32[]{:S(2)}, u32[]{:S(2)}) %collective-permute-start.16) | collective-permute-done | bytes 393248 | tf_op jit(solution)/shard_map/ppermute | solution.py:289
  69.4 1.7 %collective-permute-start.17 = (bf16[32,6144]{1,0:T(8,128)(2,1)S(1)}, bf16[32,6144]{1,0:T(8,128)(2,1)S(1)}, u32[]{:S(2)}, u32[]{:S(2)}) collective-permute-start(bf16[32,6144]{1,0:T(8,128)(2,1)S(1)} %add_convert_fusion.2), channel_id=1, source_target_pairs={{0,4},{5,1},{4,8},{9,5},{8,12},{13,9},{12,14},{15,13},{14,10},{11,... | collective-permute-start | bytes 1179656 | tf_op jit(solution)/shard_map/ppermute | solution.py:289
  71.2 2.4 %collective-permute-done.20 = bf16[32,6144]{1,0:T(8,128)(2,1)S(1)} collective-permute-done((bf16[32,6144]{1,0:T(8,128)(2,1)S(1)}, bf16[32,6144]{1,0:T(8,128)(2,1)S(1)}, u32[]{:S(2)}, u32[]{:S(2)}) %collective-permute-start.20) | collective-permute-done | bytes 393248 | tf_op jit(solution)/shard_map/ppermute | solution.py:289
  74.1 3.7 %collective-permute-done.17.arrived_ref = bf16[32,6144]{1,0:T(8,128)(2,1)S(1)} collective-permute-done((bf16[32,6144]{1,0:T(8,128)(2,1)S(1)}, bf16[32,6144]{1,0:T(8,128)(2,1)S(1)}, u32[]{:S(2)}, u32[]{:S(2)}) %collective-permute-start.17) | collective-permute-done | bytes 393248 | tf_op jit(solution)/shard_map/ppermute | solution.py:289
  77.8 1.4 %combine.1 = bf16[128,6144]{1,0:T(8,128)(2,1)} custom-call(bf16[32,6144]{1,0:T(8,128)(2,1)S(1)} %collective-permute-done.17.arrived_ref, bf16[32,6144]{1,0:T(8,128)(2,1)S(1)} %collective-permute-done.21.handed_ref, bf16[16,6144]{1,0:T(8,128)(2,1)S(1)} %get-tuple-element.93.product_ref, bf16[128,128]{1,0:T(8,128)(2,1)S(1)} %get-tuple-element.92.mixer_ref), custom_call_target="tpu_custom_call" | custom-call | tf_op jit(solution)/shard_map/combine/pallas_call | solution.py:263
  (60 shorter events, 6.2 us)
Async XLA Ops:
  1.7 3.2 %collective-permute-start = (bf16[32,6144]{1,0:T(8,128)(2,1)S(1)}, bf16[32,6144]{1,0:T(8,128)(2,1)S(1)}, u32[]{:S(2)}, u32[]{:S(2)}) collective-permute-start(bf16[32,6144]{1,0:T(8,128)(2,1)S(1)} %get-tuple-element.50), channel_id=1, source_target_pairs={{0,1},{1,0},{2,3},{3,2},{4,5},{5,4},{6,7},{7,6},{8,9},{9,8},{10,11... | collective-permute-start | bytes 1179656 | tf_op jit(solution)/shard_map/ppermute | solution.py:27
  2.2 8.3 %collective-permute-start.1 = (bf16[32,6144]{1,0:T(8,128)(2,1)S(1)}, bf16[32,6144]{1,0:T(8,128)(2,1)S(1)}, u32[]{:S(2)}, u32[]{:S(2)}) collective-permute-start(bf16[32,6144]{1,0:T(8,128)(2,1)S(1)} %get-tuple-element.49.refs_0_), channel_id=1, source_target_pairs={{0,4},{5,1},{4,8},{9,5},{8,12},{13,9},{12,14},{15,13},{14,10},{11,... | collective-permute-start | bytes 1179656 | tf_op jit(solution)/shard_map/ppermute | solution.py:289
  4.9 10.4 %collective-permute-start.2 = (bf16[32,6144]{1,0:T(8,128)(2,1)S(1)}, bf16[32,6144]{1,0:T(8,128)(2,1)S(1)}, u32[]{:S(2)}, u32[]{:S(2)}) collective-permute-start(bf16[32,6144]{1,0:T(8,128)(2,1)S(1)} %collective-permute-done.refs_1_), channel_id=1, source_target_pairs={{0,4},{5,1},{4,8},{9,5},{8,12},{13,9},{12,14},{15,13},{14,10},{11,... | collective-permute-start | bytes 1179656 | tf_op jit(solution)/shard_map/ppermute | solution.py:289
  10.6 9.0 %collective-permute-start.3 = (bf16[32,6144]{1,0:T(8,128)(2,1)S(1)}, bf16[32,6144]{1,0:T(8,128)(2,1)S(1)}, u32[]{:S(2)}, u32[]{:S(2)}) collective-permute-start(bf16[32,6144]{1,0:T(8,128)(2,1)S(1)} %collective-permute-done.1.refs_2_), channel_id=1, source_target_pairs={{0,4},{5,1},{4,8},{9,5},{8,12},{13,9},{12,14},{15,13},{14,10},{11,... | collective-permute-start | bytes 1179656 | tf_op jit(solution)/shard_map/ppermute | solution.py:289
  15.3 8.1 %collective-permute-start.4 = (bf16[32,6144]{1,0:T(8,128)(2,1)S(1)}, bf16[32,6144]{1,0:T(8,128)(2,1)S(1)}, u32[]{:S(2)}, u32[]{:S(2)}) collective-permute-start(bf16[32,6144]{1,0:T(8,128)(2,1)S(1)} %collective-permute-done.2.refs_3_), channel_id=1, source_target_pairs={{0,4},{5,1},{4,8},{9,5},{8,12},{13,9},{12,14},{15,13},{14,10},{11,... | collective-permute-start | bytes 1179656 | tf_op jit(solution)/shard_map/ppermute | solution.py:289
  19.6 8.4 %collective-permute-start.5 = (bf16[32,6144]{1,0:T(8,128)(2,1)S(1)}, bf16[32,6144]{1,0:T(8,128)(2,1)S(1)}, u32[]{:S(2)}, u32[]{:S(2)}) collective-permute-start(bf16[32,6144]{1,0:T(8,128)(2,1)S(1)} %collective-permute-done.3.refs_4_), channel_id=1, source_target_pairs={{0,4},{5,1},{4,8},{9,5},{8,12},{13,9},{12,14},{15,13},{14,10},{11,... | collective-permute-start | bytes 1179656 | tf_op jit(solution)/shard_map/ppermute | solution.py:289
  23.4 8.2 %collective-permute-start.6 = (bf16[32,6144]{1,0:T(8,128)(2,1)S(1)}, bf16[32,6144]{1,0:T(8,128)(2,1)S(1)}, u32[]{:S(2)}, u32[]{:S(2)}) collective-permute-start(bf16[32,6144]{1,0:T(8,128)(2,1)S(1)} %collective-permute-done.4.refs_5_), channel_id=1, source_target_pairs={{0,4},{5,1},{4,8},{9,5},{8,12},{13,9},{12,14},{15,13},{14,10},{11,... | collective-permute-start | bytes 1179656 | tf_op jit(solution)/shard_map/ppermute | solution.py:289
  28.0 7.9 %collective-permute-start.9 = (bf16[32,6144]{1,0:T(8,128)(2,1)S(1)}, bf16[32,6144]{1,0:T(8,128)(2,1)S(1)}, u32[]{:S(2)}, u32[]{:S(2)}) collective-permute-start(bf16[32,6144]{1,0:T(8,128)(2,1)S(1)} %collective-permute-done.5.refs_6_), channel_id=1, source_target_pairs={{0,4},{5,1},{4,8},{9,5},{8,12},{13,9},{12,14},{15,13},{14,10},{11,... | collective-permute-start | bytes 1179656 | tf_op jit(solution)/shard_map/ppermute | solution.py:289
  29.7 2.4 %collective-permute-start.7 = (bf16[64,6144]{1,0:T(8,128)(2,1)S(1)}, bf16[64,6144]{1,0:T(8,128)(2,1)S(1)}, u32[]{:S(2)}, u32[]{:S(2)}) collective-permute-start(bf16[64,6144]{1,0:T(8,128)(2,1)S(1)} %pad_maximum_fusion), channel_id=1, source_target_pairs={{0,1},{1,0},{2,3},{3,2},{4,5},{5,4},{6,7},{7,6},{8,9},{9,8},{10,11... | collective-permute-start | bytes 2359304 | tf_op jit(solution)/shard_map/ppermute | solution.py:27
  31.7 4.4 %collective-permute-start.8 = (bf16[32,6144]{1,0:T(8,128)(2,1)S(1)}, bf16[32,6144]{1,0:T(8,128)(2,1)S(1)}, u32[]{:S(2)}, u32[]{:S(2)}) collective-permute-start(bf16[32,6144]{1,0:T(8,128)(2,1)S(1)} %pad_maximum_fusion.1), channel_id=1, source_target_pairs={{0,1},{1,0},{2,3},{3,2},{4,5},{5,4},{6,7},{7,6},{8,9},{9,8},{10,11... | collective-permute-start | bytes 1179656 | tf_op jit(solution)/shard_map/ppermute | solution.py:27
  32.0 10.3 %slice-start = ((s8[12582912]{0:T(1024)(128)(4,1)}), s8[4194304]{0:T(1024)(128)(4,1)S(1)}, s32[]{:S(2)}) async-start(s8[12582912]{0:T(1024)(128)(4,1)} %bitcast.18), calls=%async_computation | async-start | bytes 8388608
  35.9 1.5 %collective-permute-start.10 = (bf16[16,6144]{1,0:T(8,128)(2,1)S(1)}, bf16[16,6144]{1,0:T(8,128)(2,1)S(1)}, u32[]{:S(2)}, u32[]{:S(2)}) collective-permute-start(bf16[16,6144]{1,0:T(8,128)(2,1)S(1)} %slice.131), channel_id=1, source_target_pairs={{0,1},{1,0},{2,3},{3,2},{4,5},{5,4},{6,7},{7,6},{8,9},{9,8},{10,11... | collective-permute-start | bytes 589832 | tf_op jit(solution)/shard_map/ppermute | solution.py:27
  37.4 5.0 %slice-start.1 = ((s8[12582912]{0:T(1024)(128)(4,1)}), s8[4194304]{0:T(1024)(128)(4,1)S(1)}, s32[]{:S(2)}) async-start(s8[12582912]{0:T(1024)(128)(4,1)} %bitcast.18), calls=%async_computation.1 | async-start | bytes 8388608
  37.4 5.0 %slice-start.2 = ((s8[12582912]{0:T(1024)(128)(4,1)}), s8[4194304]{0:T(1024)(128)(4,1)S(1)}, s32[]{:S(2)}) async-start(s8[12582912]{0:T(1024)(128)(4,1)} %bitcast.18), calls=%async_computation.2 | async-start | bytes 8388608
  44.5 2.7 %collective-permute-start.13 = (bf16[32,6144]{1,0:T(8,128)(2,1)S(1)}, bf16[32,6144]{1,0:T(8,128)(2,1)S(1)}, u32[]{:S(2)}, u32[]{:S(2)}) collective-permute-start(bf16[32,6144]{1,0:T(8,128)(2,1)S(1)} %slice.165), channel_id=1, source_target_pairs={{0,1},{1,0},{2,3},{3,2},{4,5},{5,4},{6,7},{7,6},{8,9},{9,8},{10,11... | collective-permute-start | bytes 1179656 | tf_op jit(solution)/shard_map/ppermute | solution.py:27
  44.8 7.3 %collective-permute-start.12 = (bf16[16,6144]{1,0:T(8,128)(2,1)S(1)}, bf16[16,6144]{1,0:T(8,128)(2,1)S(1)}, u32[]{:S(2)}, u32[]{:S(2)}) collective-permute-start(bf16[16,6144]{1,0:T(8,128)(2,1)S(1)} %get-tuple-element.100), channel_id=1, source_target_pairs={{1,4},{4,1},{5,8},{8,5},{9,12},{12,9},{13,14},{14,13},{15,10},{10,... | collective-permute-start | bytes 589832 | tf_op jit(solution)/shard_map/ppermute | solution.py:289
  46.8 5.7 %collective-permute-start.11 = (bf16[16,6144]{1,0:T(8,128)(2,1)S(1)}, bf16[16,6144]{1,0:T(8,128)(2,1)S(1)}, u32[]{:S(2)}, u32[]{:S(2)}) collective-permute-start(bf16[16,6144]{1,0:T(8,128)(2,1)S(1)} %get-tuple-element.101), channel_id=1, source_target_pairs={{0,4},{5,1},{4,8},{9,5},{8,12},{13,9},{12,14},{15,13},{14,10},{11,... | collective-permute-start | bytes 589832 | tf_op jit(solution)/shard_map/ppermute | solution.py:289
  47.3 9.5 %collective-permute-start.18 = (bf16[32,6144]{1,0:T(8,128)(2,1)S(1)}, bf16[32,6144]{1,0:T(8,128)(2,1)S(1)}, u32[]{:S(2)}, u32[]{:S(2)}) collective-permute-start(bf16[32,6144]{1,0:T(8,128)(2,1)S(1)} %pad_maximum_fusion.2), channel_id=1, source_target_pairs={{0,4},{5,1},{4,8},{9,5},{8,12},{13,9},{12,14},{15,13},{14,10},{11,... | collective-permute-start | bytes 1179656 | tf_op jit(solution)/shard_map/ppermute | solution.py:289
  52.6 8.3 %collective-permute-start.15 = (bf16[32,6144]{1,0:T(8,128)(2,1)S(1)}, bf16[32,6144]{1,0:T(8,128)(2,1)S(1)}, u32[]{:S(2)}, u32[]{:S(2)}) collective-permute-start(bf16[32,6144]{1,0:T(8,128)(2,1)S(1)} %add_convert_fusion.4), channel_id=1, source_target_pairs={{0,4},{5,1},{4,8},{9,5},{8,12},{13,9},{12,14},{15,13},{14,10},{11,... | collective-permute-start | bytes 1179656 | tf_op jit(solution)/shard_map/ppermute | solution.py:289
  54.4 2.4 %collective-permute-start.14 = (bf16[64,6144]{1,0:T(8,128)(2,1)S(1)}, bf16[64,6144]{1,0:T(8,128)(2,1)S(1)}, u32[]{:S(2)}, u32[]{:S(2)}) collective-permute-start(bf16[64,6144]{1,0:T(8,128)(2,1)S(1)} %slice.145), channel_id=1, source_target_pairs={{0,1},{1,0},{2,3},{3,2},{4,5},{5,4},{6,7},{7,6},{8,9},{9,8},{10,11... | collective-permute-start | bytes 2359304 | tf_op jit(solution)/shard_map/ppermute | solution.py:27
  56.9 8.2 %collective-permute-start.19 = (bf16[32,6144]{1,0:T(8,128)(2,1)S(1)}, bf16[32,6144]{1,0:T(8,128)(2,1)S(1)}, u32[]{:S(2)}, u32[]{:S(2)}) collective-permute-start(bf16[32,6144]{1,0:T(8,128)(2,1)S(1)} %add_convert_fusion.1), channel_id=1, source_target_pairs={{0,4},{5,1},{4,8},{9,5},{8,12},{13,9},{12,14},{15,13},{14,10},{11,... | collective-permute-start | bytes 1179656 | tf_op jit(solution)/shard_map/ppermute | solution.py:289
  61.0 8.3 %collective-permute-start.16 = (bf16[32,6144]{1,0:T(8,128)(2,1)S(1)}, bf16[32,6144]{1,0:T(8,128)(2,1)S(1)}, u32[]{:S(2)}, u32[]{:S(2)}) collective-permute-start(bf16[32,6144]{1,0:T(8,128)(2,1)S(1)} %add_convert_fusion.3), channel_id=1, source_target_pairs={{0,4},{5,1},{4,8},{9,5},{8,12},{13,9},{12,14},{15,13},{14,10},{11,... | collective-permute-start | bytes 1179656 | tf_op jit(solution)/shard_map/ppermute | solution.py:289
  65.2 8.3 %collective-permute-start.20 = (bf16[32,6144]{1,0:T(8,128)(2,1)S(1)}, bf16[32,6144]{1,0:T(8,128)(2,1)S(1)}, u32[]{:S(2)}, u32[]{:S(2)}) collective-permute-start(bf16[32,6144]{1,0:T(8,128)(2,1)S(1)} %add_convert_fusion), channel_id=1, source_target_pairs={{0,4},{5,1},{4,8},{9,5},{8,12},{13,9},{12,14},{15,13},{14,10},{11,... | collective-permute-start | bytes 1179656 | tf_op jit(solution)/shard_map/ppermute | solution.py:289
  69.4 8.3 %collective-permute-start.17 = (bf16[32,6144]{1,0:T(8,128)(2,1)S(1)}, bf16[32,6144]{1,0:T(8,128)(2,1)S(1)}, u32[]{:S(2)}, u32[]{:S(2)}) collective-permute-start(bf16[32,6144]{1,0:T(8,128)(2,1)S(1)} %add_convert_fusion.2), channel_id=1, source_target_pairs={{0,4},{5,1},{4,8},{9,5},{8,12},{13,9},{12,14},{15,13},{14,10},{11,... | collective-permute-start | bytes 1179656 | tf_op jit(solution)/shard_map/ppermute | solution.py:289
  73.7 4.1 %collective-permute-start.21 = (bf16[32,6144]{1,0:T(8,128)(2,1)S(1)}, bf16[32,6144]{1,0:T(8,128)(2,1)S(1)}, u32[]{:S(2)}, u32[]{:S(2)}) collective-permute-start(bf16[32,6144]{1,0:T(8,128)(2,1)S(1)} %pad_maximum_fusion.3), channel_id=1, source_target_pairs={{0,1},{1,0},{2,3},{3,2},{4,5},{5,4},{6,7},{7,6},{8,9},{9,8},{10,11... | collective-permute-start | bytes 1179656 | tf_op jit(solution)/shard_map/ppermute | solution.py:27

commit v8 on v7

--- a/solution.py
+++ b/solution.py
@@ -322,8 +322,9 @@
     ups, gates = (h if h else [w] for h, w in zip(held_weights, weights))
     up_done, gate_done = sums
 
-    rows = [(u, 0, CAP) for u in units[:-1]]
-    rows += [(given[0], BLOCK * k, BLOCK) for k in range(reach - 2)] + [(given[1], 0, BLOCK)]
+    rows = [(u, 0, CAP) for u in units[:-3]]
+    rows += [(given[0], BLOCK * k, BLOCK) for k in range(reach - 2)]
+    rows += [(u, 0, CAP) for u in units[-3:-1]] + [(given[1], 0, BLOCK)]
     rows += [(units[-1], 0, CAP), (far, 0, CAP)]
     groups = [[]]
     for row in rows:
@@ -333,21 +334,16 @@
     hidden = [hidden_of(groups[0], gates, ups, gate_done, up_done)]
     hidden += [hidden_of(group, gates, ups) for group in groups[1:]]
     hidden = jnp.concatenate(hidden, axis=0) if len(hidden) > 1 else hidden[0]
-    mine = [hidden[BLOCK * k : BLOCK * (k + 1)] for k in range(reach)]
-    others = [hidden[BLOCK * k : BLOCK * (k + 1)] for k in range(reach, 2 * reach)]
-
-    def product_of(*parts):
-        product = jnp.dot(
-            jnp.concatenate(parts, axis=0), w_down, preferred_element_type=jnp.float32
-        )
+    def product_of(part):
+        product = jnp.dot(part, w_down, preferred_element_type=jnp.float32)
         return lax.optimization_barrier(product.astype(jnp.bfloat16))
 
-    product = product_of(mine[reach - 1], *others[-2:])
+    product = product_of(hidden[-3 * BLOCK :])
     handed, kept = [swap(product[:BLOCK])], [product[BLOCK : 2 * BLOCK]]
     a = [hop(product[2 * BLOCK : 2 * BLOCK + CAP]), hop(product[2 * BLOCK + CAP :], aside)]
     first = jnp.concatenate([kept[0][:CAP], handed[0][:CAP]], axis=0)
-    first, parts = after(first, (*mine[:-1], *others[:-2]))
-    product = product_of(*parts)
+    first, part = after(first, hidden[: -3 * BLOCK])
+    product = product_of(part)
     a, product = after(a, product)
     own = product[:BLOCK]
     if reach > 2:

time: 79.5 us -> 79.5 us (level)
  no operation moved by 1% of the time
where the time goes in v8:
time: 79.5 us; the launch traced here: 79.3 us
  starting transfers between devices  27.8 us (35%)
  waiting for transfers between devices  23.9 us (30%)
  Pallas kernels  21.8 us (27%)
  matrix products  4.32 us (5%)
    ppermute x15, starting transfers between devices, hop(): return lax.ppermute(value, ('ept', 'exp'), pairs)  25.8 us
    ppermute x15, waiting for transfers between devices, hop(): return lax.ppermute(value, ('ept', 'exp'), pairs)  20.4 us
    pallas_call x7, Pallas kernels, call(): pl.pallas_call(kernel, in_specs=[pl.BlockSpec(memory_space=m) for _, m in...  20.4 us
    dot_general x2, matrix products, product_of(): product = jnp.dot(part, w_down, preferred_element_type=jnp.float32)  4.32 us
    ppermute x7, waiting for transfers between devices, swap(): return lax.ppermute(value, 'exp', [(0, 1), (1, 0)])  3.46 us
    ppermute x7, starting transfers between devices, swap(): return lax.ppermute(value, 'exp', [(0, 1), (1, 0)])  1.94 us
  transfers between devices with their start and end apart: 22, of which 13 were waited for; matrix products, arithmetic and copies ran while one was open for 4% of the time, Pallas kernels for 17%

profile of v8, /device:TPU:0, one launch (start us, length us, event | category | flops | bytes accessed | tf_op | source)
XLA Modules:
  0.0 79.3 jit_solution(4265636113606972203)
XLA Ops:
  0.0 1.7 %dispatch.1 = (bf16[32,6144]{1,0:T(8,128)(2,1)S(1)}, bf16[32,6144]{1,0:T(8,128)(2,1)S(1)}, bf16[128,128]{1,0:T(8,128)(2,1)S(1)}) custom-call(s32[1]{0:T(128)} %bitcast.me_ref, s32[2,128]{1,0:T(2,128)} %bitcast.22, f32[2,128]{1,0:T(2,128)} %bitcast.23, bf16[128,6144]{1,0:T(8,128)(2,1)} %tokens_hbm.1), custom_call_target="tpu_custom_call" | custom-call | tf_op jit(solution)/shard_map/dispatch/pallas_call | solution.py:104
  2.2 2.6 %collective-permute-start.1 = (bf16[32,6144]{1,0:T(8,128)(2,1)S(1)}, bf16[32,6144]{1,0:T(8,128)(2,1)S(1)}, u32[]{:S(2)}, u32[]{:S(2)}) collective-permute-start(bf16[32,6144]{1,0:T(8,128)(2,1)S(1)} %get-tuple-element.45.refs_0_), channel_id=1, source_target_pairs={{0,4},{5,1},{4,8},{9,5},{8,12},{13,9},{12,14},{15,13},{14,10},{11,... | collective-permute-start | bytes 1179656 | tf_op jit(solution)/shard_map/ppermute | solution.py:289
  4.9 1.7 %collective-permute-start.2 = (bf16[32,6144]{1,0:T(8,128)(2,1)S(1)}, bf16[32,6144]{1,0:T(8,128)(2,1)S(1)}, u32[]{:S(2)}, u32[]{:S(2)}) collective-permute-start(bf16[32,6144]{1,0:T(8,128)(2,1)S(1)} %collective-permute-done.refs_1_), channel_id=1, source_target_pairs={{0,4},{5,1},{4,8},{9,5},{8,12},{13,9},{12,14},{15,13},{14,10},{11,... | collective-permute-start | bytes 1179656 | tf_op jit(solution)/shard_map/ppermute | solution.py:289
  6.5 4.0 %collective-permute-done.1.refs_2_ = bf16[32,6144]{1,0:T(8,128)(2,1)S(1)} collective-permute-done((bf16[32,6144]{1,0:T(8,128)(2,1)S(1)}, bf16[32,6144]{1,0:T(8,128)(2,1)S(1)}, u32[]{:S(2)}, u32[]{:S(2)}) %collective-permute-start.1) | collective-permute-done | bytes 393248 | tf_op jit(solution)/shard_map/ppermute | solution.py:289
  10.6 2.1 %collective-permute-start.3 = (bf16[32,6144]{1,0:T(8,128)(2,1)S(1)}, bf16[32,6144]{1,0:T(8,128)(2,1)S(1)}, u32[]{:S(2)}, u32[]{:S(2)}) collective-permute-start(bf16[32,6144]{1,0:T(8,128)(2,1)S(1)} %collective-permute-done.1.refs_2_), channel_id=1, source_target_pairs={{0,4},{5,1},{4,8},{9,5},{8,12},{13,9},{12,14},{15,13},{14,10},{11,... | collective-permute-start | bytes 1179656 | tf_op jit(solution)/shard_map/ppermute | solution.py:289
  12.6 2.6 %hold_and_multiply.5 = (bf16[2304,1024]{1,0:T(8,128)(2,1)S(1)}, f32[48,1024]{1,0:T(8,128)S(1)}) custom-call(bf16[32,6144]{1,0:T(8,128)(2,1)S(1)} %get-tuple-element.45.refs_0_, bf16[32,6144]{1,0:T(8,128)(2,1)S(1)} %collective-permute-done.refs_1_, bf16[32,6144]{1,0:T(8,128)(2,1)S(1)} %collective-permute-done.1.refs_2_, bf16[6144,1024]{1,0:T(8,128)(2,1)} %bitcast.15), custom_call_target="tpu_custom_call" | custom-call | flops 226492416 | bytes 4718592 | tf_op jit(solution)/shard_map/hold_and_multiply/pallas_call | solution.py:104
  15.3 1.6 %collective-permute-start.4 = (bf16[32,6144]{1,0:T(8,128)(2,1)S(1)}, bf16[32,6144]{1,0:T(8,128)(2,1)S(1)}, u32[]{:S(2)}, u32[]{:S(2)}) collective-permute-start(bf16[32,6144]{1,0:T(8,128)(2,1)S(1)} %collective-permute-done.2.refs_3_), channel_id=1, source_target_pairs={{0,4},{5,1},{4,8},{9,5},{8,12},{13,9},{12,14},{15,13},{14,10},{11,... | collective-permute-start | bytes 1179656 | tf_op jit(solution)/shard_map/ppermute | solution.py:289
  16.9 2.6 %hold_and_multiply.6 = (bf16[2304,1024]{1,0:T(8,128)(2,1)S(1)}, f32[48,1024]{1,0:T(8,128)S(1)}) custom-call(bf16[32,6144]{1,0:T(8,128)(2,1)S(1)} %get-tuple-element.45.refs_0_, bf16[32,6144]{1,0:T(8,128)(2,1)S(1)} %collective-permute-done.refs_1_, bf16[32,6144]{1,0:T(8,128)(2,1)S(1)} %collective-permute-done.1.refs_2_, bf16[6144,1024]{1,0:T(8,128)(2,1)} %bitcast.16, ...), custom_call_target="tpu_custom_call" | custom-call | flops 226492416 | bytes 4718592 | tf_op jit(solution)/shard_map/hold_and_multiply/pallas_call | solution.py:104
  19.6 1.6 %collective-permute-start.5 = (bf16[32,6144]{1,0:T(8,128)(2,1)S(1)}, bf16[32,6144]{1,0:T(8,128)(2,1)S(1)}, u32[]{:S(2)}, u32[]{:S(2)}) collective-permute-start(bf16[32,6144]{1,0:T(8,128)(2,1)S(1)} %collective-permute-done.3.refs_4_), channel_id=1, source_target_pairs={{0,4},{5,1},{4,8},{9,5},{8,12},{13,9},{12,14},{15,13},{14,10},{11,... | collective-permute-start | bytes 1179656 | tf_op jit(solution)/shard_map/ppermute | solution.py:289
  21.2 2.1 %hold_and_multiply.7 = (bf16[1536,1024]{1,0:T(8,128)(2,1)S(1)}, f32[48,1024]{1,0:T(8,128)S(1)}) custom-call(bf16[32,6144]{1,0:T(8,128)(2,1)S(1)} %get-tuple-element.45.refs_0_, bf16[32,6144]{1,0:T(8,128)(2,1)S(1)} %collective-permute-done.refs_1_, bf16[32,6144]{1,0:T(8,128)(2,1)S(1)} %collective-permute-done.1.refs_2_, bf16[6144,1024]{1,0:T(8,128)(2,1)} %bitcast.17, ...), custom_call_target="tpu_custom_call" | custom-call | flops 150994944 | bytes 3145728 | tf_op jit(solution)/shard_map/hold_and_multiply/pallas_call | solution.py:104
  23.4 1.9 %collective-permute-start.7 = (bf16[32,6144]{1,0:T(8,128)(2,1)S(1)}, bf16[32,6144]{1,0:T(8,128)(2,1)S(1)}, u32[]{:S(2)}, u32[]{:S(2)}) collective-permute-start(bf16[32,6144]{1,0:T(8,128)(2,1)S(1)} %collective-permute-done.4.refs_5_), channel_id=1, source_target_pairs={{0,4},{5,1},{4,8},{9,5},{8,12},{13,9},{12,14},{15,13},{14,10},{11,... | collective-permute-start | bytes 1179656 | tf_op jit(solution)/shard_map/ppermute | solution.py:289
  25.3 2.7 %hold_and_multiply.8 = (bf16[2304,1024]{1,0:T(8,128)(2,1)S(1)}, f32[96,1024]{1,0:T(8,128)S(1)}) custom-call(bf16[32,6144]{1,0:T(8,128)(2,1)S(1)} %get-tuple-element.45.refs_0_, bf16[32,6144]{1,0:T(8,128)(2,1)S(1)} %collective-permute-done.refs_1_, bf16[32,6144]{1,0:T(8,128)(2,1)S(1)} %collective-permute-done.1.refs_2_, ...), custom_call_target="tpu_custom_call" | custom-call | flops 452984832 | bytes 4718592 | tf_op jit(solution)/shard_map/hold_and_multiply/pallas_call | solution.py:104
  28.0 1.6 %collective-permute-start.9 = (bf16[32,6144]{1,0:T(8,128)(2,1)S(1)}, bf16[32,6144]{1,0:T(8,128)(2,1)S(1)}, u32[]{:S(2)}, u32[]{:S(2)}) collective-permute-start(bf16[32,6144]{1,0:T(8,128)(2,1)S(1)} %collective-permute-done.5.refs_8_), channel_id=1, source_target_pairs={{0,4},{5,1},{4,8},{9,5},{8,12},{13,9},{12,14},{15,13},{14,10},{11,... | collective-permute-start | bytes 1179656 | tf_op jit(solution)/shard_map/ppermute | solution.py:289
  29.8 1.9 %collective-permute-done.7.refs_9_ = bf16[32,6144]{1,0:T(8,128)(2,1)S(1)} collective-permute-done((bf16[32,6144]{1,0:T(8,128)(2,1)S(1)}, bf16[32,6144]{1,0:T(8,128)(2,1)S(1)}, u32[]{:S(2)}, u32[]{:S(2)}) %collective-permute-start.7) | collective-permute-done | bytes 393248 | tf_op jit(solution)/shard_map/ppermute | solution.py:289
  32.0 3.8 %hold_and_multiply.9 = (bf16[3840,1024]{1,0:T(8,128)(2,1)S(1)}, f32[96,1024]{1,0:T(8,128)S(1)}) custom-call(bf16[32,6144]{1,0:T(8,128)(2,1)S(1)} %get-tuple-element.45.refs_0_, bf16[32,6144]{1,0:T(8,128)(2,1)S(1)} %collective-permute-done.refs_1_, bf16[32,6144]{1,0:T(8,128)(2,1)S(1)} %collective-permute-done.1.refs_2_, ...), custom_call_target="tpu_custom_call" | custom-call | flops 754974720 | bytes 7864320 | tf_op jit(solution)/shard_map/hold_and_multiply/pallas_call | solution.py:104
  37.4 4.9 %hidden.1 = bf16[256,1024]{1,0:T(8,128)(2,1)S(1)} custom-call(bf16[32,6144]{1,0:T(8,128)(2,1)S(1)} %get-tuple-element.45.refs_0_, bf16[32,6144]{1,0:T(8,128)(2,1)S(1)} %collective-permute-done.refs_1_, bf16[32,6144]{1,0:T(8,128)(2,1)S(1)} %collective-permute-done.1.refs_2_, bf16[32,6144]{1,0:T(8,128)(2,1)S(1)} %collective-permute-done.2.refs_3_, ...), custom_call_target="tpu_custom_call" | custom-call | flops 6442450944 | bytes 25165824 | tf_op jit(solution)/shard_map/hidden/pallas_call | solution.py:104
  42.3 2.1 %fusion.7 = bf16[96,6144]{1,0:T(8,128)(2,1)S(1)} fusion(bf16[1,1024,6144]{2,1,0:T(8,128)(2,1)S(1)} %bitcast.19, bf16[256,1024]{1,0:T(8,128)(2,1)S(1)} %hidden.1), kind=kOutput, calls=%fused_computation.5 | convolution fusion | flops 1208549376 | bytes 13959168 | tf_op jit(solution)/shard_map/dot_general | solution.py:338
  44.8 2.0 %collective-permute-start.12 = (bf16[16,6144]{1,0:T(8,128)(2,1)S(1)}, bf16[16,6144]{1,0:T(8,128)(2,1)S(1)}, u32[]{:S(2)}, u32[]{:S(2)}) collective-permute-start(bf16[16,6144]{1,0:T(8,128)(2,1)S(1)} %get-tuple-element.92), channel_id=1, source_target_pairs={{1,4},{4,1},{5,8},{8,5},{9,12},{12,9},{13,14},{14,13},{15,10},{10,... | collective-permute-start | bytes 589832 | tf_op jit(solution)/shard_map/ppermute | solution.py:289
  47.3 1.7 %collective-permute-start.18 = (bf16[32,6144]{1,0:T(8,128)(2,1)S(1)}, bf16[32,6144]{1,0:T(8,128)(2,1)S(1)}, u32[]{:S(2)}, u32[]{:S(2)}) collective-permute-start(bf16[32,6144]{1,0:T(8,128)(2,1)S(1)} %pad_maximum_fusion.2), channel_id=1, source_target_pairs={{0,4},{5,1},{4,8},{9,5},{8,12},{13,9},{12,14},{15,13},{14,10},{11,... | collective-permute-start | bytes 1179656 | tf_op jit(solution)/shard_map/ppermute | solution.py:289
  49.0 2.2 %fusion.4 = bf16[160,6144]{1,0:T(8,128)(2,1)S(1)} fusion(bf16[160,1024]{1,0:T(8,128)(2,1)S(1)} %slice.144, bf16[1,1024,6144]{2,1,0:T(8,128)(2,1)S(1)} %bitcast.19), kind=kOutput, calls=%fused_computation.4 | convolution fusion | flops 2014248960 | bytes 14876672 | tf_op jit(solution)/shard_map/dot_general | solution.py:338
  52.6 1.7 %collective-permute-start.15 = (bf16[32,6144]{1,0:T(8,128)(2,1)S(1)}, bf16[32,6144]{1,0:T(8,128)(2,1)S(1)}, u32[]{:S(2)}, u32[]{:S(2)}) collective-permute-start(bf16[32,6144]{1,0:T(8,128)(2,1)S(1)} %add_convert_fusion.4), channel_id=1, source_target_pairs={{0,4},{5,1},{4,8},{9,5},{8,12},{13,9},{12,14},{15,13},{14,10},{11,... | collective-permute-start | bytes 1179656 | tf_op jit(solution)/shard_map/ppermute | solution.py:289
  54.8 2.0 %collective-permute-done.14 = bf16[64,6144]{1,0:T(8,128)(2,1)S(1)} collective-permute-done((bf16[64,6144]{1,0:T(8,128)(2,1)S(1)}, bf16[64,6144]{1,0:T(8,128)(2,1)S(1)}, u32[]{:S(2)}, u32[]{:S(2)}) %collective-permute-start.14) | collective-permute-done | bytes 786464 | tf_op jit(solution)/shard_map/ppermute | solution.py:27
  56.9 1.6 %collective-permute-start.19 = (bf16[32,6144]{1,0:T(8,128)(2,1)S(1)}, bf16[32,6144]{1,0:T(8,128)(2,1)S(1)}, u32[]{:S(2)}, u32[]{:S(2)}) collective-permute-start(bf16[32,6144]{1,0:T(8,128)(2,1)S(1)} %add_convert_fusion.1), channel_id=1, source_target_pairs={{0,4},{5,1},{4,8},{9,5},{8,12},{13,9},{12,14},{15,13},{14,10},{11,... | collective-permute-start | bytes 1179656 | tf_op jit(solution)/shard_map/ppermute | solution.py:289
  58.5 2.4 %collective-permute-done.15 = bf16[32,6144]{1,0:T(8,128)(2,1)S(1)} collective-permute-done((bf16[32,6144]{1,0:T(8,128)(2,1)S(1)}, bf16[32,6144]{1,0:T(8,128)(2,1)S(1)}, u32[]{:S(2)}, u32[]{:S(2)}) %collective-permute-start.15) | collective-permute-done | bytes 393248 | tf_op jit(solution)/shard_map/ppermute | solution.py:289
  61.0 1.7 %collective-permute-start.16 = (bf16[32,6144]{1,0:T(8,128)(2,1)S(1)}, bf16[32,6144]{1,0:T(8,128)(2,1)S(1)}, u32[]{:S(2)}, u32[]{:S(2)}) collective-permute-start(bf16[32,6144]{1,0:T(8,128)(2,1)S(1)} %add_convert_fusion.3), channel_id=1, source_target_pairs={{0,4},{5,1},{4,8},{9,5},{8,12},{13,9},{12,14},{15,13},{14,10},{11,... | collective-permute-start | bytes 1179656 | tf_op jit(solution)/shard_map/ppermute | solution.py:289
  62.7 2.4 %collective-permute-done.19 = bf16[32,6144]{1,0:T(8,128)(2,1)S(1)} collective-permute-done((bf16[32,6144]{1,0:T(8,128)(2,1)S(1)}, bf16[32,6144]{1,0:T(8,128)(2,1)S(1)}, u32[]{:S(2)}, u32[]{:S(2)}) %collective-permute-start.19) | collective-permute-done | bytes 393248 | tf_op jit(solution)/shard_map/ppermute | solution.py:289
  65.2 1.7 %collective-permute-start.20 = (bf16[32,6144]{1,0:T(8,128)(2,1)S(1)}, bf16[32,6144]{1,0:T(8,128)(2,1)S(1)}, u32[]{:S(2)}, u32[]{:S(2)}) collective-permute-start(bf16[32,6144]{1,0:T(8,128)(2,1)S(1)} %add_convert_fusion), channel_id=1, source_target_pairs={{0,4},{5,1},{4,8},{9,5},{8,12},{13,9},{12,14},{15,13},{14,10},{11,... | collective-permute-start | bytes 1179656 | tf_op jit(solution)/shard_map/ppermute | solution.py:289
  66.9 2.4 %collective-permute-done.16 = bf16[32,6144]{1,0:T(8,128)(2,1)S(1)} collective-permute-done((bf16[32,6144]{1,0:T(8,128)(2,1)S(1)}, bf16[32,6144]{1,0:T(8,128)(2,1)S(1)}, u32[]{:S(2)}, u32[]{:S(2)}) %collective-permute-start.16) | collective-permute-done | bytes 393248 | tf_op jit(solution)/shard_map/ppermute | solution.py:289
  69.4 1.7 %collective-permute-start.17 = (bf16[32,6144]{1,0:T(8,128)(2,1)S(1)}, bf16[32,6144]{1,0:T(8,128)(2,1)S(1)}, u32[]{:S(2)}, u32[]{:S(2)}) collective-permute-start(bf16[32,6144]{1,0:T(8,128)(2,1)S(1)} %add_convert_fusion.2), channel_id=1, source_target_pairs={{0,4},{5,1},{4,8},{9,5},{8,12},{13,9},{12,14},{15,13},{14,10},{11,... | collective-permute-start | bytes 1179656 | tf_op jit(solution)/shard_map/ppermute | solution.py:289
  71.2 2.4 %collective-permute-done.20 = bf16[32,6144]{1,0:T(8,128)(2,1)S(1)} collective-permute-done((bf16[32,6144]{1,0:T(8,128)(2,1)S(1)}, bf16[32,6144]{1,0:T(8,128)(2,1)S(1)}, u32[]{:S(2)}, u32[]{:S(2)}) %collective-permute-start.20) | collective-permute-done | bytes 393248 | tf_op jit(solution)/shard_map/ppermute | solution.py:289
  74.1 3.7 %collective-permute-done.17.arrived_ref = bf16[32,6144]{1,0:T(8,128)(2,1)S(1)} collective-permute-done((bf16[32,6144]{1,0:T(8,128)(2,1)S(1)}, bf16[32,6144]{1,0:T(8,128)(2,1)S(1)}, u32[]{:S(2)}, u32[]{:S(2)}) %collective-permute-start.17) | collective-permute-done | bytes 393248 | tf_op jit(solution)/shard_map/ppermute | solution.py:289
  77.8 1.4 %combine.1 = bf16[128,6144]{1,0:T(8,128)(2,1)} custom-call(bf16[32,6144]{1,0:T(8,128)(2,1)S(1)} %collective-permute-done.17.arrived_ref, bf16[32,6144]{1,0:T(8,128)(2,1)S(1)} %collective-permute-done.21.handed_ref, bf16[16,6144]{1,0:T(8,128)(2,1)S(1)} %get-tuple-element.85.product_ref, bf16[128,128]{1,0:T(8,128)(2,1)S(1)} %get-tuple-element.84.mixer_ref), custom_call_target="tpu_custom_call" | custom-call | tf_op jit(solution)/shard_map/combine/pallas_call | solution.py:263
  (54 shorter events, 6.2 us)
Async XLA Ops:
  1.7 3.2 %collective-permute-start = (bf16[32,6144]{1,0:T(8,128)(2,1)S(1)}, bf16[32,6144]{1,0:T(8,128)(2,1)S(1)}, u32[]{:S(2)}, u32[]{:S(2)}) collective-permute-start(bf16[32,6144]{1,0:T(8,128)(2,1)S(1)} %get-tuple-element.46), channel_id=1, source_target_pairs={{0,1},{1,0},{2,3},{3,2},{4,5},{5,4},{6,7},{7,6},{8,9},{9,8},{10,11... | collective-permute-start | bytes 1179656 | tf_op jit(solution)/shard_map/ppermute | solution.py:27
  2.2 8.3 %collective-permute-start.1 = (bf16[32,6144]{1,0:T(8,128)(2,1)S(1)}, bf16[32,6144]{1,0:T(8,128)(2,1)S(1)}, u32[]{:S(2)}, u32[]{:S(2)}) collective-permute-start(bf16[32,6144]{1,0:T(8,128)(2,1)S(1)} %get-tuple-element.45.refs_0_), channel_id=1, source_target_pairs={{0,4},{5,1},{4,8},{9,5},{8,12},{13,9},{12,14},{15,13},{14,10},{11,... | collective-permute-start | bytes 1179656 | tf_op jit(solution)/shard_map/ppermute | solution.py:289
  4.9 10.4 %collective-permute-start.2 = (bf16[32,6144]{1,0:T(8,128)(2,1)S(1)}, bf16[32,6144]{1,0:T(8,128)(2,1)S(1)}, u32[]{:S(2)}, u32[]{:S(2)}) collective-permute-start(bf16[32,6144]{1,0:T(8,128)(2,1)S(1)} %collective-permute-done.refs_1_), channel_id=1, source_target_pairs={{0,4},{5,1},{4,8},{9,5},{8,12},{13,9},{12,14},{15,13},{14,10},{11,... | collective-permute-start | bytes 1179656 | tf_op jit(solution)/shard_map/ppermute | solution.py:289
  10.6 9.0 %collective-permute-start.3 = (bf16[32,6144]{1,0:T(8,128)(2,1)S(1)}, bf16[32,6144]{1,0:T(8,128)(2,1)S(1)}, u32[]{:S(2)}, u32[]{:S(2)}) collective-permute-start(bf16[32,6144]{1,0:T(8,128)(2,1)S(1)} %collective-permute-done.1.refs_2_), channel_id=1, source_target_pairs={{0,4},{5,1},{4,8},{9,5},{8,12},{13,9},{12,14},{15,13},{14,10},{11,... | collective-permute-start | bytes 1179656 | tf_op jit(solution)/shard_map/ppermute | solution.py:289
  15.3 8.1 %collective-permute-start.4 = (bf16[32,6144]{1,0:T(8,128)(2,1)S(1)}, bf16[32,6144]{1,0:T(8,128)(2,1)S(1)}, u32[]{:S(2)}, u32[]{:S(2)}) collective-permute-start(bf16[32,6144]{1,0:T(8,128)(2,1)S(1)} %collective-permute-done.2.refs_3_), channel_id=1, source_target_pairs={{0,4},{5,1},{4,8},{9,5},{8,12},{13,9},{12,14},{15,13},{14,10},{11,... | collective-permute-start | bytes 1179656 | tf_op jit(solution)/shard_map/ppermute | solution.py:289
  19.6 8.4 %collective-permute-start.5 = (bf16[32,6144]{1,0:T(8,128)(2,1)S(1)}, bf16[32,6144]{1,0:T(8,128)(2,1)S(1)}, u32[]{:S(2)}, u32[]{:S(2)}) collective-permute-start(bf16[32,6144]{1,0:T(8,128)(2,1)S(1)} %collective-permute-done.3.refs_4_), channel_id=1, source_target_pairs={{0,4},{5,1},{4,8},{9,5},{8,12},{13,9},{12,14},{15,13},{14,10},{11,... | collective-permute-start | bytes 1179656 | tf_op jit(solution)/shard_map/ppermute | solution.py:289
  23.4 8.2 %collective-permute-start.7 = (bf16[32,6144]{1,0:T(8,128)(2,1)S(1)}, bf16[32,6144]{1,0:T(8,128)(2,1)S(1)}, u32[]{:S(2)}, u32[]{:S(2)}) collective-permute-start(bf16[32,6144]{1,0:T(8,128)(2,1)S(1)} %collective-permute-done.4.refs_5_), channel_id=1, source_target_pairs={{0,4},{5,1},{4,8},{9,5},{8,12},{13,9},{12,14},{15,13},{14,10},{11,... | collective-permute-start | bytes 1179656 | tf_op jit(solution)/shard_map/ppermute | solution.py:289
  28.0 7.9 %collective-permute-start.9 = (bf16[32,6144]{1,0:T(8,128)(2,1)S(1)}, bf16[32,6144]{1,0:T(8,128)(2,1)S(1)}, u32[]{:S(2)}, u32[]{:S(2)}) collective-permute-start(bf16[32,6144]{1,0:T(8,128)(2,1)S(1)} %collective-permute-done.5.refs_8_), channel_id=1, source_target_pairs={{0,4},{5,1},{4,8},{9,5},{8,12},{13,9},{12,14},{15,13},{14,10},{11,... | collective-permute-start | bytes 1179656 | tf_op jit(solution)/shard_map/ppermute | solution.py:289
  29.7 2.4 %collective-permute-start.6 = (bf16[64,6144]{1,0:T(8,128)(2,1)S(1)}, bf16[64,6144]{1,0:T(8,128)(2,1)S(1)}, u32[]{:S(2)}, u32[]{:S(2)}) collective-permute-start(bf16[64,6144]{1,0:T(8,128)(2,1)S(1)} %pad_maximum_fusion), channel_id=1, source_target_pairs={{0,1},{1,0},{2,3},{3,2},{4,5},{5,4},{6,7},{7,6},{8,9},{9,8},{10,11... | collective-permute-start | bytes 2359304 | tf_op jit(solution)/shard_map/ppermute | solution.py:27
  31.7 4.4 %collective-permute-start.8 = (bf16[32,6144]{1,0:T(8,128)(2,1)S(1)}, bf16[32,6144]{1,0:T(8,128)(2,1)S(1)}, u32[]{:S(2)}, u32[]{:S(2)}) collective-permute-start(bf16[32,6144]{1,0:T(8,128)(2,1)S(1)} %pad_maximum_fusion.1), channel_id=1, source_target_pairs={{0,1},{1,0},{2,3},{3,2},{4,5},{5,4},{6,7},{7,6},{8,9},{9,8},{10,11... | collective-permute-start | bytes 1179656 | tf_op jit(solution)/shard_map/ppermute | solution.py:27
  32.0 10.2 %slice-start = ((s8[12582912]{0:T(1024)(128)(4,1)}), s8[4194304]{0:T(1024)(128)(4,1)S(1)}, s32[]{:S(2)}) async-start(s8[12582912]{0:T(1024)(128)(4,1)} %bitcast.18), calls=%async_computation | async-start | bytes 8388608
  35.9 1.5 %collective-permute-start.10 = (bf16[16,6144]{1,0:T(8,128)(2,1)S(1)}, bf16[16,6144]{1,0:T(8,128)(2,1)S(1)}, u32[]{:S(2)}, u32[]{:S(2)}) collective-permute-start(bf16[16,6144]{1,0:T(8,128)(2,1)S(1)} %slice.114), channel_id=1, source_target_pairs={{0,1},{1,0},{2,3},{3,2},{4,5},{5,4},{6,7},{7,6},{8,9},{9,8},{10,11... | collective-permute-start | bytes 589832 | tf_op jit(solution)/shard_map/ppermute | solution.py:27
  37.4 4.9 %slice-start.1 = ((s8[12582912]{0:T(1024)(128)(4,1)}), s8[4194304]{0:T(1024)(128)(4,1)S(1)}, s32[]{:S(2)}) async-start(s8[12582912]{0:T(1024)(128)(4,1)} %bitcast.18), calls=%async_computation.1 | async-start | bytes 8388608
  37.4 4.9 %slice-start.2 = ((s8[12582912]{0:T(1024)(128)(4,1)}), s8[4194304]{0:T(1024)(128)(4,1)S(1)}, s32[]{:S(2)}) async-start(s8[12582912]{0:T(1024)(128)(4,1)} %bitcast.18), calls=%async_computation.2 | async-start | bytes 8388608
  44.4 2.7 %collective-permute-start.13 = (bf16[32,6144]{1,0:T(8,128)(2,1)S(1)}, bf16[32,6144]{1,0:T(8,128)(2,1)S(1)}, u32[]{:S(2)}, u32[]{:S(2)}) collective-permute-start(bf16[32,6144]{1,0:T(8,128)(2,1)S(1)} %slice.142), channel_id=1, source_target_pairs={{0,1},{1,0},{2,3},{3,2},{4,5},{5,4},{6,7},{7,6},{8,9},{9,8},{10,11... | collective-permute-start | bytes 1179656 | tf_op jit(solution)/shard_map/ppermute | solution.py:27
  44.8 7.3 %collective-permute-start.12 = (bf16[16,6144]{1,0:T(8,128)(2,1)S(1)}, bf16[16,6144]{1,0:T(8,128)(2,1)S(1)}, u32[]{:S(2)}, u32[]{:S(2)}) collective-permute-start(bf16[16,6144]{1,0:T(8,128)(2,1)S(1)} %get-tuple-element.92), channel_id=1, source_target_pairs={{1,4},{4,1},{5,8},{8,5},{9,12},{12,9},{13,14},{14,13},{15,10},{10,... | collective-permute-start | bytes 589832 | tf_op jit(solution)/shard_map/ppermute | solution.py:289
  46.8 5.7 %collective-permute-start.11 = (bf16[16,6144]{1,0:T(8,128)(2,1)S(1)}, bf16[16,6144]{1,0:T(8,128)(2,1)S(1)}, u32[]{:S(2)}, u32[]{:S(2)}) collective-permute-start(bf16[16,6144]{1,0:T(8,128)(2,1)S(1)} %get-tuple-element.93), channel_id=1, source_target_pairs={{0,4},{5,1},{4,8},{9,5},{8,12},{13,9},{12,14},{15,13},{14,10},{11,... | collective-permute-start | bytes 589832 | tf_op jit(solution)/shard_map/ppermute | solution.py:289
  47.3 9.5 %collective-permute-start.18 = (bf16[32,6144]{1,0:T(8,128)(2,1)S(1)}, bf16[32,6144]{1,0:T(8,128)(2,1)S(1)}, u32[]{:S(2)}, u32[]{:S(2)}) collective-permute-start(bf16[32,6144]{1,0:T(8,128)(2,1)S(1)} %pad_maximum_fusion.2), channel_id=1, source_target_pairs={{0,4},{5,1},{4,8},{9,5},{8,12},{13,9},{12,14},{15,13},{14,10},{11,... | collective-permute-start | bytes 1179656 | tf_op jit(solution)/shard_map/ppermute | solution.py:289
  52.6 8.3 %collective-permute-start.15 = (bf16[32,6144]{1,0:T(8,128)(2,1)S(1)}, bf16[32,6144]{1,0:T(8,128)(2,1)S(1)}, u32[]{:S(2)}, u32[]{:S(2)}) collective-permute-start(bf16[32,6144]{1,0:T(8,128)(2,1)S(1)} %add_convert_fusion.4), channel_id=1, source_target_pairs={{0,4},{5,1},{4,8},{9,5},{8,12},{13,9},{12,14},{15,13},{14,10},{11,... | collective-permute-start | bytes 1179656 | tf_op jit(solution)/shard_map/ppermute | solution.py:289
  54.4 2.4 %collective-permute-start.14 = (bf16[64,6144]{1,0:T(8,128)(2,1)S(1)}, bf16[64,6144]{1,0:T(8,128)(2,1)S(1)}, u32[]{:S(2)}, u32[]{:S(2)}) collective-permute-start(bf16[64,6144]{1,0:T(8,128)(2,1)S(1)} %slice.123), channel_id=1, source_target_pairs={{0,1},{1,0},{2,3},{3,2},{4,5},{5,4},{6,7},{7,6},{8,9},{9,8},{10,11... | collective-permute-start | bytes 2359304 | tf_op jit(solution)/shard_map/ppermute | solution.py:27
  56.9 8.2 %collective-permute-start.19 = (bf16[32,6144]{1,0:T(8,128)(2,1)S(1)}, bf16[32,6144]{1,0:T(8,128)(2,1)S(1)}, u32[]{:S(2)}, u32[]{:S(2)}) collective-permute-start(bf16[32,6144]{1,0:T(8,128)(2,1)S(1)} %add_convert_fusion.1), channel_id=1, source_target_pairs={{0,4},{5,1},{4,8},{9,5},{8,12},{13,9},{12,14},{15,13},{14,10},{11,... | collective-permute-start | bytes 1179656 | tf_op jit(solution)/shard_map/ppermute | solution.py:289
  61.0 8.3 %collective-permute-start.16 = (bf16[32,6144]{1,0:T(8,128)(2,1)S(1)}, bf16[32,6144]{1,0:T(8,128)(2,1)S(1)}, u32[]{:S(2)}, u32[]{:S(2)}) collective-permute-start(bf16[32,6144]{1,0:T(8,128)(2,1)S(1)} %add_convert_fusion.3), channel_id=1, source_target_pairs={{0,4},{5,1},{4,8},{9,5},{8,12},{13,9},{12,14},{15,13},{14,10},{11,... | collective-permute-start | bytes 1179656 | tf_op jit(solution)/shard_map/ppermute | solution.py:289
  65.2 8.3 %collective-permute-start.20 = (bf16[32,6144]{1,0:T(8,128)(2,1)S(1)}, bf16[32,6144]{1,0:T(8,128)(2,1)S(1)}, u32[]{:S(2)}, u32[]{:S(2)}) collective-permute-start(bf16[32,6144]{1,0:T(8,128)(2,1)S(1)} %add_convert_fusion), channel_id=1, source_target_pairs={{0,4},{5,1},{4,8},{9,5},{8,12},{13,9},{12,14},{15,13},{14,10},{11,... | collective-permute-start | bytes 1179656 | tf_op jit(solution)/shard_map/ppermute | solution.py:289
  69.4 8.3 %collective-permute-start.17 = (bf16[32,6144]{1,0:T(8,128)(2,1)S(1)}, bf16[32,6144]{1,0:T(8,128)(2,1)S(1)}, u32[]{:S(2)}, u32[]{:S(2)}) collective-permute-start(bf16[32,6144]{1,0:T(8,128)(2,1)S(1)} %add_convert_fusion.2), channel_id=1, source_target_pairs={{0,4},{5,1},{4,8},{9,5},{8,12},{13,9},{12,14},{15,13},{14,10},{11,... | collective-permute-start | bytes 1179656 | tf_op jit(solution)/shard_map/ppermute | solution.py:289
  73.6 4.1 %collective-permute-start.21 = (bf16[32,6144]{1,0:T(8,128)(2,1)S(1)}, bf16[32,6144]{1,0:T(8,128)(2,1)S(1)}, u32[]{:S(2)}, u32[]{:S(2)}) collective-permute-start(bf16[32,6144]{1,0:T(8,128)(2,1)S(1)} %pad_maximum_fusion.3), channel_id=1, source_target_pairs={{0,1},{1,0},{2,3},{3,2},{4,5},{5,4},{6,7},{7,6},{8,9},{9,8},{10,11... | collective-permute-start | bytes 1179656 | tf_op jit(solution)/shard_map/ppermute | solution.py:27

commit v9 on v8

--- a/solution.py
+++ b/solution.py
@@ -232,7 +232,7 @@
 def combine(arrived, handed, product, mixer):
     width = arrived.shape[1]
     token_count = mixer.shape[0]
-    tile = tile_of(width, 1536)
+    tile = tile_of(width, 3072)
     steps = width // tile
 
     def kernel(arrived_ref, handed_ref, product_ref, mixer_ref, out_hbm, mixed_ref, done):

time: 79.5 us -> 79.6 us (level)
  no operation moved by 1% of the time
where the time goes in v9:
time: 79.6 us; the launch traced here: 79.4 us
  starting transfers between devices  27.8 us (35%)
  waiting for transfers between devices  23.9 us (30%)
  Pallas kernels  21.9 us (28%)
  matrix products  4.32 us (5%)
    ppermute x15, starting transfers between devices, hop(): return lax.ppermute(value, ('ept', 'exp'), pairs)  25.8 us
    ppermute x15, waiting for transfers between devices, hop(): return lax.ppermute(value, ('ept', 'exp'), pairs)  20.4 us
    pallas_call x7, Pallas kernels, call(): pl.pallas_call(kernel, in_specs=[pl.BlockSpec(memory_space=m) for _, m in...  20.4 us
    dot_general x2, matrix products, product_of(): product = jnp.dot(part, w_down, preferred_element_type=jnp.float32)  4.32 us
    ppermute x7, waiting for transfers between devices, swap(): return lax.ppermute(value, 'exp', [(0, 1), (1, 0)])  3.46 us
    ppermute x7, starting transfers between devices, swap(): return lax.ppermute(value, 'exp', [(0, 1), (1, 0)])  1.94 us
  transfers between devices with their start and end apart: 22, of which 13 were waited for; matrix products, arithmetic and copies ran while one was open for 4% of the time, Pallas kernels for 17%

profile of v9, /device:TPU:0, one launch (start us, length us, event | category | flops | bytes accessed | tf_op | source)
XLA Modules:
  0.0 79.4 jit_solution(13038249470107059257)
XLA Ops:
  0.0 1.7 %dispatch.1 = (bf16[32,6144]{1,0:T(8,128)(2,1)S(1)}, bf16[32,6144]{1,0:T(8,128)(2,1)S(1)}, bf16[128,128]{1,0:T(8,128)(2,1)S(1)}) custom-call(s32[1]{0:T(128)} %bitcast.me_ref, s32[2,128]{1,0:T(2,128)} %bitcast.22, f32[2,128]{1,0:T(2,128)} %bitcast.23, bf16[128,6144]{1,0:T(8,128)(2,1)} %tokens_hbm.1), custom_call_target="tpu_custom_call" | custom-call | tf_op jit(solution)/shard_map/dispatch/pallas_call | solution.py:104
  2.2 2.6 %collective-permute-start.1 = (bf16[32,6144]{1,0:T(8,128)(2,1)S(1)}, bf16[32,6144]{1,0:T(8,128)(2,1)S(1)}, u32[]{:S(2)}, u32[]{:S(2)}) collective-permute-start(bf16[32,6144]{1,0:T(8,128)(2,1)S(1)} %get-tuple-element.45.refs_0_), channel_id=1, source_target_pairs={{0,4},{5,1},{4,8},{9,5},{8,12},{13,9},{12,14},{15,13},{14,10},{11,... | collective-permute-start | bytes 1179656 | tf_op jit(solution)/shard_map/ppermute | solution.py:289
  4.9 1.7 %collective-permute-start.2 = (bf16[32,6144]{1,0:T(8,128)(2,1)S(1)}, bf16[32,6144]{1,0:T(8,128)(2,1)S(1)}, u32[]{:S(2)}, u32[]{:S(2)}) collective-permute-start(bf16[32,6144]{1,0:T(8,128)(2,1)S(1)} %collective-permute-done.refs_1_), channel_id=1, source_target_pairs={{0,4},{5,1},{4,8},{9,5},{8,12},{13,9},{12,14},{15,13},{14,10},{11,... | collective-permute-start | bytes 1179656 | tf_op jit(solution)/shard_map/ppermute | solution.py:289
  6.5 4.0 %collective-permute-done.1.refs_2_ = bf16[32,6144]{1,0:T(8,128)(2,1)S(1)} collective-permute-done((bf16[32,6144]{1,0:T(8,128)(2,1)S(1)}, bf16[32,6144]{1,0:T(8,128)(2,1)S(1)}, u32[]{:S(2)}, u32[]{:S(2)}) %collective-permute-start.1) | collective-permute-done | bytes 393248 | tf_op jit(solution)/shard_map/ppermute | solution.py:289
  10.6 2.1 %collective-permute-start.3 = (bf16[32,6144]{1,0:T(8,128)(2,1)S(1)}, bf16[32,6144]{1,0:T(8,128)(2,1)S(1)}, u32[]{:S(2)}, u32[]{:S(2)}) collective-permute-start(bf16[32,6144]{1,0:T(8,128)(2,1)S(1)} %collective-permute-done.1.refs_2_), channel_id=1, source_target_pairs={{0,4},{5,1},{4,8},{9,5},{8,12},{13,9},{12,14},{15,13},{14,10},{11,... | collective-permute-start | bytes 1179656 | tf_op jit(solution)/shard_map/ppermute | solution.py:289
  12.6 2.6 %hold_and_multiply.5 = (bf16[2304,1024]{1,0:T(8,128)(2,1)S(1)}, f32[48,1024]{1,0:T(8,128)S(1)}) custom-call(bf16[32,6144]{1,0:T(8,128)(2,1)S(1)} %get-tuple-element.45.refs_0_, bf16[32,6144]{1,0:T(8,128)(2,1)S(1)} %collective-permute-done.refs_1_, bf16[32,6144]{1,0:T(8,128)(2,1)S(1)} %collective-permute-done.1.refs_2_, bf16[6144,1024]{1,0:T(8,128)(2,1)} %bitcast.15), custom_call_target="tpu_custom_call" | custom-call | flops 226492416 | bytes 4718592 | tf_op jit(solution)/shard_map/hold_and_multiply/pallas_call | solution.py:104
  15.3 1.6 %collective-permute-start.4 = (bf16[32,6144]{1,0:T(8,128)(2,1)S(1)}, bf16[32,6144]{1,0:T(8,128)(2,1)S(1)}, u32[]{:S(2)}, u32[]{:S(2)}) collective-permute-start(bf16[32,6144]{1,0:T(8,128)(2,1)S(1)} %collective-permute-done.2.refs_3_), channel_id=1, source_target_pairs={{0,4},{5,1},{4,8},{9,5},{8,12},{13,9},{12,14},{15,13},{14,10},{11,... | collective-permute-start | bytes 1179656 | tf_op jit(solution)/shard_map/ppermute | solution.py:289
  16.9 2.6 %hold_and_multiply.6 = (bf16[2304,1024]{1,0:T(8,128)(2,1)S(1)}, f32[48,1024]{1,0:T(8,128)S(1)}) custom-call(bf16[32,6144]{1,0:T(8,128)(2,1)S(1)} %get-tuple-element.45.refs_0_, bf16[32,6144]{1,0:T(8,128)(2,1)S(1)} %collective-permute-done.refs_1_, bf16[32,6144]{1,0:T(8,128)(2,1)S(1)} %collective-permute-done.1.refs_2_, bf16[6144,1024]{1,0:T(8,128)(2,1)} %bitcast.16, ...), custom_call_target="tpu_custom_call" | custom-call | flops 226492416 | bytes 4718592 | tf_op jit(solution)/shard_map/hold_and_multiply/pallas_call | solution.py:104
  19.6 1.6 %collective-permute-start.5 = (bf16[32,6144]{1,0:T(8,128)(2,1)S(1)}, bf16[32,6144]{1,0:T(8,128)(2,1)S(1)}, u32[]{:S(2)}, u32[]{:S(2)}) collective-permute-start(bf16[32,6144]{1,0:T(8,128)(2,1)S(1)} %collective-permute-done.3.refs_4_), channel_id=1, source_target_pairs={{0,4},{5,1},{4,8},{9,5},{8,12},{13,9},{12,14},{15,13},{14,10},{11,... | collective-permute-start | bytes 1179656 | tf_op jit(solution)/shard_map/ppermute | solution.py:289
  21.2 2.1 %hold_and_multiply.7 = (bf16[1536,1024]{1,0:T(8,128)(2,1)S(1)}, f32[48,1024]{1,0:T(8,128)S(1)}) custom-call(bf16[32,6144]{1,0:T(8,128)(2,1)S(1)} %get-tuple-element.45.refs_0_, bf16[32,6144]{1,0:T(8,128)(2,1)S(1)} %collective-permute-done.refs_1_, bf16[32,6144]{1,0:T(8,128)(2,1)S(1)} %collective-permute-done.1.refs_2_, bf16[6144,1024]{1,0:T(8,128)(2,1)} %bitcast.17, ...), custom_call_target="tpu_custom_call" | custom-call | flops 150994944 | bytes 3145728 | tf_op jit(solution)/shard_map/hold_and_multiply/pallas_call | solution.py:104
  23.4 1.9 %collective-permute-start.7 = (bf16[32,6144]{1,0:T(8,128)(2,1)S(1)}, bf16[32,6144]{1,0:T(8,128)(2,1)S(1)}, u32[]{:S(2)}, u32[]{:S(2)}) collective-permute-start(bf16[32,6144]{1,0:T(8,128)(2,1)S(1)} %collective-permute-done.4.refs_5_), channel_id=1, source_target_pairs={{0,4},{5,1},{4,8},{9,5},{8,12},{13,9},{12,14},{15,13},{14,10},{11,... | collective-permute-start | bytes 1179656 | tf_op jit(solution)/shard_map/ppermute | solution.py:289
  25.3 2.7 %hold_and_multiply.8 = (bf16[2304,1024]{1,0:T(8,128)(2,1)S(1)}, f32[96,1024]{1,0:T(8,128)S(1)}) custom-call(bf16[32,6144]{1,0:T(8,128)(2,1)S(1)} %get-tuple-element.45.refs_0_, bf16[32,6144]{1,0:T(8,128)(2,1)S(1)} %collective-permute-done.refs_1_, bf16[32,6144]{1,0:T(8,128)(2,1)S(1)} %collective-permute-done.1.refs_2_, ...), custom_call_target="tpu_custom_call" | custom-call | flops 452984832 | bytes 4718592 | tf_op jit(solution)/shard_map/hold_and_multiply/pallas_call | solution.py:104
  28.0 1.6 %collective-permute-start.9 = (bf16[32,6144]{1,0:T(8,128)(2,1)S(1)}, bf16[32,6144]{1,0:T(8,128)(2,1)S(1)}, u32[]{:S(2)}, u32[]{:S(2)}) collective-permute-start(bf16[32,6144]{1,0:T(8,128)(2,1)S(1)} %collective-permute-done.5.refs_8_), channel_id=1, source_target_pairs={{0,4},{5,1},{4,8},{9,5},{8,12},{13,9},{12,14},{15,13},{14,10},{11,... | collective-permute-start | bytes 1179656 | tf_op jit(solution)/shard_map/ppermute | solution.py:289
  29.8 1.9 %collective-permute-done.7.refs_9_ = bf16[32,6144]{1,0:T(8,128)(2,1)S(1)} collective-permute-done((bf16[32,6144]{1,0:T(8,128)(2,1)S(1)}, bf16[32,6144]{1,0:T(8,128)(2,1)S(1)}, u32[]{:S(2)}, u32[]{:S(2)}) %collective-permute-start.7) | collective-permute-done | bytes 393248 | tf_op jit(solution)/shard_map/ppermute | solution.py:289
  32.0 3.8 %hold_and_multiply.9 = (bf16[3840,1024]{1,0:T(8,128)(2,1)S(1)}, f32[96,1024]{1,0:T(8,128)S(1)}) custom-call(bf16[32,6144]{1,0:T(8,128)(2,1)S(1)} %get-tuple-element.45.refs_0_, bf16[32,6144]{1,0:T(8,128)(2,1)S(1)} %collective-permute-done.refs_1_, bf16[32,6144]{1,0:T(8,128)(2,1)S(1)} %collective-permute-done.1.refs_2_, ...), custom_call_target="tpu_custom_call" | custom-call | flops 754974720 | bytes 7864320 | tf_op jit(solution)/shard_map/hold_and_multiply/pallas_call | solution.py:104
  37.4 4.9 %hidden.1 = bf16[256,1024]{1,0:T(8,128)(2,1)S(1)} custom-call(bf16[32,6144]{1,0:T(8,128)(2,1)S(1)} %get-tuple-element.45.refs_0_, bf16[32,6144]{1,0:T(8,128)(2,1)S(1)} %collective-permute-done.refs_1_, bf16[32,6144]{1,0:T(8,128)(2,1)S(1)} %collective-permute-done.1.refs_2_, bf16[32,6144]{1,0:T(8,128)(2,1)S(1)} %collective-permute-done.2.refs_3_, ...), custom_call_target="tpu_custom_call" | custom-call | flops 6442450944 | bytes 25165824 | tf_op jit(solution)/shard_map/hidden/pallas_call | solution.py:104
  42.3 2.1 %fusion.7 = bf16[96,6144]{1,0:T(8,128)(2,1)S(1)} fusion(bf16[1,1024,6144]{2,1,0:T(8,128)(2,1)S(1)} %bitcast.19, bf16[256,1024]{1,0:T(8,128)(2,1)S(1)} %hidden.1), kind=kOutput, calls=%fused_computation.5 | convolution fusion | flops 1208549376 | bytes 13959168 | tf_op jit(solution)/shard_map/dot_general | solution.py:338
  44.8 2.0 %collective-permute-start.12 = (bf16[16,6144]{1,0:T(8,128)(2,1)S(1)}, bf16[16,6144]{1,0:T(8,128)(2,1)S(1)}, u32[]{:S(2)}, u32[]{:S(2)}) collective-permute-start(bf16[16,6144]{1,0:T(8,128)(2,1)S(1)} %get-tuple-element.92), channel_id=1, source_target_pairs={{1,4},{4,1},{5,8},{8,5},{9,12},{12,9},{13,14},{14,13},{15,10},{10,... | collective-permute-start | bytes 589832 | tf_op jit(solution)/shard_map/ppermute | solution.py:289
  47.3 1.7 %collective-permute-start.18 = (bf16[32,6144]{1,0:T(8,128)(2,1)S(1)}, bf16[32,6144]{1,0:T(8,128)(2,1)S(1)}, u32[]{:S(2)}, u32[]{:S(2)}) collective-permute-start(bf16[32,6144]{1,0:T(8,128)(2,1)S(1)} %pad_maximum_fusion.2), channel_id=1, source_target_pairs={{0,4},{5,1},{4,8},{9,5},{8,12},{13,9},{12,14},{15,13},{14,10},{11,... | collective-permute-start | bytes 1179656 | tf_op jit(solution)/shard_map/ppermute | solution.py:289
  49.0 2.2 %fusion.4 = bf16[160,6144]{1,0:T(8,128)(2,1)S(1)} fusion(bf16[160,1024]{1,0:T(8,128)(2,1)S(1)} %slice.144, bf16[1,1024,6144]{2,1,0:T(8,128)(2,1)S(1)} %bitcast.19), kind=kOutput, calls=%fused_computation.4 | convolution fusion | flops 2014248960 | bytes 14876672 | tf_op jit(solution)/shard_map/dot_general | solution.py:338
  52.6 1.7 %collective-permute-start.15 = (bf16[32,6144]{1,0:T(8,128)(2,1)S(1)}, bf16[32,6144]{1,0:T(8,128)(2,1)S(1)}, u32[]{:S(2)}, u32[]{:S(2)}) collective-permute-start(bf16[32,6144]{1,0:T(8,128)(2,1)S(1)} %add_convert_fusion.4), channel_id=1, source_target_pairs={{0,4},{5,1},{4,8},{9,5},{8,12},{13,9},{12,14},{15,13},{14,10},{11,... | collective-permute-start | bytes 1179656 | tf_op jit(solution)/shard_map/ppermute | solution.py:289
  54.8 2.0 %collective-permute-done.14 = bf16[64,6144]{1,0:T(8,128)(2,1)S(1)} collective-permute-done((bf16[64,6144]{1,0:T(8,128)(2,1)S(1)}, bf16[64,6144]{1,0:T(8,128)(2,1)S(1)}, u32[]{:S(2)}, u32[]{:S(2)}) %collective-permute-start.14) | collective-permute-done | bytes 786464 | tf_op jit(solution)/shard_map/ppermute | solution.py:27
  56.9 1.6 %collective-permute-start.19 = (bf16[32,6144]{1,0:T(8,128)(2,1)S(1)}, bf16[32,6144]{1,0:T(8,128)(2,1)S(1)}, u32[]{:S(2)}, u32[]{:S(2)}) collective-permute-start(bf16[32,6144]{1,0:T(8,128)(2,1)S(1)} %add_convert_fusion.1), channel_id=1, source_target_pairs={{0,4},{5,1},{4,8},{9,5},{8,12},{13,9},{12,14},{15,13},{14,10},{11,... | collective-permute-start | bytes 1179656 | tf_op jit(solution)/shard_map/ppermute | solution.py:289
  58.5 2.4 %collective-permute-done.15 = bf16[32,6144]{1,0:T(8,128)(2,1)S(1)} collective-permute-done((bf16[32,6144]{1,0:T(8,128)(2,1)S(1)}, bf16[32,6144]{1,0:T(8,128)(2,1)S(1)}, u32[]{:S(2)}, u32[]{:S(2)}) %collective-permute-start.15) | collective-permute-done | bytes 393248 | tf_op jit(solution)/shard_map/ppermute | solution.py:289
  61.0 1.7 %collective-permute-start.16 = (bf16[32,6144]{1,0:T(8,128)(2,1)S(1)}, bf16[32,6144]{1,0:T(8,128)(2,1)S(1)}, u32[]{:S(2)}, u32[]{:S(2)}) collective-permute-start(bf16[32,6144]{1,0:T(8,128)(2,1)S(1)} %add_convert_fusion.3), channel_id=1, source_target_pairs={{0,4},{5,1},{4,8},{9,5},{8,12},{13,9},{12,14},{15,13},{14,10},{11,... | collective-permute-start | bytes 1179656 | tf_op jit(solution)/shard_map/ppermute | solution.py:289
  62.7 2.4 %collective-permute-done.19 = bf16[32,6144]{1,0:T(8,128)(2,1)S(1)} collective-permute-done((bf16[32,6144]{1,0:T(8,128)(2,1)S(1)}, bf16[32,6144]{1,0:T(8,128)(2,1)S(1)}, u32[]{:S(2)}, u32[]{:S(2)}) %collective-permute-start.19) | collective-permute-done | bytes 393248 | tf_op jit(solution)/shard_map/ppermute | solution.py:289
  65.2 1.7 %collective-permute-start.20 = (bf16[32,6144]{1,0:T(8,128)(2,1)S(1)}, bf16[32,6144]{1,0:T(8,128)(2,1)S(1)}, u32[]{:S(2)}, u32[]{:S(2)}) collective-permute-start(bf16[32,6144]{1,0:T(8,128)(2,1)S(1)} %add_convert_fusion), channel_id=1, source_target_pairs={{0,4},{5,1},{4,8},{9,5},{8,12},{13,9},{12,14},{15,13},{14,10},{11,... | collective-permute-start | bytes 1179656 | tf_op jit(solution)/shard_map/ppermute | solution.py:289
  66.9 2.4 %collective-permute-done.16 = bf16[32,6144]{1,0:T(8,128)(2,1)S(1)} collective-permute-done((bf16[32,6144]{1,0:T(8,128)(2,1)S(1)}, bf16[32,6144]{1,0:T(8,128)(2,1)S(1)}, u32[]{:S(2)}, u32[]{:S(2)}) %collective-permute-start.16) | collective-permute-done | bytes 393248 | tf_op jit(solution)/shard_map/ppermute | solution.py:289
  69.4 1.7 %collective-permute-start.17 = (bf16[32,6144]{1,0:T(8,128)(2,1)S(1)}, bf16[32,6144]{1,0:T(8,128)(2,1)S(1)}, u32[]{:S(2)}, u32[]{:S(2)}) collective-permute-start(bf16[32,6144]{1,0:T(8,128)(2,1)S(1)} %add_convert_fusion.2), channel_id=1, source_target_pairs={{0,4},{5,1},{4,8},{9,5},{8,12},{13,9},{12,14},{15,13},{14,10},{11,... | collective-permute-start | bytes 1179656 | tf_op jit(solution)/shard_map/ppermute | solution.py:289
  71.2 2.4 %collective-permute-done.20 = bf16[32,6144]{1,0:T(8,128)(2,1)S(1)} collective-permute-done((bf16[32,6144]{1,0:T(8,128)(2,1)S(1)}, bf16[32,6144]{1,0:T(8,128)(2,1)S(1)}, u32[]{:S(2)}, u32[]{:S(2)}) %collective-permute-start.20) | collective-permute-done | bytes 393248 | tf_op jit(solution)/shard_map/ppermute | solution.py:289
  74.1 3.7 %collective-permute-done.17.arrived_ref = bf16[32,6144]{1,0:T(8,128)(2,1)S(1)} collective-permute-done((bf16[32,6144]{1,0:T(8,128)(2,1)S(1)}, bf16[32,6144]{1,0:T(8,128)(2,1)S(1)}, u32[]{:S(2)}, u32[]{:S(2)}) %collective-permute-start.17) | collective-permute-done | bytes 393248 | tf_op jit(solution)/shard_map/ppermute | solution.py:289
  77.8 1.5 %combine.1 = bf16[128,6144]{1,0:T(8,128)(2,1)} custom-call(bf16[32,6144]{1,0:T(8,128)(2,1)S(1)} %collective-permute-done.17.arrived_ref, bf16[32,6144]{1,0:T(8,128)(2,1)S(1)} %collective-permute-done.21.handed_ref, bf16[16,6144]{1,0:T(8,128)(2,1)S(1)} %get-tuple-element.85.product_ref, bf16[128,128]{1,0:T(8,128)(2,1)S(1)} %get-tuple-element.84.mixer_ref), custom_call_target="tpu_custom_call" | custom-call | tf_op jit(solution)/shard_map/combine/pallas_call | solution.py:263
  (54 shorter events, 6.2 us)
Async XLA Ops:
  1.7 3.2 %collective-permute-start = (bf16[32,6144]{1,0:T(8,128)(2,1)S(1)}, bf16[32,6144]{1,0:T(8,128)(2,1)S(1)}, u32[]{:S(2)}, u32[]{:S(2)}) collective-permute-start(bf16[32,6144]{1,0:T(8,128)(2,1)S(1)} %get-tuple-element.46), channel_id=1, source_target_pairs={{0,1},{1,0},{2,3},{3,2},{4,5},{5,4},{6,7},{7,6},{8,9},{9,8},{10,11... | collective-permute-start | bytes 1179656 | tf_op jit(solution)/shard_map/ppermute | solution.py:27
  2.2 8.3 %collective-permute-start.1 = (bf16[32,6144]{1,0:T(8,128)(2,1)S(1)}, bf16[32,6144]{1,0:T(8,128)(2,1)S(1)}, u32[]{:S(2)}, u32[]{:S(2)}) collective-permute-start(bf16[32,6144]{1,0:T(8,128)(2,1)S(1)} %get-tuple-element.45.refs_0_), channel_id=1, source_target_pairs={{0,4},{5,1},{4,8},{9,5},{8,12},{13,9},{12,14},{15,13},{14,10},{11,... | collective-permute-start | bytes 1179656 | tf_op jit(solution)/shard_map/ppermute | solution.py:289
  4.9 10.4 %collective-permute-start.2 = (bf16[32,6144]{1,0:T(8,128)(2,1)S(1)}, bf16[32,6144]{1,0:T(8,128)(2,1)S(1)}, u32[]{:S(2)}, u32[]{:S(2)}) collective-permute-start(bf16[32,6144]{1,0:T(8,128)(2,1)S(1)} %collective-permute-done.refs_1_), channel_id=1, source_target_pairs={{0,4},{5,1},{4,8},{9,5},{8,12},{13,9},{12,14},{15,13},{14,10},{11,... | collective-permute-start | bytes 1179656 | tf_op jit(solution)/shard_map/ppermute | solution.py:289
  10.6 9.0 %collective-permute-start.3 = (bf16[32,6144]{1,0:T(8,128)(2,1)S(1)}, bf16[32,6144]{1,0:T(8,128)(2,1)S(1)}, u32[]{:S(2)}, u32[]{:S(2)}) collective-permute-start(bf16[32,6144]{1,0:T(8,128)(2,1)S(1)} %collective-permute-done.1.refs_2_), channel_id=1, source_target_pairs={{0,4},{5,1},{4,8},{9,5},{8,12},{13,9},{12,14},{15,13},{14,10},{11,... | collective-permute-start | bytes 1179656 | tf_op jit(solution)/shard_map/ppermute | solution.py:289
  15.3 8.1 %collective-permute-start.4 = (bf16[32,6144]{1,0:T(8,128)(2,1)S(1)}, bf16[32,6144]{1,0:T(8,128)(2,1)S(1)}, u32[]{:S(2)}, u32[]{:S(2)}) collective-permute-start(bf16[32,6144]{1,0:T(8,128)(2,1)S(1)} %collective-permute-done.2.refs_3_), channel_id=1, source_target_pairs={{0,4},{5,1},{4,8},{9,5},{8,12},{13,9},{12,14},{15,13},{14,10},{11,... | collective-permute-start | bytes 1179656 | tf_op jit(solution)/shard_map/ppermute | solution.py:289
  19.6 8.4 %collective-permute-start.5 = (bf16[32,6144]{1,0:T(8,128)(2,1)S(1)}, bf16[32,6144]{1,0:T(8,128)(2,1)S(1)}, u32[]{:S(2)}, u32[]{:S(2)}) collective-permute-start(bf16[32,6144]{1,0:T(8,128)(2,1)S(1)} %collective-permute-done.3.refs_4_), channel_id=1, source_target_pairs={{0,4},{5,1},{4,8},{9,5},{8,12},{13,9},{12,14},{15,13},{14,10},{11,... | collective-permute-start | bytes 1179656 | tf_op jit(solution)/shard_map/ppermute | solution.py:289
  23.4 8.2 %collective-permute-start.7 = (bf16[32,6144]{1,0:T(8,128)(2,1)S(1)}, bf16[32,6144]{1,0:T(8,128)(2,1)S(1)}, u32[]{:S(2)}, u32[]{:S(2)}) collective-permute-start(bf16[32,6144]{1,0:T(8,128)(2,1)S(1)} %collective-permute-done.4.refs_5_), channel_id=1, source_target_pairs={{0,4},{5,1},{4,8},{9,5},{8,12},{13,9},{12,14},{15,13},{14,10},{11,... | collective-permute-start | bytes 1179656 | tf_op jit(solution)/shard_map/ppermute | solution.py:289
  28.0 7.9 %collective-permute-start.9 = (bf16[32,6144]{1,0:T(8,128)(2,1)S(1)}, bf16[32,6144]{1,0:T(8,128)(2,1)S(1)}, u32[]{:S(2)}, u32[]{:S(2)}) collective-permute-start(bf16[32,6144]{1,0:T(8,128)(2,1)S(1)} %collective-permute-done.5.refs_8_), channel_id=1, source_target_pairs={{0,4},{5,1},{4,8},{9,5},{8,12},{13,9},{12,14},{15,13},{14,10},{11,... | collective-permute-start | bytes 1179656 | tf_op jit(solution)/shard_map/ppermute | solution.py:289
  29.7 2.4 %collective-permute-start.6 = (bf16[64,6144]{1,0:T(8,128)(2,1)S(1)}, bf16[64,6144]{1,0:T(8,128)(2,1)S(1)}, u32[]{:S(2)}, u32[]{:S(2)}) collective-permute-start(bf16[64,6144]{1,0:T(8,128)(2,1)S(1)} %pad_maximum_fusion), channel_id=1, source_target_pairs={{0,1},{1,0},{2,3},{3,2},{4,5},{5,4},{6,7},{7,6},{8,9},{9,8},{10,11... | collective-permute-start | bytes 2359304 | tf_op jit(solution)/shard_map/ppermute | solution.py:27
  31.7 4.4 %collective-permute-start.8 = (bf16[32,6144]{1,0:T(8,128)(2,1)S(1)}, bf16[32,6144]{1,0:T(8,128)(2,1)S(1)}, u32[]{:S(2)}, u32[]{:S(2)}) collective-permute-start(bf16[32,6144]{1,0:T(8,128)(2,1)S(1)} %pad_maximum_fusion.1), channel_id=1, source_target_pairs={{0,1},{1,0},{2,3},{3,2},{4,5},{5,4},{6,7},{7,6},{8,9},{9,8},{10,11... | collective-permute-start | bytes 1179656 | tf_op jit(solution)/shard_map/ppermute | solution.py:27
  32.0 10.2 %slice-start = ((s8[12582912]{0:T(1024)(128)(4,1)}), s8[4194304]{0:T(1024)(128)(4,1)S(1)}, s32[]{:S(2)}) async-start(s8[12582912]{0:T(1024)(128)(4,1)} %bitcast.18), calls=%async_computation | async-start | bytes 8388608
  35.9 1.5 %collective-permute-start.10 = (bf16[16,6144]{1,0:T(8,128)(2,1)S(1)}, bf16[16,6144]{1,0:T(8,128)(2,1)S(1)}, u32[]{:S(2)}, u32[]{:S(2)}) collective-permute-start(bf16[16,6144]{1,0:T(8,128)(2,1)S(1)} %slice.114), channel_id=1, source_target_pairs={{0,1},{1,0},{2,3},{3,2},{4,5},{5,4},{6,7},{7,6},{8,9},{9,8},{10,11... | collective-permute-start | bytes 589832 | tf_op jit(solution)/shard_map/ppermute | solution.py:27
  37.4 4.9 %slice-start.1 = ((s8[12582912]{0:T(1024)(128)(4,1)}), s8[4194304]{0:T(1024)(128)(4,1)S(1)}, s32[]{:S(2)}) async-start(s8[12582912]{0:T(1024)(128)(4,1)} %bitcast.18), calls=%async_computation.1 | async-start | bytes 8388608
  37.4 4.9 %slice-start.2 = ((s8[12582912]{0:T(1024)(128)(4,1)}), s8[4194304]{0:T(1024)(128)(4,1)S(1)}, s32[]{:S(2)}) async-start(s8[12582912]{0:T(1024)(128)(4,1)} %bitcast.18), calls=%async_computation.2 | async-start | bytes 8388608
  44.4 2.7 %collective-permute-start.13 = (bf16[32,6144]{1,0:T(8,128)(2,1)S(1)}, bf16[32,6144]{1,0:T(8,128)(2,1)S(1)}, u32[]{:S(2)}, u32[]{:S(2)}) collective-permute-start(bf16[32,6144]{1,0:T(8,128)(2,1)S(1)} %slice.142), channel_id=1, source_target_pairs={{0,1},{1,0},{2,3},{3,2},{4,5},{5,4},{6,7},{7,6},{8,9},{9,8},{10,11... | collective-permute-start | bytes 1179656 | tf_op jit(solution)/shard_map/ppermute | solution.py:27
  44.8 7.3 %collective-permute-start.12 = (bf16[16,6144]{1,0:T(8,128)(2,1)S(1)}, bf16[16,6144]{1,0:T(8,128)(2,1)S(1)}, u32[]{:S(2)}, u32[]{:S(2)}) collective-permute-start(bf16[16,6144]{1,0:T(8,128)(2,1)S(1)} %get-tuple-element.92), channel_id=1, source_target_pairs={{1,4},{4,1},{5,8},{8,5},{9,12},{12,9},{13,14},{14,13},{15,10},{10,... | collective-permute-start | bytes 589832 | tf_op jit(solution)/shard_map/ppermute | solution.py:289
  46.8 5.7 %collective-permute-start.11 = (bf16[16,6144]{1,0:T(8,128)(2,1)S(1)}, bf16[16,6144]{1,0:T(8,128)(2,1)S(1)}, u32[]{:S(2)}, u32[]{:S(2)}) collective-permute-start(bf16[16,6144]{1,0:T(8,128)(2,1)S(1)} %get-tuple-element.93), channel_id=1, source_target_pairs={{0,4},{5,1},{4,8},{9,5},{8,12},{13,9},{12,14},{15,13},{14,10},{11,... | collective-permute-start | bytes 589832 | tf_op jit(solution)/shard_map/ppermute | solution.py:289
  47.3 9.5 %collective-permute-start.18 = (bf16[32,6144]{1,0:T(8,128)(2,1)S(1)}, bf16[32,6144]{1,0:T(8,128)(2,1)S(1)}, u32[]{:S(2)}, u32[]{:S(2)}) collective-permute-start(bf16[32,6144]{1,0:T(8,128)(2,1)S(1)} %pad_maximum_fusion.2), channel_id=1, source_target_pairs={{0,4},{5,1},{4,8},{9,5},{8,12},{13,9},{12,14},{15,13},{14,10},{11,... | collective-permute-start | bytes 1179656 | tf_op jit(solution)/shard_map/ppermute | solution.py:289
  52.6 8.3 %collective-permute-start.15 = (bf16[32,6144]{1,0:T(8,128)(2,1)S(1)}, bf16[32,6144]{1,0:T(8,128)(2,1)S(1)}, u32[]{:S(2)}, u32[]{:S(2)}) collective-permute-start(bf16[32,6144]{1,0:T(8,128)(2,1)S(1)} %add_convert_fusion.4), channel_id=1, source_target_pairs={{0,4},{5,1},{4,8},{9,5},{8,12},{13,9},{12,14},{15,13},{14,10},{11,... | collective-permute-start | bytes 1179656 | tf_op jit(solution)/shard_map/ppermute | solution.py:289
  54.4 2.4 %collective-permute-start.14 = (bf16[64,6144]{1,0:T(8,128)(2,1)S(1)}, bf16[64,6144]{1,0:T(8,128)(2,1)S(1)}, u32[]{:S(2)}, u32[]{:S(2)}) collective-permute-start(bf16[64,6144]{1,0:T(8,128)(2,1)S(1)} %slice.123), channel_id=1, source_target_pairs={{0,1},{1,0},{2,3},{3,2},{4,5},{5,4},{6,7},{7,6},{8,9},{9,8},{10,11... | collective-permute-start | bytes 2359304 | tf_op jit(solution)/shard_map/ppermute | solution.py:27
  56.9 8.2 %collective-permute-start.19 = (bf16[32,6144]{1,0:T(8,128)(2,1)S(1)}, bf16[32,6144]{1,0:T(8,128)(2,1)S(1)}, u32[]{:S(2)}, u32[]{:S(2)}) collective-permute-start(bf16[32,6144]{1,0:T(8,128)(2,1)S(1)} %add_convert_fusion.1), channel_id=1, source_target_pairs={{0,4},{5,1},{4,8},{9,5},{8,12},{13,9},{12,14},{15,13},{14,10},{11,... | collective-permute-start | bytes 1179656 | tf_op jit(solution)/shard_map/ppermute | solution.py:289
  61.0 8.3 %collective-permute-start.16 = (bf16[32,6144]{1,0:T(8,128)(2,1)S(1)}, bf16[32,6144]{1,0:T(8,128)(2,1)S(1)}, u32[]{:S(2)}, u32[]{:S(2)}) collective-permute-start(bf16[32,6144]{1,0:T(8,128)(2,1)S(1)} %add_convert_fusion.3), channel_id=1, source_target_pairs={{0,4},{5,1},{4,8},{9,5},{8,12},{13,9},{12,14},{15,13},{14,10},{11,... | collective-permute-start | bytes 1179656 | tf_op jit(solution)/shard_map/ppermute | solution.py:289
  65.2 8.3 %collective-permute-start.20 = (bf16[32,6144]{1,0:T(8,128)(2,1)S(1)}, bf16[32,6144]{1,0:T(8,128)(2,1)S(1)}, u32[]{:S(2)}, u32[]{:S(2)}) collective-permute-start(bf16[32,6144]{1,0:T(8,128)(2,1)S(1)} %add_convert_fusion), channel_id=1, source_target_pairs={{0,4},{5,1},{4,8},{9,5},{8,12},{13,9},{12,14},{15,13},{14,10},{11,... | collective-permute-start | bytes 1179656 | tf_op jit(solution)/shard_map/ppermute | solution.py:289
  69.4 8.3 %collective-permute-start.17 = (bf16[32,6144]{1,0:T(8,128)(2,1)S(1)}, bf16[32,6144]{1,0:T(8,128)(2,1)S(1)}, u32[]{:S(2)}, u32[]{:S(2)}) collective-permute-start(bf16[32,6144]{1,0:T(8,128)(2,1)S(1)} %add_convert_fusion.2), channel_id=1, source_target_pairs={{0,4},{5,1},{4,8},{9,5},{8,12},{13,9},{12,14},{15,13},{14,10},{11,... | collective-permute-start | bytes 1179656 | tf_op jit(solution)/shard_map/ppermute | solution.py:289
  73.6 4.1 %collective-permute-start.21 = (bf16[32,6144]{1,0:T(8,128)(2,1)S(1)}, bf16[32,6144]{1,0:T(8,128)(2,1)S(1)}, u32[]{:S(2)}, u32[]{:S(2)}) collective-permute-start(bf16[32,6144]{1,0:T(8,128)(2,1)S(1)} %pad_maximum_fusion.3), channel_id=1, source_target_pairs={{0,1},{1,0},{2,3},{3,2},{4,5},{5,4},{6,7},{7,6},{8,9},{9,8},{10,11... | collective-permute-start | bytes 1179656 | tf_op jit(solution)/shard_map/ppermute | solution.py:27
